TPU v7x, 32 devices: a whole 2x2x4 slice. The times are simulated.
32 devices in a mesh: groups: 2 (over x), row: 8 (over z, y), col: 2 (over core).
Axes of the slice: x: 2, y: 2, z: 4, core: 2. Of those that a mesh axis runs over, the one named last changes fastest.
Arguments:
- pair_rep: bfloat16 [160, 80, 128], P(('groups', 'row'), 'col'), parts along dimension 0, as said below
- proj_weight: bfloat16 [128, 512], replicated, may hold values from -0.5 to 0.5
- gate_weight: bfloat16 [128, 128], replicated, may hold values from -0.5 to 0.5
- out_weight: bfloat16 [128, 128], replicated, may hold values from -0.5 to 0.5
Outputs:
- update: bfloat16 [160, 80, 128], P(('groups', 'row'), 'col'), parts along dimension 0
There are 2 independent parts, one for each index of `groups`. A program takes and returns all parts, laid end to end along the dimension named above; an argument that names none is the same for every part. Nothing has to cross between parts.
Inputs may be any that keep to these rules, and one draw needn't show every extreme that they name: `pair_rep`: real-valued pair features; each pair position and each channel carries its own scale factor between 1 and 10.
All inputs are finite; a program needn't handle non-finite values.
Results may differ from a plain program's by a relative error of at most 0.0078.
Values may be sent and summed in bfloat16 or wider, within the bound.
No kernel may reach another device: no remote copies, remote signals or barrier semaphores. Data moves between devices by JAX's collectives and lax.ppermute only.
A program may use at most 128 MiB of HBM per device.

v0:
```python
import jax
import jax.numpy as jnp
from jax import lax
from jax.sharding import PartitionSpec as P


def layer_norm(values):
    average = jnp.mean(values, axis=-1, keepdims=True)
    centered = values - average
    spread = jnp.mean(centered * centered, axis=-1, keepdims=True)
    return centered * lax.rsqrt(spread + 1e-05)


def per_device(pair_rep, proj_weight, gate_weight, out_weight):
    rows_here, cols_here, channels = pair_rep.shape
    hidden = out_weight.shape[0]
    normed = layer_norm(pair_rep.astype(jnp.float32)).astype(jnp.bfloat16)
    flat_rows = normed.reshape(-1, channels)
    projected = jnp.dot(flat_rows, proj_weight, preferred_element_type=jnp.float32)
    left_side = (jax.nn.sigmoid(projected[:, :hidden]) * projected[:, hidden : 2 * hidden]).astype(
        jnp.bfloat16
    )
    right_side = (
        jax.nn.sigmoid(projected[:, 2 * hidden : 3 * hidden]) * projected[:, 3 * hidden :]
    ).astype(jnp.bfloat16)
    left_side = left_side.reshape(rows_here, cols_here, hidden)
    right_side = right_side.reshape(rows_here, cols_here, hidden)
    gating = jax.nn.sigmoid(jnp.dot(flat_rows, gate_weight, preferred_element_type=jnp.float32))
    left_full, right_strip = (
        lax.all_gather(left_side, "col", axis=1, tiled=True),
        lax.all_gather(right_side, "col", axis=1, tiled=True),
    )
    right_all = lax.all_gather(right_strip, "row", axis=0, tiled=True)
    right_mine = lax.dynamic_slice_in_dim(
        right_all, lax.axis_index("col") * cols_here, cols_here, 0
    )
    combined = jnp.einsum("ikc,jkc->ijc", left_full, right_mine, preferred_element_type=jnp.float32)
    tri_normed = layer_norm(combined).astype(jnp.bfloat16).reshape(-1, hidden)
    update = jnp.dot(tri_normed, out_weight, preferred_element_type=jnp.float32) * gating
    return update.astype(jnp.bfloat16).reshape(rows_here, cols_here, channels)


def solution(mesh):
    placed = (P(("groups", "row"), "col", None), P(), P(), P())
    return jax.shard_map(
        per_device,
        mesh=mesh,
        in_specs=placed,
        out_specs=P(("groups", "row"), "col", None),
        check_vma=False,
    )
```

profile of v0, /device:TPU:0, one launch (start us, length us, event | category | flops | bytes accessed | tf_op | source)
XLA Modules:
  0.0 72.0 jit_solution(2186208317133575420)
XLA Ops:
  6.5 0.0 copy-start
  6.5 0.0 all-gather.2.cloned.1.call-start
  6.5 1.1 %convert_reduce_fusion = f32[10,40]{1,0:T(8,128)S(1)} fusion(bf16[10,40,128]{2,1,0:T(8,128)(2,1)} %param.4), kind=kLoop, calls=%fused_computation.10 | loop fusion | flops 102000 | bytes 104000 | tf_op jit(solution)/shard_map/reduce_sum | solution.py:8
  7.6 1.1 %fusion.6 = f32[10,40]{1,0:T(8,128)S(1)} fusion(bf16[10,40,128]{2,1,0:T(8,128)(2,1)} %param.4, f32[10,40]{1,0:T(8,128)S(1)} %broadcast_multiply_fusion.1), kind=kLoop, calls=%fused_computation.13 | loop fusion | flops 204400 | bytes 105600 | tf_op jit(solution)/shard_map/reduce_sum | solution.py:10
  8.8 1.1 %fusion.7 = bf16[10,40,128]{2,1,0:T(8,128)(2,1)S(1)} fusion(bf16[10,40,128]{2,1,0:T(8,128)(2,1)} %param.4, f32[10,40]{1,0:T(8,128)S(1)} %add_rsqrt_fusion.1, f32[10,40]{1,0:T(8,128)S(1)} %broadcast_multiply_fusion.1), kind=kLoop, calls=%fused_computation.14 | loop fusion | flops 204800 | bytes 208000 | tf_op jit(solution)/shard_map/convert_element_type | solution.py:17
  9.8 0.0 copy-done
  9.8 0.2 fusion.17
  10.1 0.0 copy-start.2
  10.1 0.1 fusion.8
  10.2 2.2 %all_gather.9 = bf16[10,80,128]{2,1,0:T(8,128)(2,1)} all-gather(bf16[10,40,128]{2,1,0:T(8,128)(2,1)S(1)} %bitcast.19), channel_id=1, replica_groups=mesh['groups'=2,'row'=8,'col'=2] {'col'}, dimensions={1}, use_global_device_ids=true | all-gather | bytes 307200 | tf_op jit(solution)/shard_map/all_gather | solution.py:31
  12.4 0.0 all-gather.2.cloned.1.call-update
  12.4 2.0 %all_gather.11 = bf16[10,80,128]{2,1,0:T(8,128)(2,1)S(1)} all-gather(bf16[10,40,128]{2,1,0:T(8,128)(2,1)S(1)} %bitcast.18), channel_id=1, replica_groups=mesh['groups'=2,'row'=8,'col'=2] {'col'}, dimensions={1}, use_global_device_ids=true | all-gather | bytes 307200 | tf_op jit(solution)/shard_map/all_gather | solution.py:30
  14.4 0.4 copy.11
  14.8 0.0 copy-done.2
  14.8 0.2 fusion.2
  15.0 44.7 %all-gather.2.cloned.1.call-done = bf16[80,80,128]{2,1,0:T(8,128)(2,1)} async-done(((bf16[10,80,128]{2,1,0:T(8,128)(2,1)}), bf16[80,80,128]{2,1,0:T(8,128)(2,1)}) %all-gather.2.cloned.1.call-update) | async-done | bytes 1638416 | tf_op jit(solution)/shard_map/all_gather | solution.py:33
  59.7 1.2 %constant_dynamic-slice_fusion = bf16[40,80,128]{2,1,0:T(8,128)(2,1)S(1)} fusion(bf16[80,80,128]{2,1,0:T(8,128)(2,1)} %all-gather.2.cloned.1.call-done, s32[]{:T(128)S(6)} %select_n.3), kind=kLoop, calls=%fused_computation.31 | loop fusion | bytes 1638404 | tf_op jit(solution)/shard_map/dynamic_slice | solution.py:34
  60.9 1.6 %copy.13 = bf16[40,80,128]{1,0,2:T(8,128)(2,1)S(1)} copy(bf16[40,80,128]{2,1,0:T(8,128)(2,1)S(1)} %constant_dynamic-slice_fusion) | data formatting | bytes 1638400
  62.5 0.8 %fusion.16 = (f32[10,40]{1,0:T(8,128)S(1)}, f32[10,40,128]{1,0,2:T(8,128)S(1)}) fusion(bf16[40,80,128]{1,0,2:T(8,128)(2,1)S(1)} %copy.13, bf16[10,80,128]{1,0,2:T(8,128)(2,1)S(1)} %copy.11), kind=kOutput, calls=%fused_computation.32 | convolution fusion | flops 8242800 | bytes 1230400 | tf_op jit(solution)/shard_map/ikc,jkc->ijc/dot_general | solution.py:37
  63.3 0.2 multiply_reduce_fusion
  63.5 0.0 copy-start.1
  63.6 0.1 multiply_convert_fusion
  63.7 0.4 copy.12
  64.0 0.3 copy-done.1
  64.3 0.8 %fusion.3 = bf16[400,128]{1,0:T(8,128)(2,1)} fusion(f32[400,128]{1,0:T(8,128)S(1)} %fusion.2, bf16[400,128]{1,0:T(8,128)(2,1)S(1)} %bitcast.15, bf16[128,128]{1,0:T(8,128)(2,1)S(1)} %copy-done.1), kind=kOutput, calls=%fused_computation.6 | convolution fusion | flops 13209600 | bytes 442368 | tf_op jit(solution)/shard_map/dot_general | solution.py:39
  (4 shorter events, 0.0 us)
Async XLA Ops:
  6.5 3.3 %copy-start = (bf16[128,512]{1,0:T(8,128)(2,1)S(1)}, bf16[128,512]{1,0:T(8,128)(2,1)}, u32[]{:S(2)}) copy-start(bf16[128,512]{1,0:T(8,128)(2,1)} %param.5) | copy-start | bytes 393220
  6.5 53.2 %all-gather.2.cloned.1.call-start = ((), (), s32[]{:S(2)}) async-start(), calls=%async_computation | async-start | bytes 1843200 | tf_op jit(solution)/shard_map/all_gather | solution.py:33
  10.1 4.7 %copy-start.2 = (bf16[128,128]{1,0:T(8,128)(2,1)S(1)}, bf16[128,128]{1,0:T(8,128)(2,1)}, u32[]{:S(2)}) copy-start(bf16[128,128]{1,0:T(8,128)(2,1)} %param.6) | copy-start | bytes 98308
  63.5 0.8 %copy-start.1 = (bf16[128,128]{1,0:T(8,128)(2,1)S(1)}, bf16[128,128]{1,0:T(8,128)(2,1)}, u32[]{:S(2)}) copy-start(bf16[128,128]{1,0:T(8,128)(2,1)} %param.7) | copy-start | bytes 98308
Sparse Core Ops, SparseCore 0:
  12.6 47.1 all-gather.1
where the time goes:
time: 72.3 us; the launch traced here: 72 us
  waiting for transfers between devices  44.7 us (62%)
  between operations  13.5 us (19%)
  blocking collectives  4.14 us (6%)
  local copies, waits for them, and re-layouts  3.85 us (5%)
  other arithmetic  3.7 us (5%)
  matrix products  2.08 us (3%)
    all_gather x1, waiting for transfers between devices, per_device(): right_all = lax.all_gather(right_strip, 'row', axis=0, tiled=True)  44.7 us
    all_gather x1, blocking collectives, per_device(): lax.all_gather(right_side, 'col', axis=1, tiled=True)  2.19 us
    all_gather x1, blocking collectives, per_device(): lax.all_gather(left_side, 'col', axis=1, tiled=True)  1.95 us
    unnamed x7, local copies, waits for them, and re-layouts  1.87 us
  transfers between devices with their start and end apart: 1, of which 1 were waited for; matrix products, arithmetic and copies ran while one was open for 1% of the time, Pallas kernels for 0%

commit v1 on v0

v1 whole, which is shorter than its diff:
```python
import functools

import jax
import jax.numpy as jnp
from jax import lax
from jax.experimental import pallas as pl
from jax.experimental.pallas import tpu as pltpu
from jax.sharding import PartitionSpec as P

F32, BF16 = jnp.float32, jnp.bfloat16
PLACED = P(("groups", "row"), "col", None)
VMEM_BUDGET = 24 * 2**20


def layer_norm(values):
    average = jnp.mean(values, axis=-1, keepdims=True)
    centered = values - average
    spread = jnp.mean(centered * centered, axis=-1, keepdims=True)
    return centered * lax.rsqrt(spread + 1e-05)


def sigmoid(values):
    return 0.5 * jnp.tanh(0.5 * values) + 0.5


def normalised(x_ref):
    x = x_ref[...].reshape(-1, x_ref.shape[-1]).astype(F32)
    return layer_norm(x).astype(BF16)


def side(normed, weight):
    both = jnp.dot(normed, weight, preferred_element_type=F32)
    hidden = both.shape[-1] // 2
    return (sigmoid(both[:, :hidden]) * both[:, hidden:]).astype(BF16).astype(F32)


def in_vmem(*arrays):
    return [pltpu.with_memory_space_constraint(a, pltpu.VMEM) for a in arrays]


def own_kernel(half, x_ref, w_ref, left_ref, right_ref):
    rows = x_ref.shape[0] * x_ref.shape[1]
    hidden = left_ref.shape[-1]
    normed = normalised(x_ref)
    left_ref[pl.ds(0, rows), :] = side(normed, w_ref[:, : 2 * hidden])
    place = lax.rem(lax.axis_index("row"), half)
    right_ref[pl.ds(pl.multiple_of(place * rows, 8), rows), :] = side(normed, w_ref[:, 2 * hidden :])


def early_kernel(half, steps, *refs):
    x_refs, (far_ref, w_ref, _, _, left_ref, right_ref) = refs[: len(steps)], refs[len(steps) :]
    rows = far_ref.shape[0] * far_ref.shape[1]
    hidden = left_ref.shape[-1]
    place = lax.rem(lax.axis_index("row"), half)
    left_ref[pl.ds(rows, rows), :] = side(normalised(far_ref), w_ref[:, : 2 * hidden])
    for step, x_ref in zip(steps, x_refs, strict=True):
        start = pl.multiple_of((place ^ step) * rows, 8)
        right_ref[pl.ds(start, rows), :] = side(normalised(x_ref), w_ref[:, 2 * hidden :])


def products(left_ref, right_ref, out_ref, strips, depth, group):
    count = out_ref.shape[0]
    for first in range(0, count, group):
        rows = range(first, min(first + group, count))

        def body(k, sums):
            rights = [right_ref[pl.ds(s * depth + k, 8, stride=depth), :] for s in strips]
            added = []
            for n, i in enumerate(rows):
                left = left_ref[pl.ds(i * depth + k, 1), :]
                added.append(tuple(a + left * r for a, r in zip(sums[n], rights, strict=True)))
            return tuple(added)

        zero = jnp.zeros((8, left_ref.shape[-1]), F32)
        sums = lax.fori_loop(0, depth, body, tuple(tuple(zero for _ in strips) for _ in rows), unroll=4)
        for n, i in enumerate(rows):
            for s, total in zip(strips, sums[n], strict=True):
                out_ref[i, pl.ds(s, 8), :] = total


def gate_kernel(half, x_ref, other_ref, g_ref, out_ref):
    ours = lax.axis_index("row") // half == lax.axis_index("col")
    x = jnp.where(ours, x_ref[...].astype(F32), other_ref[...].astype(F32))
    normed = layer_norm(x.reshape(-1, x.shape[-1])).astype(BF16)
    out_ref[...] = sigmoid(jnp.dot(normed, g_ref[...], preferred_element_type=F32))


def late_kernel(half, step, depth, x_ref, w_ref, left_ref, _, right_ref, keep_ref, give_ref):
    rows = x_ref.shape[0] * x_ref.shape[1]
    count, width = x_ref.shape[0], keep_ref.shape[1]
    hidden = left_ref.shape[-1]
    place = lax.rem(lax.axis_index("row"), half)
    ours = lax.axis_index("row") // half == lax.axis_index("col")
    start = pl.multiple_of((place ^ step) * rows, 8)
    right_ref[pl.ds(start, rows), :] = side(normalised(x_ref), w_ref[:, 2 * hidden :])
    strips = list(range(0, width, 8))

    def mine(offset):
        return left_ref.at[pl.ds(pl.multiple_of(offset * rows, 8), rows)]

    kept = jnp.where(ours, 0, 1)
    products(mine(1 - kept), right_ref, give_ref, strips, depth, 5)
    products(mine(kept), right_ref, keep_ref, strips, depth, 5)


def finish_kernel(keep_ref, got_ref, gating_ref, o_ref, out_ref):
    combined = keep_ref[...] + got_ref[...]
    tri = layer_norm(combined.reshape(-1, combined.shape[-1])).astype(BF16)
    update = jnp.dot(tri, o_ref[...], preferred_element_type=F32) * gating_ref[...]
    out_ref[...] = update.astype(BF16).reshape(out_ref.shape)


def choose_kernel(half, mine_ref, got_ref, out_ref):
    ours = lax.axis_index("row") // half == lax.axis_index("col")

    @pl.when(ours)
    def _():
        out_ref[...] = mine_ref[...]

    @pl.when(jnp.logical_not(ours))
    def _():
        out_ref[...] = got_ref[...]


def fast_plan(mesh, x, proj_weight, gate_weight, out_weight):
    rows_here, depth, _ = x.shape
    hidden = out_weight.shape[0]
    rows, half = mesh.shape["row"], mesh.shape["row"] // 2
    wide = half * rows_here
    positions = rows_here * depth
    call = functools.partial(pl.pallas_call, compiler_params=pltpu.CompilerParams(vmem_limit_bytes=40 * 2**20))

    def from_step(step):
        return lax.ppermute(x, "row", [(i, i ^ step) for i in range(rows)])

    far = from_step(half)
    steps = sorted(range(1, half), reverse=True)
    *early, last = [2, 1, 3] if half == 4 else steps
    blocks = {step: from_step(step) for step in steps}
    swap = [(0, 1), (1, 0)]
    far_other = lax.ppermute(far, "col", swap)
    x_v, w_v, g_v, o_v = in_vmem(x, proj_weight, gate_weight, out_weight)
    lefts, rights = pltpu.VMEM((2 * positions, hidden), F32), pltpu.VMEM((half * positions, hidden), F32)
    left, right = call(functools.partial(own_kernel, half), out_shape=(lefts, rights))(x_v, w_v)
    taken = in_vmem(*[blocks[s] for s in early], far)
    left, right = call(
        functools.partial(early_kernel, half, tuple(early)),
        out_shape=(lefts, rights),
        input_output_aliases={len(taken) + 1: 0, len(taken) + 2: 1},
    )(*taken, w_v, *in_vmem(left, right))
    gating = call(functools.partial(gate_kernel, half), out_shape=pltpu.VMEM((positions, hidden), F32))(
        x_v, *in_vmem(far_other), g_v
    )
    part = pltpu.VMEM((rows_here, wide, hidden), F32)
    _, keep, give = call(
        functools.partial(late_kernel, half, last, depth),
        out_shape=(rights, part, part),
        input_output_aliases={3: 0},
    )(*in_vmem(blocks[last]), w_v, *in_vmem(left, right))
    got = lax.ppermute(give, "col", swap)
    update = call(finish_kernel, out_shape=pltpu.VMEM(x.shape, BF16))(*in_vmem(keep, got, gating), o_v)
    pairs = [
        (2 * r + 1 - r // half, 2 * (r ^ half) + r // half)
        for r in range(rows)
    ]
    arrived = lax.ppermute(update, ("row", "col"), pairs)
    return call(
        functools.partial(choose_kernel, half),
        in_specs=[pl.BlockSpec(memory_space=pltpu.VMEM)] * 2,
        out_specs=pl.BlockSpec(memory_space=pltpu.VMEM),
        out_shape=jax.ShapeDtypeStruct(x.shape, BF16),
    )(*in_vmem(update, arrived))


def gather_plan(pair_rep, proj_weight, gate_weight, out_weight):
    rows_here, cols_here, channels = pair_rep.shape
    hidden = out_weight.shape[0]
    normed = layer_norm(pair_rep.astype(F32)).astype(BF16)
    flat_rows = normed.reshape(-1, channels)
    projected = jnp.dot(flat_rows, proj_weight, preferred_element_type=F32)
    left, right = (
        (jax.nn.sigmoid(projected[:, at : at + hidden]) * projected[:, at + hidden : at + 2 * hidden])
        .astype(BF16)
        .reshape(rows_here, cols_here, hidden)
        for at in (0, 2 * hidden)
    )
    gating = jax.nn.sigmoid(jnp.dot(flat_rows, gate_weight, preferred_element_type=F32))
    left_full = lax.all_gather(left, "col", axis=1, tiled=True)
    right_all = lax.all_gather(lax.all_gather(right, "col", axis=1, tiled=True), "row", axis=0, tiled=True)
    mine = lax.dynamic_slice_in_dim(right_all, lax.axis_index("col") * cols_here, cols_here, 0)
    combined = jnp.einsum("ikc,jkc->ijc", left_full, mine, preferred_element_type=F32)
    tri_normed = layer_norm(combined).astype(BF16).reshape(-1, hidden)
    update = jnp.dot(tri_normed, out_weight, preferred_element_type=F32) * gating
    return update.astype(BF16).reshape(rows_here, cols_here, channels)


def solution(mesh):
    def per_device(pair_rep, proj_weight, gate_weight, out_weight):
        rows_here, cols_here, channels = pair_rep.shape
        hidden = out_weight.shape[0]
        rows, cols = mesh.shape["row"], mesh.shape["col"]
        half = rows // 2
        held = 4 * hidden * (half + 3) * rows_here * cols_here + 12 * hidden * half * rows_here**2
        fits = held + 2 * half * pair_rep.size <= VMEM_BUDGET and channels == hidden
        even = cols == 2 and rows >= 4 and rows & (rows - 1) == 0 and half * rows_here == cols_here
        tiled = rows_here * cols_here % 16 == 0 and cols_here % 8 == 0 and channels % 128 == 0
        if fits and even and tiled:
            return fast_plan(mesh, pair_rep, proj_weight, gate_weight, out_weight)
        return gather_plan(pair_rep, proj_weight, gate_weight, out_weight)

    return jax.shard_map(
        per_device,
        mesh=mesh,
        in_specs=(PLACED, P(), P(), P()),
        out_specs=PLACED,
        check_vma=False,
    )
```

time: 72.3 us -> 25.8 us (0.36)
  the two profiles are of different devices: /device:TPU:0 before, /device:TPU:1 now
where the time goes in v1:
time: 25.8 us; the launch traced here: 25.7 us
  starting transfers between devices  10.8 us (42%)
  waiting for transfers between devices  8.53 us (33%)
  Pallas kernels  4.44 us (17%)
  local copies, waits for them, and re-layouts  1.81 us (7%)
    ppermute x4, starting transfers between devices, from_step(): return lax.ppermute(x, 'row', [(i, i ^ step) for i in range(rows)])  5.79 us
    ppermute x1, waiting for transfers between devices, fast_plan(): arrived = lax.ppermute(update, ('row', 'col'), pairs)  4.93 us
    ppermute x1, starting transfers between devices, fast_plan(): arrived = lax.ppermute(update, ('row', 'col'), pairs)  3.04 us
    ppermute x4, waiting for transfers between devices, from_step(): return lax.ppermute(x, 'row', [(i, i ^ step) for i in range(rows)])  2.38 us
    pallas_call x1, Pallas kernels, fast_plan(): call(functools.partial(late_kernel, half, last, depth), out_shape=(rights...  1.94 us
    ppermute x1, starting transfers between devices, fast_plan(): got = lax.ppermute(give, 'col', swap)  1.9 us
    unnamed x8, local copies, waits for them, and re-layouts  1.81 us
    ppermute x1, waiting for transfers between devices, fast_plan(): far_other = lax.ppermute(far, 'col', swap)  1.23 us
  transfers between devices with their start and end apart: 7, of which 4 were waited for; matrix products, arithmetic and copies ran while one was open for 0% of the time, Pallas kernels for 6%

profile of v1, /device:TPU:1, one launch (start us, length us, event | category | flops | bytes accessed | tf_op | source)
XLA Modules:
  0.0 25.7 jit_solution(9897158658713048106)
XLA Ops:
  0.0 3.1 %collective-permute-start.3 = (bf16[10,40,128]{2,1,0:T(8,128)(2,1)}, bf16[10,40,128]{2,1,0:T(8,128)(2,1)S(1)}, u32[]{:S(2)}, u32[]{:S(2)}) collective-permute-start(bf16[10,40,128]{2,1,0:T(8,128)(2,1)} %x_ref.3), channel_id=1, source_target_pairs={{0,8},{2,10},{4,12},{6,14},{8,0},{10,2},{12,4},{14,6},{1,9},{3,11}... | collective-permute-start | bytes 307208 | tf_op jit(solution)/shard_map/ppermute | solution.py:134
  3.1 1.3 %collective-permute-start.1 = (bf16[10,40,128]{2,1,0:T(8,128)(2,1)}, bf16[10,40,128]{2,1,0:T(8,128)(2,1)S(1)}, u32[]{:S(2)}, u32[]{:S(2)}) collective-permute-start(bf16[10,40,128]{2,1,0:T(8,128)(2,1)} %x_ref.3), channel_id=1, source_target_pairs={{0,4},{2,6},{4,0},{6,2},{8,12},{10,14},{12,8},{14,10},{1,5},{3,7},... | collective-permute-start | bytes 307208 | tf_op jit(solution)/shard_map/ppermute | solution.py:134
  4.4 1.2 %collective-permute-start.2 = (bf16[10,40,128]{2,1,0:T(8,128)(2,1)}, bf16[10,40,128]{2,1,0:T(8,128)(2,1)S(1)}, u32[]{:S(2)}, u32[]{:S(2)}) collective-permute-start(bf16[10,40,128]{2,1,0:T(8,128)(2,1)} %x_ref.3), channel_id=1, source_target_pairs={{0,2},{2,0},{4,6},{6,4},{8,10},{10,8},{12,14},{14,12},{1,3},{3,1},... | collective-permute-start | bytes 307208 | tf_op jit(solution)/shard_map/ppermute | solution.py:134
  5.7 0.1 collective-permute-start
  5.8 0.0 copy-start
  5.8 0.9 %copy-done = bf16[128,512]{1,0:T(8,128)(2,1)S(1)} copy-done((bf16[128,512]{1,0:T(8,128)(2,1)S(1)}, bf16[128,512]{1,0:T(8,128)(2,1)}, u32[]{:S(2)}) %copy-start) | copy-done | bytes 131096
  6.7 0.0 copy-start.1
  6.7 0.9 %copy-done.1 = bf16[10,40,128]{2,1,0:T(8,128)(2,1)S(1)} copy-done((bf16[10,40,128]{2,1,0:T(8,128)(2,1)S(1)}, bf16[10,40,128]{2,1,0:T(8,128)(2,1)}, u32[]{:S(2)}) %copy-start.1) | copy-done | bytes 102424
  7.6 0.5 %shard_map.46 = (f32[800,128]{1,0:T(8,128)S(1)}, f32[1600,128]{1,0:T(8,128)S(1)}) custom-call(bf16[10,40,128]{2,1,0:T(8,128)(2,1)S(1)} %copy-done.1, bf16[128,512]{1,0:T(8,128)(2,1)S(1)} %copy-done), custom_call_target="tpu_custom_call" | custom-call | tf_op jit(solution)/shard_map/pallas_call | solution.py:144
  8.1 0.0 collective-permute-done.3.refs_2_
  8.1 0.0 collective-permute-done.1.refs_0_
  8.1 0.3 %collective-permute-done.2.refs_1_ = bf16[10,40,128]{2,1,0:T(8,128)(2,1)S(1)} collective-permute-done((bf16[10,40,128]{2,1,0:T(8,128)(2,1)}, bf16[10,40,128]{2,1,0:T(8,128)(2,1)S(1)}, u32[]{:S(2)}, u32[]{:S(2)}) %collective-permute-start.2) | collective-permute-done | bytes 102432 | tf_op jit(solution)/shard_map/ppermute | solution.py:134
  8.5 0.6 %shard_map.47 = (f32[800,128]{1,0:T(8,128)S(1)}, f32[1600,128]{1,0:T(8,128)S(1)}) custom-call(bf16[10,40,128]{2,1,0:T(8,128)(2,1)S(1)} %collective-permute-done.1.refs_0_, bf16[10,40,128]{2,1,0:T(8,128)(2,1)S(1)} %collective-permute-done.2.refs_1_, ...), custom_call_target="tpu_custom_call", output_to_operand_aliasing={{0}: (4, {}), {1}: (5, {})} | custom-call | tf_op jit(solution)/shard_map/pallas_call | solution.py:146
  9.1 2.1 %collective-permute-done.x_ref = bf16[10,40,128]{2,1,0:T(8,128)(2,1)S(1)} collective-permute-done((bf16[10,40,128]{2,1,0:T(8,128)(2,1)}, bf16[10,40,128]{2,1,0:T(8,128)(2,1)S(1)}, u32[]{:S(2)}, u32[]{:S(2)}) %collective-permute-start) | collective-permute-done | bytes 102432 | tf_op jit(solution)/shard_map/ppermute | solution.py:134
  11.1 0.0 copy-start.2
  11.1 1.9 %shard_map.48 = (f32[1600,128]{1,0:T(8,128)S(1)}, f32[10,40,128]{2,1,0:T(8,128)S(1)}, f32[10,40,128]{2,1,0:T(8,128)S(1)}) custom-call(bf16[10,40,128]{2,1,0:T(8,128)(2,1)S(1)} %collective-permute-done.x_ref, bf16[128,512]{1,0:T(8,128)(2,1)S(1)} %copy-done, f32[800,128]{1,0:T(8,128)S(1)} %get-tuple-element.13.left_ref, ...), custom_call_target="tpu_custom_call", output_to_operand_aliasing={{0}: (3, {})} | custom-call | tf_op jit(solution)/shard_map/pallas_call | solution.py:155
  13.1 0.0 copy-start.3
  13.1 1.9 %collective-permute-start.4 = (f32[10,40,128]{2,1,0:T(8,128)S(1)}, f32[10,40,128]{2,1,0:T(8,128)S(1)}, u32[]{:S(2)}, u32[]{:S(2)}) collective-permute-start(f32[10,40,128]{2,1,0:T(8,128)S(1)} %get-tuple-element.16), channel_id=1, source_target_pairs={{0,1},{1,0},{2,3},{3,2},{4,5},{5,4},{6,7},{7,6},{8,9},{9,8},{10,11... | collective-permute-start | bytes 614408 | tf_op jit(solution)/shard_map/ppermute | solution.py:160
  15.0 0.1 collective-permute-start.5
  15.1 1.2 %collective-permute-done.5.other_ref = bf16[10,40,128]{2,1,0:T(8,128)(2,1)S(1)} collective-permute-done((bf16[10,40,128]{2,1,0:T(8,128)(2,1)S(1)}, bf16[10,40,128]{2,1,0:T(8,128)(2,1)S(1)}, u32[]{:S(2)}, u32[]{:S(2)}) %collective-permute-start.5) | collective-permute-done | bytes 102432 | tf_op jit(solution)/shard_map/ppermute | solution.py:141
  16.3 0.0 copy-done.2
  16.3 0.4 %shard_map.49.gating_ref = f32[400,128]{1,0:T(8,128)S(1)} custom-call(bf16[10,40,128]{2,1,0:T(8,128)(2,1)S(1)} %copy-done.1, bf16[10,40,128]{2,1,0:T(8,128)(2,1)S(1)} %collective-permute-done.5.other_ref, bf16[128,128]{1,0:T(8,128)(2,1)S(1)} %copy-done.2), custom_call_target="tpu_custom_call" | custom-call | tf_op jit(solution)/shard_map/pallas_call | solution.py:151
  16.7 0.0 collective-permute-done.4.got_ref
  16.7 0.0 copy-done.3
  16.7 0.4 %shard_map.50.mine_ref = bf16[10,40,128]{2,1,0:T(8,128)(2,1)S(1)} custom-call(f32[10,40,128]{2,1,0:T(8,128)S(1)} %get-tuple-element.15.keep_ref, f32[10,40,128]{2,1,0:T(8,128)S(1)} %collective-permute-done.4.got_ref, f32[400,128]{1,0:T(8,128)S(1)} %shard_map.49.gating_ref, bf16[128,128]{1,0:T(8,128)(2,1)S(1)} %copy-done.3), custom_call_target="tpu_custom_call" | custom-call | tf_op jit(solution)/shard_map/pallas_call | solution.py:161
  17.1 3.0 %collective-permute-start.6 = (bf16[10,40,128]{2,1,0:T(8,128)(2,1)S(1)}, bf16[10,40,128]{2,1,0:T(8,128)(2,1)S(1)}, u32[]{:S(2)}, u32[]{:S(2)}) collective-permute-start(bf16[10,40,128]{2,1,0:T(8,128)(2,1)S(1)} %shard_map.50.mine_ref), channel_id=1, source_target_pairs={{1,8},{3,10},{5,12},{7,14},{8,1},{10,3},{12,5},{14,7},{17,24},{19,... | collective-permute-start | bytes 307208 | tf_op jit(solution)/shard_map/ppermute | solution.py:166
  20.1 4.9 %collective-permute-done.6.got_ref = bf16[10,40,128]{2,1,0:T(8,128)(2,1)S(1)} collective-permute-done((bf16[10,40,128]{2,1,0:T(8,128)(2,1)S(1)}, bf16[10,40,128]{2,1,0:T(8,128)(2,1)S(1)}, u32[]{:S(2)}, u32[]{:S(2)}) %collective-permute-start.6) | collective-permute-done | bytes 102432 | tf_op jit(solution)/shard_map/ppermute | solution.py:166
  25.0 0.6 %shard_map.51 = bf16[10,40,128]{2,1,0:T(8,128)(2,1)} custom-call(bf16[10,40,128]{2,1,0:T(8,128)(2,1)S(1)} %shard_map.50.mine_ref, bf16[10,40,128]{2,1,0:T(8,128)(2,1)S(1)} %collective-permute-done.6.got_ref), custom_call_target="tpu_custom_call" | custom-call | tf_op jit(solution)/shard_map/pallas_call | solution.py:167
Async XLA Ops:
  0.0 8.1 %collective-permute-start.3 = (bf16[10,40,128]{2,1,0:T(8,128)(2,1)}, bf16[10,40,128]{2,1,0:T(8,128)(2,1)S(1)}, u32[]{:S(2)}, u32[]{:S(2)}) collective-permute-start(bf16[10,40,128]{2,1,0:T(8,128)(2,1)} %x_ref.3), channel_id=1, source_target_pairs={{0,8},{2,10},{4,12},{6,14},{8,0},{10,2},{12,4},{14,6},{1,9},{3,11}... | collective-permute-start | bytes 307208 | tf_op jit(solution)/shard_map/ppermute | solution.py:134
  3.1 5.0 %collective-permute-start.1 = (bf16[10,40,128]{2,1,0:T(8,128)(2,1)}, bf16[10,40,128]{2,1,0:T(8,128)(2,1)S(1)}, u32[]{:S(2)}, u32[]{:S(2)}) collective-permute-start(bf16[10,40,128]{2,1,0:T(8,128)(2,1)} %x_ref.3), channel_id=1, source_target_pairs={{0,4},{2,6},{4,0},{6,2},{8,12},{10,14},{12,8},{14,10},{1,5},{3,7},... | collective-permute-start | bytes 307208 | tf_op jit(solution)/shard_map/ppermute | solution.py:134
  4.4 4.0 %collective-permute-start.2 = (bf16[10,40,128]{2,1,0:T(8,128)(2,1)}, bf16[10,40,128]{2,1,0:T(8,128)(2,1)S(1)}, u32[]{:S(2)}, u32[]{:S(2)}) collective-permute-start(bf16[10,40,128]{2,1,0:T(8,128)(2,1)} %x_ref.3), channel_id=1, source_target_pairs={{0,2},{2,0},{4,6},{6,4},{8,10},{10,8},{12,14},{14,12},{1,3},{3,1},... | collective-permute-start | bytes 307208 | tf_op jit(solution)/shard_map/ppermute | solution.py:134
  5.7 5.4 %collective-permute-start = (bf16[10,40,128]{2,1,0:T(8,128)(2,1)}, bf16[10,40,128]{2,1,0:T(8,128)(2,1)S(1)}, u32[]{:S(2)}, u32[]{:S(2)}) collective-permute-start(bf16[10,40,128]{2,1,0:T(8,128)(2,1)} %x_ref.3), channel_id=1, source_target_pairs={{0,6},{2,4},{4,2},{6,0},{8,14},{10,12},{12,10},{14,8},{1,7},{3,5},... | collective-permute-start | bytes 307208 | tf_op jit(solution)/shard_map/ppermute | solution.py:134
  5.8 0.9 %copy-start = (bf16[128,512]{1,0:T(8,128)(2,1)S(1)}, bf16[128,512]{1,0:T(8,128)(2,1)}, u32[]{:S(2)}) copy-start(bf16[128,512]{1,0:T(8,128)(2,1)} %w_ref.3) | copy-start | bytes 393220
  6.7 0.9 %copy-start.1 = (bf16[10,40,128]{2,1,0:T(8,128)(2,1)S(1)}, bf16[10,40,128]{2,1,0:T(8,128)(2,1)}, u32[]{:S(2)}) copy-start(bf16[10,40,128]{2,1,0:T(8,128)(2,1)} %x_ref.3) | copy-start | bytes 307204
  11.1 5.2 %copy-start.2 = (bf16[128,128]{1,0:T(8,128)(2,1)S(1)}, bf16[128,128]{1,0:T(8,128)(2,1)}, u32[]{:S(2)}) copy-start(bf16[128,128]{1,0:T(8,128)(2,1)} %g_ref.1) | copy-start | bytes 98308
  13.1 3.6 %copy-start.3 = (bf16[128,128]{1,0:T(8,128)(2,1)S(1)}, bf16[128,128]{1,0:T(8,128)(2,1)}, u32[]{:S(2)}) copy-start(bf16[128,128]{1,0:T(8,128)(2,1)} %o_ref.1) | copy-start | bytes 98308
  13.1 3.6 %collective-permute-start.4 = (f32[10,40,128]{2,1,0:T(8,128)S(1)}, f32[10,40,128]{2,1,0:T(8,128)S(1)}, u32[]{:S(2)}, u32[]{:S(2)}) collective-permute-start(f32[10,40,128]{2,1,0:T(8,128)S(1)} %get-tuple-element.16), channel_id=1, source_target_pairs={{0,1},{1,0},{2,3},{3,2},{4,5},{5,4},{6,7},{7,6},{8,9},{9,8},{10,11... | collective-permute-start | bytes 614408 | tf_op jit(solution)/shard_map/ppermute | solution.py:160
  15.0 1.3 %collective-permute-start.5 = (bf16[10,40,128]{2,1,0:T(8,128)(2,1)S(1)}, bf16[10,40,128]{2,1,0:T(8,128)(2,1)S(1)}, u32[]{:S(2)}, u32[]{:S(2)}) collective-permute-start(bf16[10,40,128]{2,1,0:T(8,128)(2,1)S(1)} %collective-permute-done.3.refs_2_), channel_id=1, source_target_pairs={{0,1},{1,0},{2,3},{3,2},{4,5},{5,4},{6,7},{7,6},{8,9},{9,8},{10,11... | collective-permute-start | bytes 307208 | tf_op jit(solution)/shard_map/ppermute | solution.py:141
  17.1 8.0 %collective-permute-start.6 = (bf16[10,40,128]{2,1,0:T(8,128)(2,1)S(1)}, bf16[10,40,128]{2,1,0:T(8,128)(2,1)S(1)}, u32[]{:S(2)}, u32[]{:S(2)}) collective-permute-start(bf16[10,40,128]{2,1,0:T(8,128)(2,1)S(1)} %shard_map.50.mine_ref), channel_id=1, source_target_pairs={{1,8},{3,10},{5,12},{7,14},{8,1},{10,3},{12,5},{14,7},{17,24},{19,... | collective-permute-start | bytes 307208 | tf_op jit(solution)/shard_map/ppermute | solution.py:166

commit v2 on v1

v2 whole, which is shorter than its diff:
```python
import functools

import jax
import jax.numpy as jnp
from jax import lax
from jax.experimental import pallas as pl
from jax.experimental.pallas import tpu as pltpu
from jax.sharding import PartitionSpec as P

F32, BF16 = jnp.float32, jnp.bfloat16
PLACED = P(("groups", "row"), "col", None)
VMEM_BUDGET = 24 * 2**20


def layer_norm(values):
    average = jnp.mean(values, axis=-1, keepdims=True)
    centered = values - average
    spread = jnp.mean(centered * centered, axis=-1, keepdims=True)
    return centered * lax.rsqrt(spread + 1e-05)


def sigmoid(values):
    return 0.5 * jnp.tanh(0.5 * values) + 0.5


def normalised(x_ref):
    x = x_ref[...].reshape(-1, x_ref.shape[-1]).astype(F32)
    return layer_norm(x).astype(BF16)


def side(normed, weight):
    both = jnp.dot(normed, weight, preferred_element_type=F32)
    hidden = both.shape[-1] // 2
    return (sigmoid(both[:, :hidden]) * both[:, hidden:]).astype(BF16).astype(F32)


def in_vmem(*arrays):
    return [pltpu.with_memory_space_constraint(a, pltpu.VMEM) for a in arrays]


def place_of(half):
    row = lax.axis_index("row")
    return lax.rem(row, half), lax.div(row, half) == lax.axis_index("col")


def put_right(half, step, x_ref, w_ref, right_ref):
    rows, hidden = x_ref.shape[0] * x_ref.shape[1], right_ref.shape[-1]
    start = pl.multiple_of((place_of(half)[0] ^ step) * rows, 8)
    right_ref[pl.ds(start, rows), :] = side(normalised(x_ref), w_ref[:, 2 * hidden :])


def own_kernel(half, x_ref, w_ref, g_ref, o_ref, left_ref, right_ref, gate_ref, w_out, g_out, o_out, x_in, sems):
    pairs = ((x_ref, x_in), (w_ref, w_out), (g_ref, g_out), (o_ref, o_out))
    copies = [pltpu.make_async_copy(a, b, sems.at[n]) for n, (a, b) in enumerate(pairs)]
    for copy in copies:
        copy.start()
    for copy in copies:
        copy.wait()
    rows, hidden = gate_ref.shape
    normed = normalised(x_in)
    left_ref[pl.ds(0, rows), :] = side(normed, w_out[:, : 2 * hidden])
    start = pl.multiple_of(place_of(half)[0] * rows, 8)
    right_ref[pl.ds(start, rows), :] = side(normed, w_out[:, 2 * hidden :])
    gate_ref[...] = sigmoid(jnp.dot(normed, g_out[...], preferred_element_type=F32))


def products(left_ref, base, right_ref, strips, depth, out_ref, group):
    count = out_ref.shape[0]
    for first in range(0, count, group):
        rows = range(first, min(first + group, count))

        def body(k, sums):
            rights = [right_ref[pl.ds(s * depth + k, 8, stride=depth), :] for s in strips]
            added = []
            for n, i in enumerate(rows):
                left = left_ref[pl.ds(base + i * depth + k, 1), :]
                added.append(tuple(a + left * r for a, r in zip(sums[n], rights, strict=True)))
            return tuple(added)

        zero = jnp.zeros((8, left_ref.shape[-1]), F32)
        sums = lax.fori_loop(0, depth, body, tuple(tuple(zero for _ in strips) for _ in rows), unroll=4)
        for n, i in enumerate(rows):
            for s, total in zip(strips, sums[n], strict=True):
                out_ref[i, pl.ds(s, 8), :] = total


def strips_of(half, step, rows_here):
    bounds = [(p * rows_here // 8, -(-(p + 1) * rows_here // 8)) for p in range(half)]
    count, total = max(b - a for a, b in bounds), half * rows_here // 8
    first = jnp.minimum(lax.div((place_of(half)[0] ^ step) * rows_here, 8), total - count)
    early = [jnp.where(n < first, n, n + count) for n in range(total - count)]
    late = [first + n for n in range(count)]
    return [[pl.multiple_of(s * 8, 8) for s in strips] for strips in (early, late)]


def near_kernel(half, steps, last, depth, *refs):
    x_refs, (w_ref, left_ref, _, right_ref, tile_ref) = refs[: len(steps)], refs[len(steps) :]
    for step, x_ref in zip(steps, x_refs, strict=True):
        put_right(half, step, x_ref, w_ref, right_ref)
    early, _ = strips_of(half, last, tile_ref.shape[0])
    for n in range(0, len(early), 3):
        products(left_ref, 0, right_ref, early[n : n + 3], depth, tile_ref, 10)


def far_kernel(half, last, depth, far_ref, w_ref, right_ref, _, left_ref, tile_ref):
    rows, hidden = left_ref.shape[0] // 2, left_ref.shape[-1]
    left_ref[pl.ds(rows, rows), :] = side(normalised(far_ref), w_ref[:, : 2 * hidden])
    early, _ = strips_of(half, last, tile_ref.shape[0])
    for n in range(0, len(early), 3):
        products(left_ref, rows, right_ref, early[n : n + 3], depth, tile_ref, 10)


def late_kernel(half, step, depth, x_ref, w_ref, left_ref, tile_ref, other_ref, _, right_ref, keep_ref, give_ref):
    put_right(half, step, x_ref, w_ref, right_ref)
    ours = place_of(half)[1]
    keep_ref[...] = jnp.where(ours, tile_ref[...], other_ref[...])
    give_ref[...] = jnp.where(ours, other_ref[...], tile_ref[...])
    rows = left_ref.shape[0] // 2
    _, late = strips_of(half, step, keep_ref.shape[0])
    for ref, base in ((give_ref, jnp.where(ours, rows, 0)), (keep_ref, jnp.where(ours, 0, rows))):
        for n in range(0, len(late), 2):
            products(left_ref, pl.multiple_of(base, 8), right_ref, late[n : n + 2], depth, ref, 10)


def norm_kernel(keep_ref, got_ref, tri_ref):
    tri_ref[...] = layer_norm(keep_ref[...] + got_ref[...]).astype(BF16)


def finish_kernel(half, tri_ref, got_ref, gate_ref, o_ref, out_ref):
    tri = jnp.where(place_of(half)[1], tri_ref[...].astype(F32), got_ref[...].astype(F32)).astype(BF16)
    update = jnp.dot(tri.reshape(gate_ref.shape), o_ref[...], preferred_element_type=F32)
    out_ref[...] = (update * gate_ref[...]).astype(BF16).reshape(out_ref.shape)


def fast_plan(mesh, x, proj_weight, gate_weight, out_weight):
    rows_here, depth, _ = x.shape
    hidden = out_weight.shape[0]
    rows, half = mesh.shape["row"], mesh.shape["row"] // 2
    positions = rows_here * depth
    call = functools.partial(pl.pallas_call, compiler_params=pltpu.CompilerParams(vmem_limit_bytes=40 * 2**20))

    def from_step(step):
        return lax.ppermute(x, "row", [(i, i ^ step) for i in range(rows)])

    far = from_step(half)
    steps = sorted(range(1, half), reverse=True)
    *early, last = [3, 1, 2] if half == 4 else steps
    blocks = {step: from_step(step) for step in [*early, last]}
    lefts, rights = pltpu.VMEM((2 * positions, hidden), F32), pltpu.VMEM((half * positions, hidden), F32)
    part = pltpu.VMEM((rows_here, half * rows_here, hidden), F32)
    brought = (x, proj_weight, gate_weight, out_weight)
    left, right, gate, w_v, _, o_v = in_vmem(
        *call(
            functools.partial(own_kernel, half),
            in_specs=[pl.BlockSpec(memory_space=pltpu.HBM)] * 4,
            out_shape=(lefts, rights, pltpu.VMEM((positions, hidden), F32), *[pltpu.VMEM(a.shape, a.dtype) for a in brought[1:]]),
            scratch_shapes=[pltpu.VMEM(x.shape, x.dtype), pltpu.SemaphoreType.DMA((4,))],
        )(*[pltpu.with_memory_space_constraint(a, pltpu.HBM) for a in brought])
    )
    right, tile = in_vmem(
        *call(
            functools.partial(near_kernel, half, tuple(early), last, depth),
            out_shape=(rights, part),
            input_output_aliases={len(early) + 2: 0},
        )(*in_vmem(*[blocks[s] for s in early]), w_v, left, right)
    )
    left, far_tile = in_vmem(
        *call(
            functools.partial(far_kernel, half, last, depth),
            out_shape=(lefts, part),
            input_output_aliases={3: 0},
        )(*in_vmem(far), w_v, right, left)
    )
    _, keep, give = call(
        functools.partial(late_kernel, half, last, depth),
        out_shape=(rights, part, part),
        input_output_aliases={5: 0},
    )(*in_vmem(blocks[last]), w_v, left, tile, far_tile, right)
    got = lax.ppermute(give, "col", [(0, 1), (1, 0)])
    tri = call(norm_kernel, out_shape=pltpu.VMEM(x.shape, BF16))(*in_vmem(keep, got))
    pairs = [(2 * r + 1 - r // half, 2 * (r ^ half) + r // half) for r in range(rows)]
    pairs += [(2 * r + r // half, 2 * (r ^ 1) + r // half) for r in range(rows)]
    arrived = lax.ppermute(tri, ("row", "col"), pairs)
    return call(
        functools.partial(finish_kernel, half),
        in_specs=[pl.BlockSpec(memory_space=pltpu.VMEM)] * 4,
        out_specs=pl.BlockSpec(memory_space=pltpu.VMEM),
        out_shape=jax.ShapeDtypeStruct(x.shape, BF16),
    )(*in_vmem(tri, arrived), gate, o_v)


def gather_plan(pair_rep, proj_weight, gate_weight, out_weight):
    rows_here, cols_here, channels = pair_rep.shape
    hidden = out_weight.shape[0]
    normed = layer_norm(pair_rep.astype(F32)).astype(BF16)
    flat_rows = normed.reshape(-1, channels)
    projected = jnp.dot(flat_rows, proj_weight, preferred_element_type=F32)
    left, right = (
        (jax.nn.sigmoid(projected[:, at : at + hidden]) * projected[:, at + hidden : at + 2 * hidden])
        .astype(BF16)
        .reshape(rows_here, cols_here, hidden)
        for at in (0, 2 * hidden)
    )
    gating = jax.nn.sigmoid(jnp.dot(flat_rows, gate_weight, preferred_element_type=F32))
    left_full = lax.all_gather(left, "col", axis=1, tiled=True)
    right_all = lax.all_gather(lax.all_gather(right, "col", axis=1, tiled=True), "row", axis=0, tiled=True)
    mine = lax.dynamic_slice_in_dim(right_all, lax.axis_index("col") * cols_here, cols_here, 0)
    combined = jnp.einsum("ikc,jkc->ijc", left_full, mine, preferred_element_type=F32)
    tri_normed = layer_norm(combined).astype(BF16).reshape(-1, hidden)
    update = jnp.dot(tri_normed, out_weight, preferred_element_type=F32) * gating
    return update.astype(BF16).reshape(rows_here, cols_here, channels)


def solution(mesh):
    def per_device(pair_rep, proj_weight, gate_weight, out_weight):
        rows_here, cols_here, channels = pair_rep.shape
        hidden = out_weight.shape[0]
        rows, cols = mesh.shape["row"], mesh.shape["col"]
        half = rows // 2
        held = 4 * hidden * (half + 3) * rows_here * cols_here + 12 * hidden * half * rows_here**2
        fits = held + 2 * half * pair_rep.size <= VMEM_BUDGET and channels == hidden
        even = cols == 2 and rows >= 4 and rows & (rows - 1) == 0 and half * rows_here == cols_here
        tiled = rows_here * cols_here % 16 == 0 and cols_here % 8 == 0 and channels % 128 == 0
        if fits and even and tiled:
            return fast_plan(mesh, pair_rep, proj_weight, gate_weight, out_weight)
        return gather_plan(pair_rep, proj_weight, gate_weight, out_weight)

    return jax.shard_map(
        per_device,
        mesh=mesh,
        in_specs=(PLACED, P(), P(), P()),
        out_specs=PLACED,
        check_vma=False,
    )
```

time: 25.8 us -> 21.1 us (0.82)
  the two profiles are of different devices: /device:TPU:1 before, /device:TPU:26 now
where the time goes in v2:
time: 21.1 us; the launch traced here: 20.7 us
  waiting for transfers between devices  11.3 us (54%)
  Pallas kernels  5.42 us (26%)
  starting transfers between devices  3.97 us (19%)
    ppermute x1, waiting for transfers between devices, fast_plan(): arrived = lax.ppermute(tri, ('row', 'col'), pairs)  4.97 us
    ppermute x4, waiting for transfers between devices, from_step(): return lax.ppermute(x, 'row', [(i, i ^ step) for i in range(rows)])  4.86 us
    ppermute x4, starting transfers between devices, from_step(): return lax.ppermute(x, 'row', [(i, i ^ step) for i in range(rows)])  3.82 us
    pallas_call x1, Pallas kernels, fast_plan(): call(functools.partial(own_kernel, half), in_specs=[pl.BlockSpec(memory_s...  1.61 us
    ppermute x1, waiting for transfers between devices, fast_plan(): got = lax.ppermute(give, 'col', [(0, 1), (1, 0)])  1.44 us
    pallas_call x1, Pallas kernels, fast_plan(): call(functools.partial(late_kernel, half, last, depth), out_shape=(rights...  0.98 us
    pallas_call x1, Pallas kernels, fast_plan(): call(functools.partial(near_kernel, half, tuple(early), last, depth), out...  0.95 us
    pallas_call x1, Pallas kernels, fast_plan(): call(functools.partial(finish_kernel, half), in_specs=[pl.BlockSpec(memor...  0.85 us
  transfers between devices with their start and end apart: 6, of which 3 were waited for; matrix products, arithmetic and copies ran while one was open for 0% of the time, Pallas kernels for 16%

profile of v2, /device:TPU:26, one launch (start us, length us, event | category | flops | bytes accessed | tf_op | source)
XLA Modules:
  0.0 20.7 jit_solution(944107843223908919)
XLA Ops:
  0.0 1.5 %collective-permute-start.3 = (bf16[10,40,128]{2,1,0:T(8,128)(2,1)}, bf16[10,40,128]{2,1,0:T(8,128)(2,1)S(1)}, u32[]{:S(2)}, u32[]{:S(2)}) collective-permute-start(bf16[10,40,128]{2,1,0:T(8,128)(2,1)} %x_ref.1), channel_id=1, source_target_pairs={{0,2},{2,0},{4,6},{6,4},{8,10},{10,8},{12,14},{14,12},{1,3},{3,1},... | collective-permute-start | bytes 307208 | tf_op jit(solution)/shard_map/ppermute | solution.py:143
  1.5 0.4 %collective-permute-start.2 = (bf16[10,40,128]{2,1,0:T(8,128)(2,1)}, bf16[10,40,128]{2,1,0:T(8,128)(2,1)S(1)}, u32[]{:S(2)}, u32[]{:S(2)}) collective-permute-start(bf16[10,40,128]{2,1,0:T(8,128)(2,1)} %x_ref.1), channel_id=1, source_target_pairs={{0,6},{2,4},{4,2},{6,0},{8,14},{10,12},{12,10},{14,8},{1,7},{3,5},... | collective-permute-start | bytes 307208 | tf_op jit(solution)/shard_map/ppermute | solution.py:143
  1.9 0.3 %collective-permute-start.1 = (bf16[10,40,128]{2,1,0:T(8,128)(2,1)}, bf16[10,40,128]{2,1,0:T(8,128)(2,1)S(1)}, u32[]{:S(2)}, u32[]{:S(2)}) collective-permute-start(bf16[10,40,128]{2,1,0:T(8,128)(2,1)} %x_ref.1), channel_id=1, source_target_pairs={{0,8},{2,10},{4,12},{6,14},{8,0},{10,2},{12,4},{14,6},{1,9},{3,11}... | collective-permute-start | bytes 307208 | tf_op jit(solution)/shard_map/ppermute | solution.py:143
  2.2 1.6 %collective-permute-start = (bf16[10,40,128]{2,1,0:T(8,128)(2,1)}, bf16[10,40,128]{2,1,0:T(8,128)(2,1)S(1)}, u32[]{:S(2)}, u32[]{:S(2)}) collective-permute-start(bf16[10,40,128]{2,1,0:T(8,128)(2,1)} %x_ref.1), channel_id=1, source_target_pairs={{0,4},{2,6},{4,0},{6,2},{8,12},{10,14},{12,8},{14,10},{1,5},{3,7},... | collective-permute-start | bytes 307208 | tf_op jit(solution)/shard_map/ppermute | solution.py:143
  3.8 1.6 %shard_map.46 = (f32[800,128]{1,0:T(8,128)S(1)}, f32[1600,128]{1,0:T(8,128)S(1)}, f32[400,128]{1,0:T(8,128)S(1)}, bf16[128,512]{1,0:T(8,128)(2,1)S(1)}, bf16[128...) custom-call(bf16[10,40,128]{2,1,0:T(8,128)(2,1)} %x_ref.1, bf16[128,512]{1,0:T(8,128)(2,1)} %w_ref.1, ...), custom_call_target="tpu_custom_call" | custom-call | tf_op jit(solution)/shard_map/pallas_call | solution.py:153
  5.4 0.0 collective-permute-done.3.refs_1_
  5.5 4.9 %collective-permute-done.2.refs_0_ = bf16[10,40,128]{2,1,0:T(8,128)(2,1)S(1)} collective-permute-done((bf16[10,40,128]{2,1,0:T(8,128)(2,1)}, bf16[10,40,128]{2,1,0:T(8,128)(2,1)S(1)}, u32[]{:S(2)}, u32[]{:S(2)}) %collective-permute-start.2) | collective-permute-done | bytes 102432 | tf_op jit(solution)/shard_map/ppermute | solution.py:143
  10.3 1.0 %shard_map.47 = (f32[1600,128]{1,0:T(8,128)S(1)}, f32[10,40,128]{2,1,0:T(8,128)S(1)}) custom-call(bf16[10,40,128]{2,1,0:T(8,128)(2,1)S(1)} %collective-permute-done.2.refs_0_, bf16[10,40,128]{2,1,0:T(8,128)(2,1)S(1)} %collective-permute-done.3.refs_1_, bf16[128,512]{1,0:T(8,128)(2,1)S(1)} %get-tuple-element.16.refs_2_.w_ref, ...), custom_call_target="tpu_custom_call", output_to_operand_aliasing={{0}: (4, {})} | custom-call | tf_op jit(solution)/shard_map/pallas_call | solution.py:161
  11.3 0.0 collective-permute-done.1.far_ref
  11.3 0.8 %shard_map.48 = (f32[800,128]{1,0:T(8,128)S(1)}, f32[10,40,128]{2,1,0:T(8,128)S(1)}) custom-call(bf16[10,40,128]{2,1,0:T(8,128)(2,1)S(1)} %collective-permute-done.1.far_ref, bf16[128,512]{1,0:T(8,128)(2,1)S(1)} %get-tuple-element.16.refs_2_.w_ref, f32[1600,128]{1,0:T(8,128)S(1)} %get-tuple-element.19.right_ref._, ...), custom_call_target="tpu_custom_call", output_to_operand_aliasing={{0}: (3, {})} | custom-call | tf_op jit(solution)/shard_map/pallas_call | solution.py:168
  12.1 0.0 collective-permute-done.x_ref
  12.1 1.0 %shard_map.49 = (f32[1600,128]{1,0:T(8,128)S(1)}, f32[10,40,128]{2,1,0:T(8,128)S(1)}, f32[10,40,128]{2,1,0:T(8,128)S(1)}) custom-call(bf16[10,40,128]{2,1,0:T(8,128)(2,1)S(1)} %collective-permute-done.x_ref, bf16[128,512]{1,0:T(8,128)(2,1)S(1)} %get-tuple-element.16.refs_2_.w_ref, ...), custom_call_target="tpu_custom_call", output_to_operand_aliasing={{0}: (5, {})} | custom-call | tf_op jit(solution)/shard_map/pallas_call | solution.py:174
  13.1 0.1 collective-permute-start.4
  13.2 1.4 %collective-permute-done.4.got_ref = f32[10,40,128]{2,1,0:T(8,128)S(1)} collective-permute-done((f32[10,40,128]{2,1,0:T(8,128)S(1)}, f32[10,40,128]{2,1,0:T(8,128)S(1)}, u32[]{:S(2)}, u32[]{:S(2)}) %collective-permute-start.4) | collective-permute-done | bytes 204832 | tf_op jit(solution)/shard_map/ppermute | solution.py:179
  14.6 0.2 %shard_map.50.tri_ref = bf16[10,40,128]{2,1,0:T(8,128)(2,1)S(1)} custom-call(f32[10,40,128]{2,1,0:T(8,128)S(1)} %get-tuple-element.23.keep_ref, f32[10,40,128]{2,1,0:T(8,128)S(1)} %collective-permute-done.4.got_ref), custom_call_target="tpu_custom_call" | custom-call | tf_op jit(solution)/shard_map/pallas_call | solution.py:180
  14.8 0.1 collective-permute-start.5
  14.9 5.0 %collective-permute-done.5.got_ref = bf16[10,40,128]{2,1,0:T(8,128)(2,1)S(1)} collective-permute-done((bf16[10,40,128]{2,1,0:T(8,128)(2,1)S(1)}, bf16[10,40,128]{2,1,0:T(8,128)(2,1)S(1)}, u32[]{:S(2)}, u32[]{:S(2)}) %collective-permute-start.5) | collective-permute-done | bytes 102432 | tf_op jit(solution)/shard_map/ppermute | solution.py:183
  19.9 0.9 %shard_map.51 = bf16[10,40,128]{2,1,0:T(8,128)(2,1)} custom-call(bf16[10,40,128]{2,1,0:T(8,128)(2,1)S(1)} %shard_map.50.tri_ref, bf16[10,40,128]{2,1,0:T(8,128)(2,1)S(1)} %collective-permute-done.5.got_ref, f32[400,128]{1,0:T(8,128)S(1)} %get-tuple-element.25.gate_ref, bf16[128,128]{1,0:T(8,128)(2,1)S(1)} %get-tuple-element.26.o_ref), custom_call_target="tpu_custom_call" | custom-call | tf_op jit(solution)/shard_map/pallas_call | solution.py:184
Async XLA Ops:
  0.0 5.4 %collective-permute-start.3 = (bf16[10,40,128]{2,1,0:T(8,128)(2,1)}, bf16[10,40,128]{2,1,0:T(8,128)(2,1)S(1)}, u32[]{:S(2)}, u32[]{:S(2)}) collective-permute-start(bf16[10,40,128]{2,1,0:T(8,128)(2,1)} %x_ref.1), channel_id=1, source_target_pairs={{0,2},{2,0},{4,6},{6,4},{8,10},{10,8},{12,14},{14,12},{1,3},{3,1},... | collective-permute-start | bytes 307208 | tf_op jit(solution)/shard_map/ppermute | solution.py:143
  1.5 8.8 %collective-permute-start.2 = (bf16[10,40,128]{2,1,0:T(8,128)(2,1)}, bf16[10,40,128]{2,1,0:T(8,128)(2,1)S(1)}, u32[]{:S(2)}, u32[]{:S(2)}) collective-permute-start(bf16[10,40,128]{2,1,0:T(8,128)(2,1)} %x_ref.1), channel_id=1, source_target_pairs={{0,6},{2,4},{4,2},{6,0},{8,14},{10,12},{12,10},{14,8},{1,7},{3,5},... | collective-permute-start | bytes 307208 | tf_op jit(solution)/shard_map/ppermute | solution.py:143
  1.9 9.4 %collective-permute-start.1 = (bf16[10,40,128]{2,1,0:T(8,128)(2,1)}, bf16[10,40,128]{2,1,0:T(8,128)(2,1)S(1)}, u32[]{:S(2)}, u32[]{:S(2)}) collective-permute-start(bf16[10,40,128]{2,1,0:T(8,128)(2,1)} %x_ref.1), channel_id=1, source_target_pairs={{0,8},{2,10},{4,12},{6,14},{8,0},{10,2},{12,4},{14,6},{1,9},{3,11}... | collective-permute-start | bytes 307208 | tf_op jit(solution)/shard_map/ppermute | solution.py:143
  2.2 9.8 %collective-permute-start = (bf16[10,40,128]{2,1,0:T(8,128)(2,1)}, bf16[10,40,128]{2,1,0:T(8,128)(2,1)S(1)}, u32[]{:S(2)}, u32[]{:S(2)}) collective-permute-start(bf16[10,40,128]{2,1,0:T(8,128)(2,1)} %x_ref.1), channel_id=1, source_target_pairs={{0,4},{2,6},{4,0},{6,2},{8,12},{10,14},{12,8},{14,10},{1,5},{3,7},... | collective-permute-start | bytes 307208 | tf_op jit(solution)/shard_map/ppermute | solution.py:143
  13.1 1.5 %collective-permute-start.4 = (f32[10,40,128]{2,1,0:T(8,128)S(1)}, f32[10,40,128]{2,1,0:T(8,128)S(1)}, u32[]{:S(2)}, u32[]{:S(2)}) collective-permute-start(f32[10,40,128]{2,1,0:T(8,128)S(1)} %get-tuple-element.24), channel_id=1, source_target_pairs={{0,1},{1,0},{2,3},{3,2},{4,5},{5,4},{6,7},{7,6},{8,9},{9,8},{10,11... | collective-permute-start | bytes 614408 | tf_op jit(solution)/shard_map/ppermute | solution.py:179
  14.8 5.0 %collective-permute-start.5 = (bf16[10,40,128]{2,1,0:T(8,128)(2,1)S(1)}, bf16[10,40,128]{2,1,0:T(8,128)(2,1)S(1)}, u32[]{:S(2)}, u32[]{:S(2)}) collective-permute-start(bf16[10,40,128]{2,1,0:T(8,128)(2,1)S(1)} %shard_map.50.tri_ref), channel_id=1, source_target_pairs={{1,8},{3,10},{5,12},{7,14},{8,1},{10,3},{12,5},{14,7},{0,2},{2,0},... | collective-permute-start | bytes 307208 | tf_op jit(solution)/shard_map/ppermute | solution.py:183

commit v3 on v2

--- a/solution.py
+++ b/solution.py
@@ -1,4 +1,5 @@
 import functools
+import itertools
 
 import jax
 import jax.numpy as jnp
@@ -64,13 +65,14 @@
     gate_ref[...] = sigmoid(jnp.dot(normed, g_out[...], preferred_element_type=F32))
 
 
-def products(left_ref, base, right_ref, strips, depth, out_ref, group):
+def products(left_ref, base, right_ref, strips, places, out_ref):
     count = out_ref.shape[0]
-    for first in range(0, count, group):
-        rows = range(first, min(first + group, count))
+    depth = left_ref.shape[0] // (2 * count)
+    for first, at in itertools.product(range(0, count, 10), range(0, len(strips), 3)):
+        rows, some = range(first, min(first + 10, count)), strips[at : at + 3]
 
         def body(k, sums):
-            rights = [right_ref[pl.ds(s * depth + k, 8, stride=depth), :] for s in strips]
+            rights = [right_ref[pl.ds(s * depth + k, 8, stride=depth), :] for s in some]
             added = []
             for n, i in enumerate(rows):
                 left = left_ref[pl.ds(base + i * depth + k, 1), :]
@@ -78,48 +80,52 @@
             return tuple(added)
 
         zero = jnp.zeros((8, left_ref.shape[-1]), F32)
-        sums = lax.fori_loop(0, depth, body, tuple(tuple(zero for _ in strips) for _ in rows), unroll=4)
+        sums = lax.fori_loop(0, depth, body, tuple(tuple(zero for _ in some) for _ in rows), unroll=4)
         for n, i in enumerate(rows):
-            for s, total in zip(strips, sums[n], strict=True):
-                out_ref[i, pl.ds(s, 8), :] = total
-
-
-def strips_of(half, step, rows_here):
-    bounds = [(p * rows_here // 8, -(-(p + 1) * rows_here // 8)) for p in range(half)]
-    count, total = max(b - a for a, b in bounds), half * rows_here // 8
-    first = jnp.minimum(lax.div((place_of(half)[0] ^ step) * rows_here, 8), total - count)
-    early = [jnp.where(n < first, n, n + count) for n in range(total - count)]
-    late = [first + n for n in range(count)]
+            for place, total in zip(places[at : at + 3], sums[n], strict=True):
+                out_ref[i, pl.ds(place, 8), :] = total
+
+
+def strips_of(half, rows_here):
+    part = half // 2 * rows_here
+    total = half * rows_here // 8
+    count = min(part // 8, total - -(-part // 8))
+    second = lax.div(place_of(half)[0], half // 2)
+    early = [second * (total - count) + n for n in range(count)]
+    late = [(1 - second) * count + n for n in range(total - count)]
     return [[pl.multiple_of(s * 8, 8) for s in strips] for strips in (early, late)]
 
 
-def near_kernel(half, steps, last, depth, *refs):
-    x_refs, (w_ref, left_ref, _, right_ref, tile_ref) = refs[: len(steps)], refs[len(steps) :]
-    for step, x_ref in zip(steps, x_refs, strict=True):
-        put_right(half, step, x_ref, w_ref, right_ref)
-    early, _ = strips_of(half, last, tile_ref.shape[0])
-    for n in range(0, len(early), 3):
-        products(left_ref, 0, right_ref, early[n : n + 3], depth, tile_ref, 10)
-
-
-def far_kernel(half, last, depth, far_ref, w_ref, right_ref, _, left_ref, tile_ref):
+def right_kernel(half, step, x_ref, w_ref, _, right_ref):
+    put_right(half, step, x_ref, w_ref, right_ref)
+
+
+def near_kernel(half, step, x_ref, w_ref, left_ref, _, right_ref, tile_ref):
+    put_right(half, step, x_ref, w_ref, right_ref)
+    early, _ = strips_of(half, tile_ref.shape[0])
+    products(left_ref, 0, right_ref, early, range(0, tile_ref.shape[1], 8), tile_ref)
+
+
+def far_kernel(half, far_ref, w_ref, right_ref, _, left_ref, tile_ref):
     rows, hidden = left_ref.shape[0] // 2, left_ref.shape[-1]
     left_ref[pl.ds(rows, rows), :] = side(normalised(far_ref), w_ref[:, : 2 * hidden])
-    early, _ = strips_of(half, last, tile_ref.shape[0])
-    for n in range(0, len(early), 3):
-        products(left_ref, rows, right_ref, early[n : n + 3], depth, tile_ref, 10)
-
-
-def late_kernel(half, step, depth, x_ref, w_ref, left_ref, tile_ref, other_ref, _, right_ref, keep_ref, give_ref):
+    early, _ = strips_of(half, tile_ref.shape[0])
+    products(left_ref, rows, right_ref, early, range(0, tile_ref.shape[1], 8), tile_ref)
+
+
+def whole_tile(half, given, left_ref, right_ref, own_ref, far_ref, out_ref):
+    own = place_of(half)[1] != given
+    early, late = strips_of(half, out_ref.shape[0])
+    for n, s in enumerate(early):
+        here = slice(8 * n, 8 * n + 8)
+        out_ref[:, pl.ds(s, 8), :] = jnp.where(own, own_ref[:, here, :], far_ref[:, here, :])
+    base = pl.multiple_of(jnp.where(own, 0, left_ref.shape[0] // 2), 8)
+    products(left_ref, base, right_ref, late, late, out_ref)
+
+
+def late_kernel(half, step, x_ref, w_ref, left_ref, own_ref, far_ref, _, right_ref, give_ref):
     put_right(half, step, x_ref, w_ref, right_ref)
-    ours = place_of(half)[1]
-    keep_ref[...] = jnp.where(ours, tile_ref[...], other_ref[...])
-    give_ref[...] = jnp.where(ours, other_ref[...], tile_ref[...])
-    rows = left_ref.shape[0] // 2
-    _, late = strips_of(half, step, keep_ref.shape[0])
-    for ref, base in ((give_ref, jnp.where(ours, rows, 0)), (keep_ref, jnp.where(ours, 0, rows))):
-        for n in range(0, len(late), 2):
-            products(left_ref, pl.multiple_of(base, 8), right_ref, late[n : n + 2], depth, ref, 10)
+    whole_tile(half, True, left_ref, right_ref, own_ref, far_ref, give_ref)
 
 
 def norm_kernel(keep_ref, got_ref, tri_ref):
@@ -143,11 +149,8 @@
         return lax.ppermute(x, "row", [(i, i ^ step) for i in range(rows)])
 
     far = from_step(half)
-    steps = sorted(range(1, half), reverse=True)
-    *early, last = [3, 1, 2] if half == 4 else steps
-    blocks = {step: from_step(step) for step in [*early, last]}
+    blocks = {step: from_step(step) for step in range(1, half)}
     lefts, rights = pltpu.VMEM((2 * positions, hidden), F32), pltpu.VMEM((half * positions, hidden), F32)
-    part = pltpu.VMEM((rows_here, half * rows_here, hidden), F32)
     brought = (x, proj_weight, gate_weight, out_weight)
     left, right, gate, w_v, _, o_v = in_vmem(
         *call(
@@ -157,26 +160,37 @@
             scratch_shapes=[pltpu.VMEM(x.shape, x.dtype), pltpu.SemaphoreType.DMA((4,))],
         )(*[pltpu.with_memory_space_constraint(a, pltpu.HBM) for a in brought])
     )
-    right, tile = in_vmem(
+
+    def with_block(step, right):
+        body = functools.partial(right_kernel, half, step)
+        return call(body, out_shape=rights, input_output_aliases={2: 0})(*in_vmem(blocks[step]), w_v, *in_vmem(right))
+
+    def with_far(left, right):
+        return in_vmem(
+            *call(functools.partial(far_kernel, half), out_shape=(lefts, early_part), input_output_aliases={3: 0})(
+                *in_vmem(far), w_v, *in_vmem(right), left
+            )
+        )
+
+    for step in range(half // 2 - 1, 1, -1):
+        right = with_block(step, right)
+    early_part = pltpu.VMEM((rows_here, 8 * len(strips_of(half, rows_here)[0]), hidden), F32)
+    tile_part = pltpu.VMEM((rows_here, half * rows_here, hidden), F32)
+    right, own_early = in_vmem(
+        *call(functools.partial(near_kernel, half, 1), out_shape=(rights, early_part), input_output_aliases={3: 0})(
+            *in_vmem(blocks[1]), w_v, left, *in_vmem(right)
+        )
+    )
+    for step in range(half - 1, half // 2, -1):
+        right = with_block(step, right)
+    left, far_early = with_far(left, right)
+    right, give = in_vmem(
         *call(
-            functools.partial(near_kernel, half, tuple(early), last, depth),
-            out_shape=(rights, part),
-            input_output_aliases={len(early) + 2: 0},
-        )(*in_vmem(*[blocks[s] for s in early]), w_v, left, right)
-    )
-    left, far_tile = in_vmem(
-        *call(
-            functools.partial(far_kernel, half, last, depth),
-            out_shape=(lefts, part),
-            input_output_aliases={3: 0},
-        )(*in_vmem(far), w_v, right, left)
-    )
-    _, keep, give = call(
-        functools.partial(late_kernel, half, last, depth),
-        out_shape=(rights, part, part),
-        input_output_aliases={5: 0},
-    )(*in_vmem(blocks[last]), w_v, left, tile, far_tile, right)
+            functools.partial(late_kernel, half, half // 2), out_shape=(rights, tile_part), input_output_aliases={5: 0}
+        )(*in_vmem(blocks[half // 2]), w_v, left, own_early, far_early, *in_vmem(right))
+    )
     got = lax.ppermute(give, "col", [(0, 1), (1, 0)])
+    keep = call(functools.partial(whole_tile, half, False), out_shape=tile_part)(left, right, own_early, far_early)
     tri = call(norm_kernel, out_shape=pltpu.VMEM(x.shape, BF16))(*in_vmem(keep, got))
     pairs = [(2 * r + 1 - r // half, 2 * (r ^ half) + r // half) for r in range(rows)]
     pairs += [(2 * r + r // half, 2 * (r ^ 1) + r // half) for r in range(rows)]

time: 21.1 us -> 20.6 us (0.976)
  the two profiles are of different devices: /device:TPU:26 before, /device:TPU:1 now
where the time goes in v3:
time: 20.6 us; the launch traced here: 20.4 us
  starting transfers between devices  9.36 us (45%)
  Pallas kernels  5.65 us (27%)
  waiting for transfers between devices  5.32 us (26%)
    ppermute x4, starting transfers between devices, from_step(): return lax.ppermute(x, 'row', [(i, i ^ step) for i in range(rows)])  5.79 us
    ppermute x1, waiting for transfers between devices, fast_plan(): arrived = lax.ppermute(tri, ('row', 'col'), pairs)  2.82 us
    ppermute x1, starting transfers between devices, fast_plan(): arrived = lax.ppermute(tri, ('row', 'col'), pairs)  2.23 us
    ppermute x4, waiting for transfers between devices, from_step(): return lax.ppermute(x, 'row', [(i, i ^ step) for i in range(rows)])  1.89 us
    pallas_call x1, Pallas kernels, fast_plan(): call(functools.partial(own_kernel, half), in_specs=[pl.BlockSpec(memory_s...  1.61 us
    ppermute x1, starting transfers between devices, fast_plan(): got = lax.ppermute(give, 'col', [(0, 1), (1, 0)])  1.35 us
    pallas_call x1, Pallas kernels, fast_plan(): call(functools.partial(finish_kernel, half), in_specs=[pl.BlockSpec(memor...  0.85 us
    pallas_call x1, Pallas kernels, fast_plan(): call(functools.partial(late_kernel, half, half // 2), out_shape=(rights,...  0.82 us
  transfers between devices with their start and end apart: 6, of which 4 were waited for; matrix products, arithmetic and copies ran while one was open for 0% of the time, Pallas kernels for 18%

profile of v3, /device:TPU:1, one launch (start us, length us, event | category | flops | bytes accessed | tf_op | source)
XLA Modules:
  0.0 20.4 jit_solution(15958169399276471900)
XLA Ops:
  0.0 2.1 %collective-permute-start.2 = (bf16[10,40,128]{2,1,0:T(8,128)(2,1)}, bf16[10,40,128]{2,1,0:T(8,128)(2,1)S(1)}, u32[]{:S(2)}, u32[]{:S(2)}) collective-permute-start(bf16[10,40,128]{2,1,0:T(8,128)(2,1)} %x_ref.1), channel_id=1, source_target_pairs={{0,2},{2,0},{4,6},{6,4},{8,10},{10,8},{12,14},{14,12},{1,3},{3,1},... | collective-permute-start | bytes 307208 | tf_op jit(solution)/shard_map/ppermute | solution.py:149
  2.1 1.2 %collective-permute-start.1 = (bf16[10,40,128]{2,1,0:T(8,128)(2,1)}, bf16[10,40,128]{2,1,0:T(8,128)(2,1)S(1)}, u32[]{:S(2)}, u32[]{:S(2)}) collective-permute-start(bf16[10,40,128]{2,1,0:T(8,128)(2,1)} %x_ref.1), channel_id=1, source_target_pairs={{0,6},{2,4},{4,2},{6,0},{8,14},{10,12},{12,10},{14,8},{1,7},{3,5},... | collective-permute-start | bytes 307208 | tf_op jit(solution)/shard_map/ppermute | solution.py:149
  3.3 2.3 %collective-permute-start = (bf16[10,40,128]{2,1,0:T(8,128)(2,1)}, bf16[10,40,128]{2,1,0:T(8,128)(2,1)S(1)}, u32[]{:S(2)}, u32[]{:S(2)}) collective-permute-start(bf16[10,40,128]{2,1,0:T(8,128)(2,1)} %x_ref.1), channel_id=1, source_target_pairs={{0,8},{2,10},{4,12},{6,14},{8,0},{10,2},{12,4},{14,6},{1,9},{3,11}... | collective-permute-start | bytes 307208 | tf_op jit(solution)/shard_map/ppermute | solution.py:149
  5.6 0.2 collective-permute-start.3
  5.8 1.6 %shard_map.46 = (f32[800,128]{1,0:T(8,128)S(1)}, f32[1600,128]{1,0:T(8,128)S(1)}, f32[400,128]{1,0:T(8,128)S(1)}, bf16[128,512]{1,0:T(8,128)(2,1)S(1)}, bf16[128...) custom-call(bf16[10,40,128]{2,1,0:T(8,128)(2,1)} %x_ref.1, bf16[128,512]{1,0:T(8,128)(2,1)} %w_ref.1, ...), custom_call_target="tpu_custom_call" | custom-call | tf_op jit(solution)/shard_map/pallas_call | solution.py:156
  7.4 0.0 collective-permute-done.2.x_ref
  7.4 0.7 %shard_map.47 = (f32[1600,128]{1,0:T(8,128)S(1)}, f32[10,16,128]{2,1,0:T(8,128)S(1)}) custom-call(bf16[10,40,128]{2,1,0:T(8,128)(2,1)S(1)} %collective-permute-done.2.x_ref, bf16[128,512]{1,0:T(8,128)(2,1)S(1)} %get-tuple-element.16.w_ref, f32[800,128]{1,0:T(8,128)S(1)} %get-tuple-element.17.left_ref._, ...), custom_call_target="tpu_custom_call", output_to_operand_aliasing={{0}: (3, {})} | custom-call | tf_op jit(solution)/shard_map/pallas_call | solution.py:180
  8.1 0.0 collective-permute-done.1.x_ref
  8.1 0.4 %shard_map.48.right_ref._ = f32[1600,128]{1,0:T(8,128)S(1)} custom-call(bf16[10,40,128]{2,1,0:T(8,128)(2,1)S(1)} %collective-permute-done.1.x_ref, bf16[128,512]{1,0:T(8,128)(2,1)S(1)} %get-tuple-element.16.w_ref, f32[1600,128]{1,0:T(8,128)S(1)} %get-tuple-element.19._), custom_call_target="tpu_custom_call", output_to_operand_aliasing={{}: (2, {})} | custom-call | tf_op jit(solution)/shard_map/pallas_call | solution.py:166
  8.5 0.3 %collective-permute-done.far_ref = bf16[10,40,128]{2,1,0:T(8,128)(2,1)S(1)} collective-permute-done((bf16[10,40,128]{2,1,0:T(8,128)(2,1)}, bf16[10,40,128]{2,1,0:T(8,128)(2,1)S(1)}, u32[]{:S(2)}, u32[]{:S(2)}) %collective-permute-start) | collective-permute-done | bytes 102432 | tf_op jit(solution)/shard_map/ppermute | solution.py:149
  8.8 0.7 %shard_map.49 = (f32[800,128]{1,0:T(8,128)S(1)}, f32[10,16,128]{2,1,0:T(8,128)S(1)}) custom-call(bf16[10,40,128]{2,1,0:T(8,128)(2,1)S(1)} %collective-permute-done.far_ref, bf16[128,512]{1,0:T(8,128)(2,1)S(1)} %get-tuple-element.16.w_ref, f32[1600,128]{1,0:T(8,128)S(1)} %shard_map.48.right_ref._, ...), custom_call_target="tpu_custom_call", output_to_operand_aliasing={{0}: (3, {})} | custom-call | tf_op jit(solution)/shard_map/pallas_call | solution.py:170
  9.5 1.6 %collective-permute-done.3.x_ref = bf16[10,40,128]{2,1,0:T(8,128)(2,1)S(1)} collective-permute-done((bf16[10,40,128]{2,1,0:T(8,128)(2,1)}, bf16[10,40,128]{2,1,0:T(8,128)(2,1)S(1)}, u32[]{:S(2)}, u32[]{:S(2)}) %collective-permute-start.3) | collective-permute-done | bytes 102432 | tf_op jit(solution)/shard_map/ppermute | solution.py:149
  11.0 0.8 %shard_map.50 = (f32[1600,128]{1,0:T(8,128)S(1)}, f32[10,40,128]{2,1,0:T(8,128)S(1)}) custom-call(bf16[10,40,128]{2,1,0:T(8,128)(2,1)S(1)} %collective-permute-done.3.x_ref, bf16[128,512]{1,0:T(8,128)(2,1)S(1)} %get-tuple-element.16.w_ref, f32[800,128]{1,0:T(8,128)S(1)} %get-tuple-element.20.left_ref, ...), custom_call_target="tpu_custom_call", output_to_operand_aliasing={{0}: (5, {})} | custom-call | tf_op jit(solution)/shard_map/pallas_call | solution.py:188
  11.9 1.3 %collective-permute-start.4 = (f32[10,40,128]{2,1,0:T(8,128)S(1)}, f32[10,40,128]{2,1,0:T(8,128)S(1)}, u32[]{:S(2)}, u32[]{:S(2)}) collective-permute-start(f32[10,40,128]{2,1,0:T(8,128)S(1)} %get-tuple-element.24), channel_id=1, source_target_pairs={{0,1},{1,0},{2,3},{3,2},{4,5},{5,4},{6,7},{7,6},{8,9},{9,8},{10,11... | collective-permute-start | bytes 614408 | tf_op jit(solution)/shard_map/ppermute | solution.py:192
  13.2 0.5 %shard_map.51.keep_ref = f32[10,40,128]{2,1,0:T(8,128)S(1)} custom-call(f32[800,128]{1,0:T(8,128)S(1)} %get-tuple-element.20.left_ref, f32[1600,128]{1,0:T(8,128)S(1)} %get-tuple-element.23.right_ref, f32[10,16,128]{2,1,0:T(8,128)S(1)} %get-tuple-element.21.own_ref, f32[10,16,128]{2,1,0:T(8,128)S(1)} %get-tuple-element.22.far_ref), custom_call_target="tpu_custom_call" | custom-call | tf_op jit(solution)/shard_map/pallas_call | solution.py:193
  13.7 0.6 %collective-permute-done.4.got_ref = f32[10,40,128]{2,1,0:T(8,128)S(1)} collective-permute-done((f32[10,40,128]{2,1,0:T(8,128)S(1)}, f32[10,40,128]{2,1,0:T(8,128)S(1)}, u32[]{:S(2)}, u32[]{:S(2)}) %collective-permute-start.4) | collective-permute-done | bytes 204832 | tf_op jit(solution)/shard_map/ppermute | solution.py:192
  14.3 0.2 %shard_map.52.tri_ref = bf16[10,40,128]{2,1,0:T(8,128)(2,1)S(1)} custom-call(f32[10,40,128]{2,1,0:T(8,128)S(1)} %shard_map.51.keep_ref, f32[10,40,128]{2,1,0:T(8,128)S(1)} %collective-permute-done.4.got_ref), custom_call_target="tpu_custom_call" | custom-call | tf_op jit(solution)/shard_map/pallas_call | solution.py:194
  14.5 2.2 %collective-permute-start.5 = (bf16[10,40,128]{2,1,0:T(8,128)(2,1)S(1)}, bf16[10,40,128]{2,1,0:T(8,128)(2,1)S(1)}, u32[]{:S(2)}, u32[]{:S(2)}) collective-permute-start(bf16[10,40,128]{2,1,0:T(8,128)(2,1)S(1)} %shard_map.52.tri_ref), channel_id=1, source_target_pairs={{1,8},{3,10},{5,12},{7,14},{8,1},{10,3},{12,5},{14,7},{0,2},{2,0},... | collective-permute-start | bytes 307208 | tf_op jit(solution)/shard_map/ppermute | solution.py:197
  16.7 2.8 %collective-permute-done.5.got_ref = bf16[10,40,128]{2,1,0:T(8,128)(2,1)S(1)} collective-permute-done((bf16[10,40,128]{2,1,0:T(8,128)(2,1)S(1)}, bf16[10,40,128]{2,1,0:T(8,128)(2,1)S(1)}, u32[]{:S(2)}, u32[]{:S(2)}) %collective-permute-start.5) | collective-permute-done | bytes 102432 | tf_op jit(solution)/shard_map/ppermute | solution.py:197
  19.6 0.9 %shard_map.53 = bf16[10,40,128]{2,1,0:T(8,128)(2,1)} custom-call(bf16[10,40,128]{2,1,0:T(8,128)(2,1)S(1)} %shard_map.52.tri_ref, bf16[10,40,128]{2,1,0:T(8,128)(2,1)S(1)} %collective-permute-done.5.got_ref, f32[400,128]{1,0:T(8,128)S(1)} %get-tuple-element.25.gate_ref, bf16[128,128]{1,0:T(8,128)(2,1)S(1)} %get-tuple-element.26.o_ref), custom_call_target="tpu_custom_call" | custom-call | tf_op jit(solution)/shard_map/pallas_call | solution.py:198
Async XLA Ops:
  0.0 7.4 %collective-permute-start.2 = (bf16[10,40,128]{2,1,0:T(8,128)(2,1)}, bf16[10,40,128]{2,1,0:T(8,128)(2,1)S(1)}, u32[]{:S(2)}, u32[]{:S(2)}) collective-permute-start(bf16[10,40,128]{2,1,0:T(8,128)(2,1)} %x_ref.1), channel_id=1, source_target_pairs={{0,2},{2,0},{4,6},{6,4},{8,10},{10,8},{12,14},{14,12},{1,3},{3,1},... | collective-permute-start | bytes 307208 | tf_op jit(solution)/shard_map/ppermute | solution.py:149
  2.1 6.0 %collective-permute-start.1 = (bf16[10,40,128]{2,1,0:T(8,128)(2,1)}, bf16[10,40,128]{2,1,0:T(8,128)(2,1)S(1)}, u32[]{:S(2)}, u32[]{:S(2)}) collective-permute-start(bf16[10,40,128]{2,1,0:T(8,128)(2,1)} %x_ref.1), channel_id=1, source_target_pairs={{0,6},{2,4},{4,2},{6,0},{8,14},{10,12},{12,10},{14,8},{1,7},{3,5},... | collective-permute-start | bytes 307208 | tf_op jit(solution)/shard_map/ppermute | solution.py:149
  3.3 5.5 %collective-permute-start = (bf16[10,40,128]{2,1,0:T(8,128)(2,1)}, bf16[10,40,128]{2,1,0:T(8,128)(2,1)S(1)}, u32[]{:S(2)}, u32[]{:S(2)}) collective-permute-start(bf16[10,40,128]{2,1,0:T(8,128)(2,1)} %x_ref.1), channel_id=1, source_target_pairs={{0,8},{2,10},{4,12},{6,14},{8,0},{10,2},{12,4},{14,6},{1,9},{3,11}... | collective-permute-start | bytes 307208 | tf_op jit(solution)/shard_map/ppermute | solution.py:149
  5.6 5.4 %collective-permute-start.3 = (bf16[10,40,128]{2,1,0:T(8,128)(2,1)}, bf16[10,40,128]{2,1,0:T(8,128)(2,1)S(1)}, u32[]{:S(2)}, u32[]{:S(2)}) collective-permute-start(bf16[10,40,128]{2,1,0:T(8,128)(2,1)} %x_ref.1), channel_id=1, source_target_pairs={{0,4},{2,6},{4,0},{6,2},{8,12},{10,14},{12,8},{14,10},{1,5},{3,7},... | collective-permute-start | bytes 307208 | tf_op jit(solution)/shard_map/ppermute | solution.py:149
  11.9 2.4 %collective-permute-start.4 = (f32[10,40,128]{2,1,0:T(8,128)S(1)}, f32[10,40,128]{2,1,0:T(8,128)S(1)}, u32[]{:S(2)}, u32[]{:S(2)}) collective-permute-start(f32[10,40,128]{2,1,0:T(8,128)S(1)} %get-tuple-element.24), channel_id=1, source_target_pairs={{0,1},{1,0},{2,3},{3,2},{4,5},{5,4},{6,7},{7,6},{8,9},{9,8},{10,11... | collective-permute-start | bytes 614408 | tf_op jit(solution)/shard_map/ppermute | solution.py:192
  14.5 5.0 %collective-permute-start.5 = (bf16[10,40,128]{2,1,0:T(8,128)(2,1)S(1)}, bf16[10,40,128]{2,1,0:T(8,128)(2,1)S(1)}, u32[]{:S(2)}, u32[]{:S(2)}) collective-permute-start(bf16[10,40,128]{2,1,0:T(8,128)(2,1)S(1)} %shard_map.52.tri_ref), channel_id=1, source_target_pairs={{1,8},{3,10},{5,12},{7,14},{8,1},{10,3},{12,5},{14,7},{0,2},{2,0},... | collective-permute-start | bytes 307208 | tf_op jit(solution)/shard_map/ppermute | solution.py:197

commit v4 on v3

--- a/solution.py
+++ b/solution.py
@@ -87,45 +87,57 @@
 
 
 def strips_of(half, rows_here):
-    part = half // 2 * rows_here
-    total = half * rows_here // 8
-    count = min(part // 8, total - -(-part // 8))
-    second = lax.div(place_of(half)[0], half // 2)
-    early = [second * (total - count) + n for n in range(count)]
-    late = [(1 - second) * count + n for n in range(total - count)]
-    return [[pl.multiple_of(s * 8, 8) for s in strips] for strips in (early, late)]
+    part, total = half // 2, half * rows_here // 8
+    count = min(part * rows_here // 8, total - -(-part * rows_here // 8))
+    place = place_of(half)[0]
+    second = lax.div(place, part)
+    bounds = [(p * rows_here // 8, -(-(p + 1) * rows_here // 8)) for p in range(half)]
+    held, others = max(b - a for a, b in bounds), total - count
+    start = (1 - second) * count
+    first = jnp.clip(lax.div((place ^ part) * rows_here, 8) - start, 0, others - held)
+    early = [second * others + n for n in range(count)]
+    middle = [start + jnp.where(n < first, n, n + held) for n in range(others - held)]
+    late = [start + first + n for n in range(held)]
+    return [[pl.multiple_of(s * 8, 8) for s in strips] for strips in (early, middle, late)]
 
 
 def right_kernel(half, step, x_ref, w_ref, _, right_ref):
     put_right(half, step, x_ref, w_ref, right_ref)
 
 
+def middle_kernel(half, step, x_ref, w_ref, left_ref, _, right_ref, own_ref):
+    put_right(half, step, x_ref, w_ref, right_ref)
+    _, middle, _ = strips_of(half, own_ref.shape[0])
+    products(left_ref, 0, right_ref, middle, range(0, own_ref.shape[1], 8), own_ref)
+
+
 def near_kernel(half, step, x_ref, w_ref, left_ref, _, right_ref, tile_ref):
     put_right(half, step, x_ref, w_ref, right_ref)
-    early, _ = strips_of(half, tile_ref.shape[0])
+    early, _, _ = strips_of(half, tile_ref.shape[0])
     products(left_ref, 0, right_ref, early, range(0, tile_ref.shape[1], 8), tile_ref)
 
 
 def far_kernel(half, far_ref, w_ref, right_ref, _, left_ref, tile_ref):
     rows, hidden = left_ref.shape[0] // 2, left_ref.shape[-1]
     left_ref[pl.ds(rows, rows), :] = side(normalised(far_ref), w_ref[:, : 2 * hidden])
-    early, _ = strips_of(half, tile_ref.shape[0])
-    products(left_ref, rows, right_ref, early, range(0, tile_ref.shape[1], 8), tile_ref)
-
-
-def whole_tile(half, given, left_ref, right_ref, own_ref, far_ref, out_ref):
+    early, middle, _ = strips_of(half, tile_ref.shape[0])
+    products(left_ref, rows, right_ref, early + middle, range(0, tile_ref.shape[1], 8), tile_ref)
+
+
+def whole_tile(half, given, left_ref, right_ref, own_ref, middle_ref, far_ref, out_ref):
     own = place_of(half)[1] != given
-    early, late = strips_of(half, out_ref.shape[0])
-    for n, s in enumerate(early):
-        here = slice(8 * n, 8 * n + 8)
-        out_ref[:, pl.ds(s, 8), :] = jnp.where(own, own_ref[:, here, :], far_ref[:, here, :])
+    early, middle, late = strips_of(half, out_ref.shape[0])
+    for strips, mine_ref, at in ((early, own_ref, 0), (middle, middle_ref, len(early))):
+        for n, s in enumerate(strips):
+            mine, far = mine_ref[:, 8 * n : 8 * n + 8, :], far_ref[:, 8 * (at + n) : 8 * (at + n) + 8, :]
+            out_ref[:, pl.ds(s, 8), :] = jnp.where(own, mine, far)
     base = pl.multiple_of(jnp.where(own, 0, left_ref.shape[0] // 2), 8)
     products(left_ref, base, right_ref, late, late, out_ref)
 
 
-def late_kernel(half, step, x_ref, w_ref, left_ref, own_ref, far_ref, _, right_ref, give_ref):
-    put_right(half, step, x_ref, w_ref, right_ref)
-    whole_tile(half, True, left_ref, right_ref, own_ref, far_ref, give_ref)
+def late_kernel(half, step, x_ref, w_ref, left_ref, own_ref, middle_ref, far_ref, _, right_ref, give_ref):
+    put_right(half, step, x_ref, w_ref, right_ref)
+    whole_tile(half, True, left_ref, right_ref, own_ref, middle_ref, far_ref, give_ref)
 
 
 def norm_kernel(keep_ref, got_ref, tri_ref):
@@ -165,32 +177,40 @@
         body = functools.partial(right_kernel, half, step)
         return call(body, out_shape=rights, input_output_aliases={2: 0})(*in_vmem(blocks[step]), w_v, *in_vmem(right))
 
-    def with_far(left, right):
-        return in_vmem(
-            *call(functools.partial(far_kernel, half), out_shape=(lefts, early_part), input_output_aliases={3: 0})(
-                *in_vmem(far), w_v, *in_vmem(right), left
-            )
-        )
-
     for step in range(half // 2 - 1, 1, -1):
         right = with_block(step, right)
-    early_part = pltpu.VMEM((rows_here, 8 * len(strips_of(half, rows_here)[0]), hidden), F32)
+    early, middle, _ = strips_of(half, rows_here)
+    early_part, middle_part, far_part = (
+        pltpu.VMEM((rows_here, 8 * len(strips), hidden), F32) for strips in (early, middle, early + middle)
+    )
     tile_part = pltpu.VMEM((rows_here, half * rows_here, hidden), F32)
     right, own_early = in_vmem(
         *call(functools.partial(near_kernel, half, 1), out_shape=(rights, early_part), input_output_aliases={3: 0})(
             *in_vmem(blocks[1]), w_v, left, *in_vmem(right)
         )
     )
-    for step in range(half - 1, half // 2, -1):
+    for step in range(half - 1, half // 2 + 1, -1):
         right = with_block(step, right)
-    left, far_early = with_far(left, right)
+    step = half // 2 + 1
+    right, own_middle = in_vmem(
+        *call(
+            functools.partial(middle_kernel, half, step), out_shape=(rights, middle_part), input_output_aliases={3: 0}
+        )(*in_vmem(blocks[step]), w_v, left, *in_vmem(right))
+    )
+    left, far_sums = in_vmem(
+        *call(functools.partial(far_kernel, half), out_shape=(lefts, far_part), input_output_aliases={3: 0})(
+            *in_vmem(far), w_v, right, left
+        )
+    )
     right, give = in_vmem(
         *call(
-            functools.partial(late_kernel, half, half // 2), out_shape=(rights, tile_part), input_output_aliases={5: 0}
-        )(*in_vmem(blocks[half // 2]), w_v, left, own_early, far_early, *in_vmem(right))
+            functools.partial(late_kernel, half, half // 2), out_shape=(rights, tile_part), input_output_aliases={6: 0}
+        )(*in_vmem(blocks[half // 2]), w_v, left, own_early, own_middle, far_sums, *in_vmem(right))
     )
     got = lax.ppermute(give, "col", [(0, 1), (1, 0)])
-    keep = call(functools.partial(whole_tile, half, False), out_shape=tile_part)(left, right, own_early, far_early)
+    keep = call(functools.partial(whole_tile, half, False), out_shape=tile_part)(
+        left, right, own_early, own_middle, far_sums
+    )
     tri = call(norm_kernel, out_shape=pltpu.VMEM(x.shape, BF16))(*in_vmem(keep, got))
     pairs = [(2 * r + 1 - r // half, 2 * (r ^ half) + r // half) for r in range(rows)]
     pairs += [(2 * r + r // half, 2 * (r ^ 1) + r // half) for r in range(rows)]

time: 20.6 us -> 20.4 us (level)
  the two profiles are of different devices: /device:TPU:1 before, /device:TPU:26 now
where the time goes in v4:
time: 20.4 us; the launch traced here: 20 us
  waiting for transfers between devices  10.3 us (50%)
  Pallas kernels  5.72 us (28%)
  starting transfers between devices  3.97 us (19%)
    ppermute x1, waiting for transfers between devices, fast_plan(): arrived = lax.ppermute(tri, ('row', 'col'), pairs)  4.97 us
    ppermute x4, waiting for transfers between devices, from_step(): return lax.ppermute(x, 'row', [(i, i ^ step) for i in range(rows)])  4.18 us
    ppermute x4, starting transfers between devices, from_step(): return lax.ppermute(x, 'row', [(i, i ^ step) for i in range(rows)])  3.82 us
    pallas_call x1, Pallas kernels, fast_plan(): call(functools.partial(own_kernel, half), in_specs=[pl.BlockSpec(memory_s...  1.61 us
    ppermute x1, waiting for transfers between devices, fast_plan(): got = lax.ppermute(give, 'col', [(0, 1), (1, 0)])  1.1 us
    pallas_call x1, Pallas kernels, fast_plan(): call(functools.partial(finish_kernel, half), in_specs=[pl.BlockSpec(memor...  0.85 us
    pallas_call x1, Pallas kernels, fast_plan(): call(functools.partial(far_kernel, half), out_shape=(lefts, far_part), in...  0.82 us
    pallas_call x1, Pallas kernels, fast_plan(): call(functools.partial(late_kernel, half, half // 2), out_shape=(rights,...  0.68 us
  transfers between devices with their start and end apart: 6, of which 3 were waited for; matrix products, arithmetic and copies ran while one was open for 0% of the time, Pallas kernels for 20%

profile of v4, /device:TPU:26, one launch (start us, length us, event | category | flops | bytes accessed | tf_op | source)
XLA Modules:
  0.0 20.0 jit_solution(12345032507629416138)
XLA Ops:
  0.0 1.5 %collective-permute-start.2 = (bf16[10,40,128]{2,1,0:T(8,128)(2,1)}, bf16[10,40,128]{2,1,0:T(8,128)(2,1)S(1)}, u32[]{:S(2)}, u32[]{:S(2)}) collective-permute-start(bf16[10,40,128]{2,1,0:T(8,128)(2,1)} %x_ref.1), channel_id=1, source_target_pairs={{0,2},{2,0},{4,6},{6,4},{8,10},{10,8},{12,14},{14,12},{1,3},{3,1},... | collective-permute-start | bytes 307208 | tf_op jit(solution)/shard_map/ppermute | solution.py:161
  1.5 0.4 %collective-permute-start.1 = (bf16[10,40,128]{2,1,0:T(8,128)(2,1)}, bf16[10,40,128]{2,1,0:T(8,128)(2,1)S(1)}, u32[]{:S(2)}, u32[]{:S(2)}) collective-permute-start(bf16[10,40,128]{2,1,0:T(8,128)(2,1)} %x_ref.1), channel_id=1, source_target_pairs={{0,6},{2,4},{4,2},{6,0},{8,14},{10,12},{12,10},{14,8},{1,7},{3,5},... | collective-permute-start | bytes 307208 | tf_op jit(solution)/shard_map/ppermute | solution.py:161
  1.9 0.3 %collective-permute-start = (bf16[10,40,128]{2,1,0:T(8,128)(2,1)}, bf16[10,40,128]{2,1,0:T(8,128)(2,1)S(1)}, u32[]{:S(2)}, u32[]{:S(2)}) collective-permute-start(bf16[10,40,128]{2,1,0:T(8,128)(2,1)} %x_ref.1), channel_id=1, source_target_pairs={{0,8},{2,10},{4,12},{6,14},{8,0},{10,2},{12,4},{14,6},{1,9},{3,11}... | collective-permute-start | bytes 307208 | tf_op jit(solution)/shard_map/ppermute | solution.py:161
  2.2 1.6 %collective-permute-start.3 = (bf16[10,40,128]{2,1,0:T(8,128)(2,1)}, bf16[10,40,128]{2,1,0:T(8,128)(2,1)S(1)}, u32[]{:S(2)}, u32[]{:S(2)}) collective-permute-start(bf16[10,40,128]{2,1,0:T(8,128)(2,1)} %x_ref.1), channel_id=1, source_target_pairs={{0,4},{2,6},{4,0},{6,2},{8,12},{10,14},{12,8},{14,10},{1,5},{3,7},... | collective-permute-start | bytes 307208 | tf_op jit(solution)/shard_map/ppermute | solution.py:161
  3.8 1.6 %shard_map.46 = (f32[800,128]{1,0:T(8,128)S(1)}, f32[1600,128]{1,0:T(8,128)S(1)}, f32[400,128]{1,0:T(8,128)S(1)}, bf16[128,512]{1,0:T(8,128)(2,1)S(1)}, bf16[128...) custom-call(bf16[10,40,128]{2,1,0:T(8,128)(2,1)} %x_ref.1, bf16[128,512]{1,0:T(8,128)(2,1)} %w_ref.1, ...), custom_call_target="tpu_custom_call" | custom-call | tf_op jit(solution)/shard_map/pallas_call | solution.py:168
  5.4 0.0 collective-permute-done.2.x_ref
  5.5 0.7 %shard_map.47 = (f32[1600,128]{1,0:T(8,128)S(1)}, f32[10,16,128]{2,1,0:T(8,128)S(1)}) custom-call(bf16[10,40,128]{2,1,0:T(8,128)(2,1)S(1)} %collective-permute-done.2.x_ref, bf16[128,512]{1,0:T(8,128)(2,1)S(1)} %get-tuple-element.18.w_ref, f32[800,128]{1,0:T(8,128)S(1)} %get-tuple-element.19.left_ref._, ...), custom_call_target="tpu_custom_call", output_to_operand_aliasing={{0}: (3, {})} | custom-call | tf_op jit(solution)/shard_map/pallas_call | solution.py:188
  6.1 4.2 %collective-permute-done.1.x_ref = bf16[10,40,128]{2,1,0:T(8,128)(2,1)S(1)} collective-permute-done((bf16[10,40,128]{2,1,0:T(8,128)(2,1)}, bf16[10,40,128]{2,1,0:T(8,128)(2,1)S(1)}, u32[]{:S(2)}, u32[]{:S(2)}) %collective-permute-start.1) | collective-permute-done | bytes 102432 | tf_op jit(solution)/shard_map/ppermute | solution.py:161
  10.3 0.5 %shard_map.48 = (f32[1600,128]{1,0:T(8,128)S(1)}, f32[10,8,128]{2,1,0:T(8,128)S(1)}) custom-call(bf16[10,40,128]{2,1,0:T(8,128)(2,1)S(1)} %collective-permute-done.1.x_ref, bf16[128,512]{1,0:T(8,128)(2,1)S(1)} %get-tuple-element.18.w_ref, f32[800,128]{1,0:T(8,128)S(1)} %get-tuple-element.19.left_ref._, ...), custom_call_target="tpu_custom_call", output_to_operand_aliasing={{0}: (3, {})} | custom-call | tf_op jit(solution)/shard_map/pallas_call | solution.py:196
  10.9 0.0 collective-permute-done.far_ref
  10.9 0.8 %shard_map.49 = (f32[800,128]{1,0:T(8,128)S(1)}, f32[10,24,128]{2,1,0:T(8,128)S(1)}) custom-call(bf16[10,40,128]{2,1,0:T(8,128)(2,1)S(1)} %collective-permute-done.far_ref, bf16[128,512]{1,0:T(8,128)(2,1)S(1)} %get-tuple-element.18.w_ref, f32[1600,128]{1,0:T(8,128)S(1)} %get-tuple-element.22.right_ref._, ...), custom_call_target="tpu_custom_call", output_to_operand_aliasing={{0}: (3, {})} | custom-call | tf_op jit(solution)/shard_map/pallas_call | solution.py:201
  11.7 0.0 collective-permute-done.3.x_ref
  11.7 0.7 %shard_map.50 = (f32[1600,128]{1,0:T(8,128)S(1)}, f32[10,40,128]{2,1,0:T(8,128)S(1)}) custom-call(bf16[10,40,128]{2,1,0:T(8,128)(2,1)S(1)} %collective-permute-done.3.x_ref, bf16[128,512]{1,0:T(8,128)(2,1)S(1)} %get-tuple-element.18.w_ref, f32[800,128]{1,0:T(8,128)S(1)} %get-tuple-element.23.left_ref, ...), custom_call_target="tpu_custom_call", output_to_operand_aliasing={{0}: (6, {})} | custom-call | tf_op jit(solution)/shard_map/pallas_call | solution.py:206
  12.4 0.1 collective-permute-start.4
  12.5 0.3 %shard_map.51.keep_ref = f32[10,40,128]{2,1,0:T(8,128)S(1)} custom-call(f32[800,128]{1,0:T(8,128)S(1)} %get-tuple-element.23.left_ref, f32[1600,128]{1,0:T(8,128)S(1)} %get-tuple-element.27.right_ref, f32[10,16,128]{2,1,0:T(8,128)S(1)} %get-tuple-element.24.own_ref, f32[10,8,128]{2,1,0:T(8,128)S(1)} %get-tuple-element.25.middle_ref, ...), custom_call_target="tpu_custom_call" | custom-call | tf_op jit(solution)/shard_map/pallas_call | solution.py:211
  12.8 1.1 %collective-permute-done.4.got_ref = f32[10,40,128]{2,1,0:T(8,128)S(1)} collective-permute-done((f32[10,40,128]{2,1,0:T(8,128)S(1)}, f32[10,40,128]{2,1,0:T(8,128)S(1)}, u32[]{:S(2)}, u32[]{:S(2)}) %collective-permute-start.4) | collective-permute-done | bytes 204832 | tf_op jit(solution)/shard_map/ppermute | solution.py:210
  13.9 0.2 %shard_map.52.tri_ref = bf16[10,40,128]{2,1,0:T(8,128)(2,1)S(1)} custom-call(f32[10,40,128]{2,1,0:T(8,128)S(1)} %shard_map.51.keep_ref, f32[10,40,128]{2,1,0:T(8,128)S(1)} %collective-permute-done.4.got_ref), custom_call_target="tpu_custom_call" | custom-call | tf_op jit(solution)/shard_map/pallas_call | solution.py:214
  14.1 0.1 collective-permute-start.5
  14.2 5.0 %collective-permute-done.5.got_ref = bf16[10,40,128]{2,1,0:T(8,128)(2,1)S(1)} collective-permute-done((bf16[10,40,128]{2,1,0:T(8,128)(2,1)S(1)}, bf16[10,40,128]{2,1,0:T(8,128)(2,1)S(1)}, u32[]{:S(2)}, u32[]{:S(2)}) %collective-permute-start.5) | collective-permute-done | bytes 102432 | tf_op jit(solution)/shard_map/ppermute | solution.py:217
  19.2 0.9 %shard_map.53 = bf16[10,40,128]{2,1,0:T(8,128)(2,1)} custom-call(bf16[10,40,128]{2,1,0:T(8,128)(2,1)S(1)} %shard_map.52.tri_ref, bf16[10,40,128]{2,1,0:T(8,128)(2,1)S(1)} %collective-permute-done.5.got_ref, f32[400,128]{1,0:T(8,128)S(1)} %get-tuple-element.29.gate_ref, bf16[128,128]{1,0:T(8,128)(2,1)S(1)} %get-tuple-element.30.o_ref), custom_call_target="tpu_custom_call" | custom-call | tf_op jit(solution)/shard_map/pallas_call | solution.py:218
Async XLA Ops:
  0.0 5.4 %collective-permute-start.2 = (bf16[10,40,128]{2,1,0:T(8,128)(2,1)}, bf16[10,40,128]{2,1,0:T(8,128)(2,1)S(1)}, u32[]{:S(2)}, u32[]{:S(2)}) collective-permute-start(bf16[10,40,128]{2,1,0:T(8,128)(2,1)} %x_ref.1), channel_id=1, source_target_pairs={{0,2},{2,0},{4,6},{6,4},{8,10},{10,8},{12,14},{14,12},{1,3},{3,1},... | collective-permute-start | bytes 307208 | tf_op jit(solution)/shard_map/ppermute | solution.py:161
  1.5 8.8 %collective-permute-start.1 = (bf16[10,40,128]{2,1,0:T(8,128)(2,1)}, bf16[10,40,128]{2,1,0:T(8,128)(2,1)S(1)}, u32[]{:S(2)}, u32[]{:S(2)}) collective-permute-start(bf16[10,40,128]{2,1,0:T(8,128)(2,1)} %x_ref.1), channel_id=1, source_target_pairs={{0,6},{2,4},{4,2},{6,0},{8,14},{10,12},{12,10},{14,8},{1,7},{3,5},... | collective-permute-start | bytes 307208 | tf_op jit(solution)/shard_map/ppermute | solution.py:161
  1.9 8.9 %collective-permute-start = (bf16[10,40,128]{2,1,0:T(8,128)(2,1)}, bf16[10,40,128]{2,1,0:T(8,128)(2,1)S(1)}, u32[]{:S(2)}, u32[]{:S(2)}) collective-permute-start(bf16[10,40,128]{2,1,0:T(8,128)(2,1)} %x_ref.1), channel_id=1, source_target_pairs={{0,8},{2,10},{4,12},{6,14},{8,0},{10,2},{12,4},{14,6},{1,9},{3,11}... | collective-permute-start | bytes 307208 | tf_op jit(solution)/shard_map/ppermute | solution.py:161
  2.2 9.4 %collective-permute-start.3 = (bf16[10,40,128]{2,1,0:T(8,128)(2,1)}, bf16[10,40,128]{2,1,0:T(8,128)(2,1)S(1)}, u32[]{:S(2)}, u32[]{:S(2)}) collective-permute-start(bf16[10,40,128]{2,1,0:T(8,128)(2,1)} %x_ref.1), channel_id=1, source_target_pairs={{0,4},{2,6},{4,0},{6,2},{8,12},{10,14},{12,8},{14,10},{1,5},{3,7},... | collective-permute-start | bytes 307208 | tf_op jit(solution)/shard_map/ppermute | solution.py:161
  12.4 1.5 %collective-permute-start.4 = (f32[10,40,128]{2,1,0:T(8,128)S(1)}, f32[10,40,128]{2,1,0:T(8,128)S(1)}, u32[]{:S(2)}, u32[]{:S(2)}) collective-permute-start(f32[10,40,128]{2,1,0:T(8,128)S(1)} %get-tuple-element.28), channel_id=1, source_target_pairs={{0,1},{1,0},{2,3},{3,2},{4,5},{5,4},{6,7},{7,6},{8,9},{9,8},{10,11... | collective-permute-start | bytes 614408 | tf_op jit(solution)/shard_map/ppermute | solution.py:210
  14.1 5.0 %collective-permute-start.5 = (bf16[10,40,128]{2,1,0:T(8,128)(2,1)S(1)}, bf16[10,40,128]{2,1,0:T(8,128)(2,1)S(1)}, u32[]{:S(2)}, u32[]{:S(2)}) collective-permute-start(bf16[10,40,128]{2,1,0:T(8,128)(2,1)S(1)} %shard_map.52.tri_ref), channel_id=1, source_target_pairs={{1,8},{3,10},{5,12},{7,14},{8,1},{10,3},{12,5},{14,7},{0,2},{2,0},... | collective-permute-start | bytes 307208 | tf_op jit(solution)/shard_map/ppermute | solution.py:217

commit v5 on v4

--- a/solution.py
+++ b/solution.py
@@ -108,7 +108,10 @@
 def middle_kernel(half, step, x_ref, w_ref, left_ref, _, right_ref, own_ref):
     put_right(half, step, x_ref, w_ref, right_ref)
     _, middle, _ = strips_of(half, own_ref.shape[0])
-    products(left_ref, 0, right_ref, middle, range(0, own_ref.shape[1], 8), own_ref)
+
+    @pl.when(jnp.logical_not(place_of(half)[1]))
+    def _():
+        products(left_ref, 0, right_ref, middle, range(0, own_ref.shape[1], 8), own_ref)
 
 
 def near_kernel(half, step, x_ref, w_ref, left_ref, _, right_ref, tile_ref):
@@ -121,33 +124,54 @@
     rows, hidden = left_ref.shape[0] // 2, left_ref.shape[-1]
     left_ref[pl.ds(rows, rows), :] = side(normalised(far_ref), w_ref[:, : 2 * hidden])
     early, middle, _ = strips_of(half, tile_ref.shape[0])
-    products(left_ref, rows, right_ref, early + middle, range(0, tile_ref.shape[1], 8), tile_ref)
-
-
-def whole_tile(half, given, left_ref, right_ref, own_ref, middle_ref, far_ref, out_ref):
-    own = place_of(half)[1] != given
-    early, middle, late = strips_of(half, out_ref.shape[0])
+
+    @pl.when(place_of(half)[1])
+    def _():
+        products(left_ref, rows, right_ref, early + middle, range(0, tile_ref.shape[1], 8), tile_ref)
+
+
+def late_kernel(half, step, x_ref, w_ref, left_ref, own_ref, middle_ref, far_ref, _, right_ref, give_ref):
+    put_right(half, step, x_ref, w_ref, right_ref)
+    ours = place_of(half)[1]
+    early, middle, late = strips_of(half, give_ref.shape[0])
     for strips, mine_ref, at in ((early, own_ref, 0), (middle, middle_ref, len(early))):
         for n, s in enumerate(strips):
             mine, far = mine_ref[:, 8 * n : 8 * n + 8, :], far_ref[:, 8 * (at + n) : 8 * (at + n) + 8, :]
-            out_ref[:, pl.ds(s, 8), :] = jnp.where(own, mine, far)
-    base = pl.multiple_of(jnp.where(own, 0, left_ref.shape[0] // 2), 8)
-    products(left_ref, base, right_ref, late, late, out_ref)
-
-
-def late_kernel(half, step, x_ref, w_ref, left_ref, own_ref, middle_ref, far_ref, _, right_ref, give_ref):
-    put_right(half, step, x_ref, w_ref, right_ref)
-    whole_tile(half, True, left_ref, right_ref, own_ref, middle_ref, far_ref, give_ref)
+            give_ref[:, pl.ds(s, 8), :] = jnp.where(ours, far, mine)
+    base = pl.multiple_of(jnp.where(ours, left_ref.shape[0] // 2, 0), 8)
+    products(left_ref, base, right_ref, late, late, give_ref)
+
+
+def keep_kernel(half, left_ref, right_ref, own_ref, keep_ref):
+    ours = place_of(half)[1]
+    early, middle, late = strips_of(half, keep_ref.shape[0])
+
+    @pl.when(ours)
+    def _():
+        for n, s in enumerate(early):
+            keep_ref[:, pl.ds(s, 8), :] = own_ref[:, 8 * n : 8 * n + 8, :]
+        products(left_ref, 0, right_ref, middle + late, middle + late, keep_ref)
+
+    @pl.when(jnp.logical_not(ours))
+    def _():
+        strips = early + middle + late
+        products(left_ref, left_ref.shape[0] // 2, right_ref, strips, strips, keep_ref)
 
 
 def norm_kernel(keep_ref, got_ref, tri_ref):
     tri_ref[...] = layer_norm(keep_ref[...] + got_ref[...]).astype(BF16)
 
 
-def finish_kernel(half, tri_ref, got_ref, gate_ref, o_ref, out_ref):
-    tri = jnp.where(place_of(half)[1], tri_ref[...].astype(F32), got_ref[...].astype(F32)).astype(BF16)
-    update = jnp.dot(tri.reshape(gate_ref.shape), o_ref[...], preferred_element_type=F32)
-    out_ref[...] = (update * gate_ref[...]).astype(BF16).reshape(out_ref.shape)
+def finish_kernel(half, kept, tri_ref, gate_ref, o_ref, *refs):
+    out_ref, done_ref, sem = refs[-3:]
+
+    @pl.when(place_of(half)[1] == kept)
+    def _():
+        update = jnp.dot(tri_ref[...].reshape(gate_ref.shape), o_ref[...], preferred_element_type=F32)
+        done_ref[...] = (update * gate_ref[...]).astype(BF16).reshape(done_ref.shape)
+        copy = pltpu.make_async_copy(done_ref, out_ref, sem)
+        copy.start()
+        copy.wait()
 
 
 def fast_plan(mesh, x, proj_weight, gate_weight, out_weight):
@@ -208,19 +232,29 @@
         )(*in_vmem(blocks[half // 2]), w_v, left, own_early, own_middle, far_sums, *in_vmem(right))
     )
     got = lax.ppermute(give, "col", [(0, 1), (1, 0)])
-    keep = call(functools.partial(whole_tile, half, False), out_shape=tile_part)(
-        left, right, own_early, own_middle, far_sums
-    )
-    tri = call(norm_kernel, out_shape=pltpu.VMEM(x.shape, BF16))(*in_vmem(keep, got))
+    keep = call(functools.partial(keep_kernel, half), out_shape=tile_part)(left, right, own_early)
+    (tri,) = in_vmem(call(norm_kernel, out_shape=pltpu.VMEM(x.shape, BF16))(*in_vmem(keep, got)))
     pairs = [(2 * r + 1 - r // half, 2 * (r ^ half) + r // half) for r in range(rows)]
     pairs += [(2 * r + r // half, 2 * (r ^ 1) + r // half) for r in range(rows)]
     arrived = lax.ppermute(tri, ("row", "col"), pairs)
+    in_place = pl.BlockSpec(memory_space=pltpu.VMEM)
+    in_hbm = pl.BlockSpec(memory_space=pltpu.HBM)
+    scratch = [pltpu.VMEM(x.shape, BF16), pltpu.SemaphoreType.DMA]
+    out = call(
+        functools.partial(finish_kernel, half, True),
+        in_specs=[in_place] * 3,
+        out_specs=in_hbm,
+        out_shape=pltpu.HBM(x.shape, BF16),
+        scratch_shapes=scratch,
+    )(tri, gate, o_v)
     return call(
-        functools.partial(finish_kernel, half),
-        in_specs=[pl.BlockSpec(memory_space=pltpu.VMEM)] * 4,
-        out_specs=pl.BlockSpec(memory_space=pltpu.VMEM),
-        out_shape=jax.ShapeDtypeStruct(x.shape, BF16),
-    )(*in_vmem(tri, arrived), gate, o_v)
+        functools.partial(finish_kernel, half, False),
+        in_specs=[in_place] * 3 + [in_hbm],
+        out_specs=in_hbm,
+        out_shape=pltpu.HBM(x.shape, BF16),
+        input_output_aliases={3: 0},
+        scratch_shapes=scratch,
+    )(*in_vmem(arrived), gate, o_v, pltpu.with_memory_space_constraint(out, pltpu.HBM))
 
 
 def gather_plan(pair_rep, proj_weight, gate_weight, out_weight):

time: 20.4 us -> 20.4 us (level)
  the two profiles are of different devices: /device:TPU:26 before, /device:TPU:1 now
where the time goes in v5:
time: 20.4 us; the launch traced here: 20.3 us
  starting transfers between devices  9.36 us (46%)
  Pallas kernels  5.69 us (28%)
  waiting for transfers between devices  5.13 us (25%)
    ppermute x4, starting transfers between devices, from_step(): return lax.ppermute(x, 'row', [(i, i ^ step) for i in range(rows)])  5.79 us
    ppermute x1, waiting for transfers between devices, fast_plan(): arrived = lax.ppermute(tri, ('row', 'col'), pairs)  2.8 us
    ppermute x1, starting transfers between devices, fast_plan(): arrived = lax.ppermute(tri, ('row', 'col'), pairs)  2.23 us
    ppermute x4, waiting for transfers between devices, from_step(): return lax.ppermute(x, 'row', [(i, i ^ step) for i in range(rows)])  2.01 us
    pallas_call x1, Pallas kernels, fast_plan(): call(functools.partial(own_kernel, half), in_specs=[pl.BlockSpec(memory_s...  1.61 us
    ppermute x1, starting transfers between devices, fast_plan(): got = lax.ppermute(give, 'col', [(0, 1), (1, 0)])  1.35 us
    pallas_call x1, Pallas kernels, fast_plan(): call(functools.partial(finish_kernel, half, False), in_specs=[in_place] *...  0.85 us
    pallas_call x1, Pallas kernels, fast_plan(): call(functools.partial(keep_kernel, half), out_shape=tile_part)  0.76 us
  transfers between devices with their start and end apart: 6, of which 4 were waited for; matrix products, arithmetic and copies ran while one was open for 0% of the time, Pallas kernels for 19%

profile of v5, /device:TPU:1, one launch (start us, length us, event | category | flops | bytes accessed | tf_op | source)
XLA Modules:
  0.0 20.3 jit_solution(4084162788819330203)
XLA Ops:
  0.0 2.1 %collective-permute-start.2 = (bf16[10,40,128]{2,1,0:T(8,128)(2,1)}, bf16[10,40,128]{2,1,0:T(8,128)(2,1)S(1)}, u32[]{:S(2)}, u32[]{:S(2)}) collective-permute-start(bf16[10,40,128]{2,1,0:T(8,128)(2,1)} %x_ref.1), channel_id=1, source_target_pairs={{0,2},{2,0},{4,6},{6,4},{8,10},{10,8},{12,14},{14,12},{1,3},{3,1},... | collective-permute-start | bytes 307208 | tf_op jit(solution)/shard_map/ppermute | solution.py:185
  2.1 1.2 %collective-permute-start.1 = (bf16[10,40,128]{2,1,0:T(8,128)(2,1)}, bf16[10,40,128]{2,1,0:T(8,128)(2,1)S(1)}, u32[]{:S(2)}, u32[]{:S(2)}) collective-permute-start(bf16[10,40,128]{2,1,0:T(8,128)(2,1)} %x_ref.1), channel_id=1, source_target_pairs={{0,6},{2,4},{4,2},{6,0},{8,14},{10,12},{12,10},{14,8},{1,7},{3,5},... | collective-permute-start | bytes 307208 | tf_op jit(solution)/shard_map/ppermute | solution.py:185
  3.3 2.3 %collective-permute-start = (bf16[10,40,128]{2,1,0:T(8,128)(2,1)}, bf16[10,40,128]{2,1,0:T(8,128)(2,1)S(1)}, u32[]{:S(2)}, u32[]{:S(2)}) collective-permute-start(bf16[10,40,128]{2,1,0:T(8,128)(2,1)} %x_ref.1), channel_id=1, source_target_pairs={{0,8},{2,10},{4,12},{6,14},{8,0},{10,2},{12,4},{14,6},{1,9},{3,11}... | collective-permute-start | bytes 307208 | tf_op jit(solution)/shard_map/ppermute | solution.py:185
  5.6 0.2 collective-permute-start.3
  5.8 1.6 %shard_map.46 = (f32[800,128]{1,0:T(8,128)S(1)}, f32[1600,128]{1,0:T(8,128)S(1)}, f32[400,128]{1,0:T(8,128)S(1)}, bf16[128,512]{1,0:T(8,128)(2,1)S(1)}, bf16[128...) custom-call(bf16[10,40,128]{2,1,0:T(8,128)(2,1)} %x_ref.1, bf16[128,512]{1,0:T(8,128)(2,1)} %w_ref.1, ...), custom_call_target="tpu_custom_call" | custom-call | tf_op jit(solution)/shard_map/pallas_call | solution.py:192
  7.4 0.0 collective-permute-done.2.x_ref
  7.4 0.7 %shard_map.47 = (f32[1600,128]{1,0:T(8,128)S(1)}, f32[10,16,128]{2,1,0:T(8,128)S(1)}) custom-call(bf16[10,40,128]{2,1,0:T(8,128)(2,1)S(1)} %collective-permute-done.2.x_ref, bf16[128,512]{1,0:T(8,128)(2,1)S(1)} %get-tuple-element.18.w_ref, f32[800,128]{1,0:T(8,128)S(1)} %get-tuple-element.19.left_ref._, ...), custom_call_target="tpu_custom_call", output_to_operand_aliasing={{0}: (3, {})} | custom-call | tf_op jit(solution)/shard_map/pallas_call | solution.py:212
  8.1 0.0 collective-permute-done.1.x_ref
  8.1 0.5 %shard_map.48 = (f32[1600,128]{1,0:T(8,128)S(1)}, f32[10,8,128]{2,1,0:T(8,128)S(1)}) custom-call(bf16[10,40,128]{2,1,0:T(8,128)(2,1)S(1)} %collective-permute-done.1.x_ref, bf16[128,512]{1,0:T(8,128)(2,1)S(1)} %get-tuple-element.18.w_ref, f32[800,128]{1,0:T(8,128)S(1)} %get-tuple-element.19.left_ref._, ...), custom_call_target="tpu_custom_call", output_to_operand_aliasing={{0}: (3, {})} | custom-call | tf_op jit(solution)/shard_map/pallas_call | solution.py:220
  8.7 0.1 collective-permute-done.far_ref
  8.8 0.4 %shard_map.49 = (f32[800,128]{1,0:T(8,128)S(1)}, f32[10,24,128]{2,1,0:T(8,128)S(1)}) custom-call(bf16[10,40,128]{2,1,0:T(8,128)(2,1)S(1)} %collective-permute-done.far_ref, bf16[128,512]{1,0:T(8,128)(2,1)S(1)} %get-tuple-element.18.w_ref, f32[1600,128]{1,0:T(8,128)S(1)} %get-tuple-element.22.right_ref._, ...), custom_call_target="tpu_custom_call", output_to_operand_aliasing={{0}: (3, {})} | custom-call | tf_op jit(solution)/shard_map/pallas_call | solution.py:225
  9.2 1.9 %collective-permute-done.3.x_ref = bf16[10,40,128]{2,1,0:T(8,128)(2,1)S(1)} collective-permute-done((bf16[10,40,128]{2,1,0:T(8,128)(2,1)}, bf16[10,40,128]{2,1,0:T(8,128)(2,1)S(1)}, u32[]{:S(2)}, u32[]{:S(2)}) %collective-permute-start.3) | collective-permute-done | bytes 102432 | tf_op jit(solution)/shard_map/ppermute | solution.py:185
  11.0 0.7 %shard_map.50 = (f32[1600,128]{1,0:T(8,128)S(1)}, f32[10,40,128]{2,1,0:T(8,128)S(1)}) custom-call(bf16[10,40,128]{2,1,0:T(8,128)(2,1)S(1)} %collective-permute-done.3.x_ref, bf16[128,512]{1,0:T(8,128)(2,1)S(1)} %get-tuple-element.18.w_ref, f32[800,128]{1,0:T(8,128)S(1)} %get-tuple-element.23.left_ref, ...), custom_call_target="tpu_custom_call", output_to_operand_aliasing={{0}: (6, {})} | custom-call | tf_op jit(solution)/shard_map/pallas_call | solution.py:230
  11.7 1.3 %collective-permute-start.4 = (f32[10,40,128]{2,1,0:T(8,128)S(1)}, f32[10,40,128]{2,1,0:T(8,128)S(1)}, u32[]{:S(2)}, u32[]{:S(2)}) collective-permute-start(f32[10,40,128]{2,1,0:T(8,128)S(1)} %get-tuple-element.28), channel_id=1, source_target_pairs={{0,1},{1,0},{2,3},{3,2},{4,5},{5,4},{6,7},{7,6},{8,9},{9,8},{10,11... | collective-permute-start | bytes 614408 | tf_op jit(solution)/shard_map/ppermute | solution.py:234
  13.1 0.8 %shard_map.51.keep_ref = f32[10,40,128]{2,1,0:T(8,128)S(1)} custom-call(f32[800,128]{1,0:T(8,128)S(1)} %get-tuple-element.23.left_ref, f32[1600,128]{1,0:T(8,128)S(1)} %get-tuple-element.27.right_ref, f32[10,16,128]{2,1,0:T(8,128)S(1)} %get-tuple-element.24.own_ref), custom_call_target="tpu_custom_call" | custom-call | tf_op jit(solution)/shard_map/pallas_call | solution.py:235
  13.8 0.3 %collective-permute-done.4.got_ref = f32[10,40,128]{2,1,0:T(8,128)S(1)} collective-permute-done((f32[10,40,128]{2,1,0:T(8,128)S(1)}, f32[10,40,128]{2,1,0:T(8,128)S(1)}, u32[]{:S(2)}, u32[]{:S(2)}) %collective-permute-start.4) | collective-permute-done | bytes 204832 | tf_op jit(solution)/shard_map/ppermute | solution.py:234
  14.1 0.2 %shard_map.52.tri_ref = bf16[10,40,128]{2,1,0:T(8,128)(2,1)S(1)} custom-call(f32[10,40,128]{2,1,0:T(8,128)S(1)} %shard_map.51.keep_ref, f32[10,40,128]{2,1,0:T(8,128)S(1)} %collective-permute-done.4.got_ref), custom_call_target="tpu_custom_call" | custom-call | tf_op jit(solution)/shard_map/pallas_call | solution.py:236
  14.4 2.2 %collective-permute-start.5 = (bf16[10,40,128]{2,1,0:T(8,128)(2,1)S(1)}, bf16[10,40,128]{2,1,0:T(8,128)(2,1)S(1)}, u32[]{:S(2)}, u32[]{:S(2)}) collective-permute-start(bf16[10,40,128]{2,1,0:T(8,128)(2,1)S(1)} %shard_map.52.tri_ref), channel_id=1, source_target_pairs={{1,8},{3,10},{5,12},{7,14},{8,1},{10,3},{12,5},{14,7},{0,2},{2,0},... | collective-permute-start | bytes 307208 | tf_op jit(solution)/shard_map/ppermute | solution.py:239
  16.6 2.8 %collective-permute-done.5.tri_ref = bf16[10,40,128]{2,1,0:T(8,128)(2,1)S(1)} collective-permute-done((bf16[10,40,128]{2,1,0:T(8,128)(2,1)S(1)}, bf16[10,40,128]{2,1,0:T(8,128)(2,1)S(1)}, u32[]{:S(2)}, u32[]{:S(2)}) %collective-permute-start.5) | collective-permute-done | bytes 102432 | tf_op jit(solution)/shard_map/ppermute | solution.py:239
  19.4 0.8 %shard_map.54 = bf16[10,40,128]{2,1,0:T(8,128)(2,1)} custom-call(bf16[10,40,128]{2,1,0:T(8,128)(2,1)S(1)} %collective-permute-done.5.tri_ref, f32[400,128]{1,0:T(8,128)S(1)} %get-tuple-element.29.gate_ref, bf16[128,128]{1,0:T(8,128)(2,1)S(1)} %get-tuple-element.30.o_ref, bf16[10,40,128]{2,1,0:T(8,128)(2,1)} %shard_map.53.refs_0_), custom_call_target="tpu_custom_call", output_to_operand_aliasing={{}: (3, {})} | custom-call | tf_op jit(solution)/shard_map/pallas_call | solution.py:250
  (1 shorter events, 0.0 us)
Async XLA Ops:
  0.0 7.4 %collective-permute-start.2 = (bf16[10,40,128]{2,1,0:T(8,128)(2,1)}, bf16[10,40,128]{2,1,0:T(8,128)(2,1)S(1)}, u32[]{:S(2)}, u32[]{:S(2)}) collective-permute-start(bf16[10,40,128]{2,1,0:T(8,128)(2,1)} %x_ref.1), channel_id=1, source_target_pairs={{0,2},{2,0},{4,6},{6,4},{8,10},{10,8},{12,14},{14,12},{1,3},{3,1},... | collective-permute-start | bytes 307208 | tf_op jit(solution)/shard_map/ppermute | solution.py:185
  2.1 6.0 %collective-permute-start.1 = (bf16[10,40,128]{2,1,0:T(8,128)(2,1)}, bf16[10,40,128]{2,1,0:T(8,128)(2,1)S(1)}, u32[]{:S(2)}, u32[]{:S(2)}) collective-permute-start(bf16[10,40,128]{2,1,0:T(8,128)(2,1)} %x_ref.1), channel_id=1, source_target_pairs={{0,6},{2,4},{4,2},{6,0},{8,14},{10,12},{12,10},{14,8},{1,7},{3,5},... | collective-permute-start | bytes 307208 | tf_op jit(solution)/shard_map/ppermute | solution.py:185
  3.3 5.5 %collective-permute-start = (bf16[10,40,128]{2,1,0:T(8,128)(2,1)}, bf16[10,40,128]{2,1,0:T(8,128)(2,1)S(1)}, u32[]{:S(2)}, u32[]{:S(2)}) collective-permute-start(bf16[10,40,128]{2,1,0:T(8,128)(2,1)} %x_ref.1), channel_id=1, source_target_pairs={{0,8},{2,10},{4,12},{6,14},{8,0},{10,2},{12,4},{14,6},{1,9},{3,11}... | collective-permute-start | bytes 307208 | tf_op jit(solution)/shard_map/ppermute | solution.py:185
  5.6 5.4 %collective-permute-start.3 = (bf16[10,40,128]{2,1,0:T(8,128)(2,1)}, bf16[10,40,128]{2,1,0:T(8,128)(2,1)S(1)}, u32[]{:S(2)}, u32[]{:S(2)}) collective-permute-start(bf16[10,40,128]{2,1,0:T(8,128)(2,1)} %x_ref.1), channel_id=1, source_target_pairs={{0,4},{2,6},{4,0},{6,2},{8,12},{10,14},{12,8},{14,10},{1,5},{3,7},... | collective-permute-start | bytes 307208 | tf_op jit(solution)/shard_map/ppermute | solution.py:185
  11.7 2.4 %collective-permute-start.4 = (f32[10,40,128]{2,1,0:T(8,128)S(1)}, f32[10,40,128]{2,1,0:T(8,128)S(1)}, u32[]{:S(2)}, u32[]{:S(2)}) collective-permute-start(f32[10,40,128]{2,1,0:T(8,128)S(1)} %get-tuple-element.28), channel_id=1, source_target_pairs={{0,1},{1,0},{2,3},{3,2},{4,5},{5,4},{6,7},{7,6},{8,9},{9,8},{10,11... | collective-permute-start | bytes 614408 | tf_op jit(solution)/shard_map/ppermute | solution.py:234
  14.4 5.0 %collective-permute-start.5 = (bf16[10,40,128]{2,1,0:T(8,128)(2,1)S(1)}, bf16[10,40,128]{2,1,0:T(8,128)(2,1)S(1)}, u32[]{:S(2)}, u32[]{:S(2)}) collective-permute-start(bf16[10,40,128]{2,1,0:T(8,128)(2,1)S(1)} %shard_map.52.tri_ref), channel_id=1, source_target_pairs={{1,8},{3,10},{5,12},{7,14},{8,1},{10,3},{12,5},{14,7},{0,2},{2,0},... | collective-permute-start | bytes 307208 | tf_op jit(solution)/shard_map/ppermute | solution.py:239

commit v6 on v4

--- a/solution.py
+++ b/solution.py
@@ -11,6 +11,7 @@
 F32, BF16 = jnp.float32, jnp.bfloat16
 PLACED = P(("groups", "row"), "col", None)
 VMEM_BUDGET = 24 * 2**20
+PIECES = 3
 
 
 def layer_norm(values):
@@ -105,12 +106,6 @@
     put_right(half, step, x_ref, w_ref, right_ref)
 
 
-def middle_kernel(half, step, x_ref, w_ref, left_ref, _, right_ref, own_ref):
-    put_right(half, step, x_ref, w_ref, right_ref)
-    _, middle, _ = strips_of(half, own_ref.shape[0])
-    products(left_ref, 0, right_ref, middle, range(0, own_ref.shape[1], 8), own_ref)
-
-
 def near_kernel(half, step, x_ref, w_ref, left_ref, _, right_ref, tile_ref):
     put_right(half, step, x_ref, w_ref, right_ref)
     early, _, _ = strips_of(half, tile_ref.shape[0])
@@ -121,33 +116,70 @@
     rows, hidden = left_ref.shape[0] // 2, left_ref.shape[-1]
     left_ref[pl.ds(rows, rows), :] = side(normalised(far_ref), w_ref[:, : 2 * hidden])
     early, middle, _ = strips_of(half, tile_ref.shape[0])
-    products(left_ref, rows, right_ref, early + middle, range(0, tile_ref.shape[1], 8), tile_ref)
-
-
-def whole_tile(half, given, left_ref, right_ref, own_ref, middle_ref, far_ref, out_ref):
-    own = place_of(half)[1] != given
-    early, middle, late = strips_of(half, out_ref.shape[0])
-    for strips, mine_ref, at in ((early, own_ref, 0), (middle, middle_ref, len(early))):
-        for n, s in enumerate(strips):
-            mine, far = mine_ref[:, 8 * n : 8 * n + 8, :], far_ref[:, 8 * (at + n) : 8 * (at + n) + 8, :]
-            out_ref[:, pl.ds(s, 8), :] = jnp.where(own, mine, far)
-    base = pl.multiple_of(jnp.where(own, 0, left_ref.shape[0] // 2), 8)
-    products(left_ref, base, right_ref, late, late, out_ref)
-
-
-def late_kernel(half, step, x_ref, w_ref, left_ref, own_ref, middle_ref, far_ref, _, right_ref, give_ref):
-    put_right(half, step, x_ref, w_ref, right_ref)
-    whole_tile(half, True, left_ref, right_ref, own_ref, middle_ref, far_ref, give_ref)
-
-
-def norm_kernel(keep_ref, got_ref, tri_ref):
-    tri_ref[...] = layer_norm(keep_ref[...] + got_ref[...]).astype(BF16)
-
-
-def finish_kernel(half, tri_ref, got_ref, gate_ref, o_ref, out_ref):
-    tri = jnp.where(place_of(half)[1], tri_ref[...].astype(F32), got_ref[...].astype(F32)).astype(BF16)
+    products(left_ref, rows, right_ref, early + middle, early + middle, tile_ref)
+
+
+def give_kernel(half, step, x_ref, w_ref, left_ref, _r, _t, right_ref, tile_ref):
+    _, _, late = strips_of(half, tile_ref.shape[0])
+
+    @pl.when(lax.axis_index("col") == 1)
+    def _():
+        put_right(half, step, x_ref, w_ref, right_ref)
+        products(left_ref, left_ref.shape[0] // 2, right_ref, late, late, tile_ref)
+
+
+def keep_kernel(half, step, x_ref, w_ref, left_ref, own_ref, _, right_ref, last_ref, part_ref, *piece_refs):
+    early, middle, late = strips_of(half, part_ref.shape[0])
+
+    @pl.when(lax.axis_index("col") == 0)
+    def _():
+        put_right(half, step, x_ref, w_ref, right_ref)
+        products(left_ref, left_ref.shape[0] // 2, right_ref, late, range(0, last_ref.shape[1], 8), last_ref)
+
+    for n, s in enumerate(early):
+        part_ref[:, pl.ds(s, 8), :] = own_ref[:, 8 * n : 8 * n + 8, :]
+    products(left_ref, 0, right_ref, middle + late, middle + late, part_ref)
+    for ref, rows in zip(piece_refs, pieces_of(part_ref.shape[0]), strict=True):
+        ref[...] = part_ref[rows]
+
+
+def pieces_of(count):
+    ends = [count * n // PIECES for n in range(PIECES + 1)]
+    return [slice(a, b) for a, b in itertools.pairwise(ends)]
+
+
+def norm_kernel(half, tile_ref, last_ref, got_ref, *refs):
+    tri_ref, sum_ref = refs[PIECES], refs[-1]
+
+    @pl.when(lax.axis_index("col") == 0)
+    def _():
+        sum_ref[...] = tile_ref[...] + got_ref[...]
+        for n, s in enumerate(strips_of(half, tri_ref.shape[0])[2]):
+            sum_ref[:, pl.ds(s, 8), :] = last_ref[:, 8 * n : 8 * n + 8, :] + got_ref[:, pl.ds(s, 8), :]
+        tri_ref[...] = layer_norm(sum_ref[...]).astype(BF16)
+
+
+def write_update(tri, gate_ref, o_ref, out_ref, done_ref, sem):
     update = jnp.dot(tri.reshape(gate_ref.shape), o_ref[...], preferred_element_type=F32)
-    out_ref[...] = (update * gate_ref[...]).astype(BF16).reshape(out_ref.shape)
+    done_ref[...] = (update * gate_ref[...]).astype(BF16).reshape(done_ref.shape)
+    copy = pltpu.make_async_copy(done_ref, out_ref, sem)
+    copy.start()
+    copy.wait()
+
+
+def finish_own_kernel(half, keep_ref, *refs):
+    @pl.when(place_of(half)[1])
+    def _():
+        got_refs, (gate_ref, o_ref, out_ref, done_ref, sem) = refs[:PIECES], refs[PIECES:]
+        sums = jnp.concatenate([ref[...] for ref in got_refs], axis=0)
+        tri = layer_norm(keep_ref[...] + sums).astype(BF16)
+        write_update(tri, gate_ref, o_ref, out_ref, done_ref, sem)
+
+
+def finish_far_kernel(half, tri_ref, gate_ref, o_ref, _, out_ref, done_ref, sem):
+    @pl.when(jnp.logical_not(place_of(half)[1]))
+    def _():
+        write_update(tri_ref[...], gate_ref, o_ref, out_ref, done_ref, sem)
 
 
 def fast_plan(mesh, x, proj_weight, gate_weight, out_weight):
@@ -179,48 +211,67 @@
 
     for step in range(half // 2 - 1, 1, -1):
         right = with_block(step, right)
-    early, middle, _ = strips_of(half, rows_here)
-    early_part, middle_part, far_part = (
-        pltpu.VMEM((rows_here, 8 * len(strips), hidden), F32) for strips in (early, middle, early + middle)
-    )
+    early, _, late = strips_of(half, rows_here)
+    early_part, late_part = (pltpu.VMEM((rows_here, 8 * len(s), hidden), F32) for s in (early, late))
     tile_part = pltpu.VMEM((rows_here, half * rows_here, hidden), F32)
     right, own_early = in_vmem(
         *call(functools.partial(near_kernel, half, 1), out_shape=(rights, early_part), input_output_aliases={3: 0})(
             *in_vmem(blocks[1]), w_v, left, *in_vmem(right)
         )
     )
-    for step in range(half - 1, half // 2 + 1, -1):
+    for step in range(half - 1, half // 2, -1):
         right = with_block(step, right)
-    step = half // 2 + 1
-    right, own_middle = in_vmem(
+    left, far_tile = in_vmem(
+        *call(functools.partial(far_kernel, half), out_shape=(lefts, tile_part), input_output_aliases={3: 0})(
+            *in_vmem(far), w_v, *in_vmem(right), left
+        )
+    )
+    last, swap = half // 2, [(0, 1), (1, 0)]
+    (block,) = in_vmem(blocks[last])
+    right, far_tile = in_vmem(
         *call(
-            functools.partial(middle_kernel, half, step), out_shape=(rights, middle_part), input_output_aliases={3: 0}
-        )(*in_vmem(blocks[step]), w_v, left, *in_vmem(right))
-    )
-    left, far_sums = in_vmem(
-        *call(functools.partial(far_kernel, half), out_shape=(lefts, far_part), input_output_aliases={3: 0})(
-            *in_vmem(far), w_v, right, left
-        )
-    )
-    right, give = in_vmem(
+            functools.partial(give_kernel, half, last), out_shape=(rights, tile_part), input_output_aliases={3: 0, 4: 1}
+        )(block, w_v, left, *in_vmem(right), far_tile)
+    )
+    got_far = lax.ppermute(far_tile, "col", swap)
+    own_pieces = [pltpu.VMEM((p.stop - p.start, *tile_part.shape[1:]), F32) for p in pieces_of(rows_here)]
+    _, far_last, own_tile, *pieces = in_vmem(
         *call(
-            functools.partial(late_kernel, half, half // 2), out_shape=(rights, tile_part), input_output_aliases={6: 0}
-        )(*in_vmem(blocks[half // 2]), w_v, left, own_early, own_middle, far_sums, *in_vmem(right))
-    )
-    got = lax.ppermute(give, "col", [(0, 1), (1, 0)])
-    keep = call(functools.partial(whole_tile, half, False), out_shape=tile_part)(
-        left, right, own_early, own_middle, far_sums
-    )
-    tri = call(norm_kernel, out_shape=pltpu.VMEM(x.shape, BF16))(*in_vmem(keep, got))
-    pairs = [(2 * r + 1 - r // half, 2 * (r ^ half) + r // half) for r in range(rows)]
-    pairs += [(2 * r + r // half, 2 * (r ^ 1) + r // half) for r in range(rows)]
+            functools.partial(keep_kernel, half, last),
+            out_shape=(rights, late_part, tile_part, *own_pieces),
+            input_output_aliases={4: 0},
+        )(block, w_v, left, own_early, right)
+    )
+    tri, *pieces = in_vmem(
+        *call(
+            functools.partial(norm_kernel, half),
+            out_shape=(pltpu.VMEM(x.shape, BF16), *own_pieces),
+            input_output_aliases={3 + n: 1 + n for n in range(PIECES)},
+            scratch_shapes=[pltpu.VMEM(tile_part.shape, F32)],
+        )(far_tile, far_last, *in_vmem(got_far), *pieces)
+    )
+    pairs = [(2 * r, 2 * (r ^ half) + r // half) for r in range(rows)]
+    pairs += [(2 * r + 1, 2 * r if r < half else 2 * (r ^ 1) + 1) for r in range(rows)]
     arrived = lax.ppermute(tri, ("row", "col"), pairs)
+    got_own = [lax.ppermute(piece, "col", swap) for piece in pieces]
+    in_place = pl.BlockSpec(memory_space=pltpu.VMEM)
+    in_hbm = pl.BlockSpec(memory_space=pltpu.HBM)
+    scratch = [pltpu.VMEM(x.shape, BF16), pltpu.SemaphoreType.DMA]
+    out = call(
+        functools.partial(finish_own_kernel, half),
+        in_specs=[in_place] * (3 + PIECES),
+        out_specs=in_hbm,
+        out_shape=pltpu.HBM(x.shape, BF16),
+        scratch_shapes=scratch,
+    )(own_tile, *in_vmem(*got_own), gate, o_v)
     return call(
-        functools.partial(finish_kernel, half),
-        in_specs=[pl.BlockSpec(memory_space=pltpu.VMEM)] * 4,
-        out_specs=pl.BlockSpec(memory_space=pltpu.VMEM),
-        out_shape=jax.ShapeDtypeStruct(x.shape, BF16),
-    )(*in_vmem(tri, arrived), gate, o_v)
+        functools.partial(finish_far_kernel, half),
+        in_specs=[in_place] * 3 + [in_hbm],
+        out_specs=in_hbm,
+        out_shape=pltpu.HBM(x.shape, BF16),
+        input_output_aliases={3: 0},
+        scratch_shapes=scratch,
+    )(*in_vmem(arrived), gate, o_v, pltpu.with_memory_space_constraint(out, pltpu.HBM))
 
 
 def gather_plan(pair_rep, proj_weight, gate_weight, out_weight):

time: 20.4 us -> 19.9 us (0.975); the launches traced: 20 us -> 19.8 us
  waiting for transfers between devices: 10.3 us -> 9.31 us
  starting transfers between devices: 3.97 us -> 4.6 us
    ppermute x1, waiting for transfers between devices: 4.97 us -> 3.7 us  [fast_plan(): arrived = lax.ppermute(tri, ('row', 'col'), pairs)]
    ppermute x1 -> x4, starting transfers between devices: 0.07 us -> 0.72 us  [the longest x3 0.65 us: fast_plan(): got_own = [lax.ppermute(piece, 'col', swap) for piece in pieces]]
    ppermute x1 -> x4, waiting for transfers between devices: 1.1 us -> 1.43 us  [the longest x3 1.17 us: fast_plan(): got_own = [lax.ppermute(piece, 'col', swap) for piece in pieces]]
    pallas_call x6 -> x7, Pallas kernels: 3.44 us -> 3.5 us  [the longest x1 1.17 us: fast_plan(): call(functools.partial(keep_kernel, half, last), out_shape=(rights, late_...]
  transfers between devices with their start and end apart: 6 -> 9, of which waited for: 3 -> 5; matrix products, arithmetic and copies ran while one was open for 0% -> 0% of each run, Pallas kernels for 20% -> 23%
where the time goes in v6:
time: 19.9 us; the launch traced here: 19.8 us
  waiting for transfers between devices  9.31 us (47%)
  Pallas kernels  5.78 us (29%)
  starting transfers between devices  4.6 us (23%)
    ppermute x4, waiting for transfers between devices, from_step(): return lax.ppermute(x, 'row', [(i, i ^ step) for i in range(rows)])  4.18 us
    ppermute x4, starting transfers between devices, from_step(): return lax.ppermute(x, 'row', [(i, i ^ step) for i in range(rows)])  3.82 us
    ppermute x1, waiting for transfers between devices, fast_plan(): arrived = lax.ppermute(tri, ('row', 'col'), pairs)  3.7 us
    pallas_call x1, Pallas kernels, fast_plan(): call(functools.partial(own_kernel, half), in_specs=[pl.BlockSpec(memory_s...  1.61 us
    pallas_call x1, Pallas kernels, fast_plan(): call(functools.partial(keep_kernel, half, last), out_shape=(rights, late_...  1.17 us
    ppermute x3, waiting for transfers between devices, fast_plan(): got_own = [lax.ppermute(piece, 'col', swap) for piece in pieces]  1.17 us
    pallas_call x1, Pallas kernels, fast_plan(): call(functools.partial(finish_far_kernel, half), in_specs=[in_place] * 3...  0.85 us
    pallas_call x1, Pallas kernels, fast_plan(): call(functools.partial(far_kernel, half), out_shape=(lefts, tile_part), i...  0.83 us
  transfers between devices with their start and end apart: 9, of which 5 were waited for; matrix products, arithmetic and copies ran while one was open for 0% of the time, Pallas kernels for 23%

profile of v6, /device:TPU:26, one launch (start us, length us, event | category | flops | bytes accessed | tf_op | source)
XLA Modules:
  0.0 19.8 jit_solution(3874865361284756000)
XLA Ops:
  0.0 1.5 %collective-permute-start.3 = (bf16[10,40,128]{2,1,0:T(8,128)(2,1)}, bf16[10,40,128]{2,1,0:T(8,128)(2,1)S(1)}, u32[]{:S(2)}, u32[]{:S(2)}) collective-permute-start(bf16[10,40,128]{2,1,0:T(8,128)(2,1)} %x_ref.1), channel_id=1, source_target_pairs={{0,2},{2,0},{4,6},{6,4},{8,10},{10,8},{12,14},{14,12},{1,3},{3,1},... | collective-permute-start | bytes 307208 | tf_op jit(solution)/shard_map/ppermute | solution.py:193
  1.5 0.4 %collective-permute-start.2 = (bf16[10,40,128]{2,1,0:T(8,128)(2,1)}, bf16[10,40,128]{2,1,0:T(8,128)(2,1)S(1)}, u32[]{:S(2)}, u32[]{:S(2)}) collective-permute-start(bf16[10,40,128]{2,1,0:T(8,128)(2,1)} %x_ref.1), channel_id=1, source_target_pairs={{0,6},{2,4},{4,2},{6,0},{8,14},{10,12},{12,10},{14,8},{1,7},{3,5},... | collective-permute-start | bytes 307208 | tf_op jit(solution)/shard_map/ppermute | solution.py:193
  1.9 0.3 %collective-permute-start.1 = (bf16[10,40,128]{2,1,0:T(8,128)(2,1)}, bf16[10,40,128]{2,1,0:T(8,128)(2,1)S(1)}, u32[]{:S(2)}, u32[]{:S(2)}) collective-permute-start(bf16[10,40,128]{2,1,0:T(8,128)(2,1)} %x_ref.1), channel_id=1, source_target_pairs={{0,8},{2,10},{4,12},{6,14},{8,0},{10,2},{12,4},{14,6},{1,9},{3,11}... | collective-permute-start | bytes 307208 | tf_op jit(solution)/shard_map/ppermute | solution.py:193
  2.2 1.6 %collective-permute-start = (bf16[10,40,128]{2,1,0:T(8,128)(2,1)}, bf16[10,40,128]{2,1,0:T(8,128)(2,1)S(1)}, u32[]{:S(2)}, u32[]{:S(2)}) collective-permute-start(bf16[10,40,128]{2,1,0:T(8,128)(2,1)} %x_ref.1), channel_id=1, source_target_pairs={{0,4},{2,6},{4,0},{6,2},{8,12},{10,14},{12,8},{14,10},{1,5},{3,7},... | collective-permute-start | bytes 307208 | tf_op jit(solution)/shard_map/ppermute | solution.py:193
  3.8 1.6 %shard_map.46 = (f32[800,128]{1,0:T(8,128)S(1)}, f32[1600,128]{1,0:T(8,128)S(1)}, f32[400,128]{1,0:T(8,128)S(1)}, bf16[128,512]{1,0:T(8,128)(2,1)S(1)}, bf16[128...) custom-call(bf16[10,40,128]{2,1,0:T(8,128)(2,1)} %x_ref.1, bf16[128,512]{1,0:T(8,128)(2,1)} %w_ref.1, ...), custom_call_target="tpu_custom_call" | custom-call | tf_op jit(solution)/shard_map/pallas_call | solution.py:200
  5.4 0.0 collective-permute-done.3.x_ref
  5.5 0.7 %shard_map.47 = (f32[1600,128]{1,0:T(8,128)S(1)}, f32[10,16,128]{2,1,0:T(8,128)S(1)}) custom-call(bf16[10,40,128]{2,1,0:T(8,128)(2,1)S(1)} %collective-permute-done.3.x_ref, bf16[128,512]{1,0:T(8,128)(2,1)S(1)} %get-tuple-element.25.w_ref, f32[800,128]{1,0:T(8,128)S(1)} %get-tuple-element.26.left_ref._, ...), custom_call_target="tpu_custom_call", output_to_operand_aliasing={{0}: (3, {})} | custom-call | tf_op jit(solution)/shard_map/pallas_call | solution.py:218
  6.1 4.2 %collective-permute-done.2.x_ref = bf16[10,40,128]{2,1,0:T(8,128)(2,1)S(1)} collective-permute-done((bf16[10,40,128]{2,1,0:T(8,128)(2,1)}, bf16[10,40,128]{2,1,0:T(8,128)(2,1)S(1)}, u32[]{:S(2)}, u32[]{:S(2)}) %collective-permute-start.2) | collective-permute-done | bytes 102432 | tf_op jit(solution)/shard_map/ppermute | solution.py:193
  10.3 0.4 %shard_map.48.right_ref._r = f32[1600,128]{1,0:T(8,128)S(1)} custom-call(bf16[10,40,128]{2,1,0:T(8,128)(2,1)S(1)} %collective-permute-done.2.x_ref, bf16[128,512]{1,0:T(8,128)(2,1)S(1)} %get-tuple-element.25.w_ref, f32[1600,128]{1,0:T(8,128)S(1)} %get-tuple-element.28._), custom_call_target="tpu_custom_call", output_to_operand_aliasing={{}: (2, {})} | custom-call | tf_op jit(solution)/shard_map/pallas_call | solution.py:210
  10.7 0.0 collective-permute-done.1.far_ref
  10.7 0.8 %shard_map.49 = (f32[800,128]{1,0:T(8,128)S(1)}, f32[10,40,128]{2,1,0:T(8,128)S(1)}) custom-call(bf16[10,40,128]{2,1,0:T(8,128)(2,1)S(1)} %collective-permute-done.1.far_ref, bf16[128,512]{1,0:T(8,128)(2,1)S(1)} %get-tuple-element.25.w_ref, f32[1600,128]{1,0:T(8,128)S(1)} %shard_map.48.right_ref._r, ...), custom_call_target="tpu_custom_call", output_to_operand_aliasing={{0}: (3, {})} | custom-call | tf_op jit(solution)/shard_map/pallas_call | solution.py:225
  11.5 0.0 collective-permute-done.x_ref
  11.6 0.1 collective-permute-start.4
  11.6 1.2 %shard_map.51 = (f32[1600,128]{1,0:T(8,128)S(1)}, f32[10,16,128]{2,1,0:T(8,128)S(1)}, f32[10,40,128]{2,1,0:T(8,128)S(1)}, f32[3,40,128]{2,1,0:T(8,128)S(1)}, f32...) custom-call(bf16[10,40,128]{2,1,0:T(8,128)(2,1)S(1)} %collective-permute-done.x_ref, ...), custom_call_target="tpu_custom_call", output_to_operand_aliasing={{0}: (4, {})} | custom-call | tf_op jit(solution)/shard_map/pallas_call | solution.py:239
  12.8 0.3 %collective-permute-done.4.got_ref = f32[10,40,128]{2,1,0:T(8,128)S(1)} collective-permute-done((f32[10,40,128]{2,1,0:T(8,128)S(1)}, f32[10,40,128]{2,1,0:T(8,128)S(1)}, u32[]{:S(2)}, u32[]{:S(2)}) %collective-permute-start.4) | collective-permute-done | bytes 204832 | tf_op jit(solution)/shard_map/ppermute | solution.py:236
  13.1 0.3 %shard_map.52 = (bf16[10,40,128]{2,1,0:T(8,128)(2,1)S(1)}, f32[3,40,128]{2,1,0:T(8,128)S(1)}, f32[3,40,128]{2,1,0:T(8,128)S(1)}, f32[4,40,128]{2,1,0:T(8,128)S(1)}) custom-call(f32[10,40,128]{2,1,0:T(8,128)S(1)} %get-tuple-element.31.tile_ref, ...), custom_call_target="tpu_custom_call", output_to_operand_aliasing={{1}: (3, {}), {2}: (4, {}), {3}: (5, {})} | custom-call | tf_op jit(solution)/shard_map/pallas_call | solution.py:246
  13.3 0.1 collective-permute-start.5
  13.4 0.1 collective-permute-start.8
  13.5 0.5 %collective-permute-start.6 = (f32[3,40,128]{2,1,0:T(8,128)S(1)}, f32[3,40,128]{2,1,0:T(8,128)S(1)}, u32[]{:S(2)}, u32[]{:S(2)}) collective-permute-start(f32[3,40,128]{2,1,0:T(8,128)S(1)} %get-tuple-element.42), channel_id=1, source_target_pairs={{0,1},{1,0},{2,3},{3,2},{4,5},{5,4},{6,7},{7,6},{8,9},{9,8},{10,11... | collective-permute-start | bytes 184328 | tf_op jit(solution)/shard_map/ppermute | solution.py:256
  14.0 0.1 collective-permute-start.7
  14.1 0.8 %collective-permute-done.6.refs_0_ = f32[3,40,128]{2,1,0:T(8,128)S(1)} collective-permute-done((f32[3,40,128]{2,1,0:T(8,128)S(1)}, f32[3,40,128]{2,1,0:T(8,128)S(1)}, u32[]{:S(2)}, u32[]{:S(2)}) %collective-permute-start.6) | collective-permute-done | bytes 61472 | tf_op jit(solution)/shard_map/ppermute | solution.py:256
  14.9 0.4 %collective-permute-done.7.refs_1_ = f32[3,40,128]{2,1,0:T(8,128)S(1)} collective-permute-done((f32[3,40,128]{2,1,0:T(8,128)S(1)}, f32[3,40,128]{2,1,0:T(8,128)S(1)}, u32[]{:S(2)}, u32[]{:S(2)}) %collective-permute-start.7) | collective-permute-done | bytes 61472 | tf_op jit(solution)/shard_map/ppermute | solution.py:256
  15.2 0.0 collective-permute-done.8.refs_2_
  15.3 3.7 %collective-permute-done.5.tri_ref = bf16[10,40,128]{2,1,0:T(8,128)(2,1)S(1)} collective-permute-done((bf16[10,40,128]{2,1,0:T(8,128)(2,1)S(1)}, bf16[10,40,128]{2,1,0:T(8,128)(2,1)S(1)}, u32[]{:S(2)}, u32[]{:S(2)}) %collective-permute-start.5) | collective-permute-done | bytes 102432 | tf_op jit(solution)/shard_map/ppermute | solution.py:255
  19.0 0.9 %shard_map.54 = bf16[10,40,128]{2,1,0:T(8,128)(2,1)} custom-call(bf16[10,40,128]{2,1,0:T(8,128)(2,1)S(1)} %collective-permute-done.5.tri_ref, f32[400,128]{1,0:T(8,128)S(1)} %get-tuple-element.39.refs_3_.gate_ref, bf16[128,128]{1,0:T(8,128)(2,1)S(1)} %get-tuple-element.40.refs_4_.o_ref, bf16[10,40,128]{2,1,0:T(8,128)(2,1)} %shard_map.53._), custom_call_target="tpu_custom_call", output_to_operand_aliasing={{}: (3, {})} | custom-call | tf_op jit(solution)/shard_map/pallas_call | solution.py:267
  (2 shorter events, 0.0 us)
Async XLA Ops:
  0.0 5.4 %collective-permute-start.3 = (bf16[10,40,128]{2,1,0:T(8,128)(2,1)}, bf16[10,40,128]{2,1,0:T(8,128)(2,1)S(1)}, u32[]{:S(2)}, u32[]{:S(2)}) collective-permute-start(bf16[10,40,128]{2,1,0:T(8,128)(2,1)} %x_ref.1), channel_id=1, source_target_pairs={{0,2},{2,0},{4,6},{6,4},{8,10},{10,8},{12,14},{14,12},{1,3},{3,1},... | collective-permute-start | bytes 307208 | tf_op jit(solution)/shard_map/ppermute | solution.py:193
  1.5 8.8 %collective-permute-start.2 = (bf16[10,40,128]{2,1,0:T(8,128)(2,1)}, bf16[10,40,128]{2,1,0:T(8,128)(2,1)S(1)}, u32[]{:S(2)}, u32[]{:S(2)}) collective-permute-start(bf16[10,40,128]{2,1,0:T(8,128)(2,1)} %x_ref.1), channel_id=1, source_target_pairs={{0,6},{2,4},{4,2},{6,0},{8,14},{10,12},{12,10},{14,8},{1,7},{3,5},... | collective-permute-start | bytes 307208 | tf_op jit(solution)/shard_map/ppermute | solution.py:193
  1.9 8.8 %collective-permute-start.1 = (bf16[10,40,128]{2,1,0:T(8,128)(2,1)}, bf16[10,40,128]{2,1,0:T(8,128)(2,1)S(1)}, u32[]{:S(2)}, u32[]{:S(2)}) collective-permute-start(bf16[10,40,128]{2,1,0:T(8,128)(2,1)} %x_ref.1), channel_id=1, source_target_pairs={{0,8},{2,10},{4,12},{6,14},{8,0},{10,2},{12,4},{14,6},{1,9},{3,11}... | collective-permute-start | bytes 307208 | tf_op jit(solution)/shard_map/ppermute | solution.py:193
  2.2 9.3 %collective-permute-start = (bf16[10,40,128]{2,1,0:T(8,128)(2,1)}, bf16[10,40,128]{2,1,0:T(8,128)(2,1)S(1)}, u32[]{:S(2)}, u32[]{:S(2)}) collective-permute-start(bf16[10,40,128]{2,1,0:T(8,128)(2,1)} %x_ref.1), channel_id=1, source_target_pairs={{0,4},{2,6},{4,0},{6,2},{8,12},{10,14},{12,8},{14,10},{1,5},{3,7},... | collective-permute-start | bytes 307208 | tf_op jit(solution)/shard_map/ppermute | solution.py:193
  11.6 1.5 %collective-permute-start.4 = (f32[10,40,128]{2,1,0:T(8,128)S(1)}, f32[10,40,128]{2,1,0:T(8,128)S(1)}, u32[]{:S(2)}, u32[]{:S(2)}) collective-permute-start(f32[10,40,128]{2,1,0:T(8,128)S(1)} %get-tuple-element.31.tile_ref), channel_id=1, source_target_pairs={{0,1},{1,0},{2,3},{3,2},{4,5},{5,4},{6,7},{7,6},{8,9},{9,8},{10,11... | collective-permute-start | bytes 614408 | tf_op jit(solution)/shard_map/ppermute | solution.py:236
  13.3 5.6 %collective-permute-start.5 = (bf16[10,40,128]{2,1,0:T(8,128)(2,1)S(1)}, bf16[10,40,128]{2,1,0:T(8,128)(2,1)S(1)}, u32[]{:S(2)}, u32[]{:S(2)}) collective-permute-start(bf16[10,40,128]{2,1,0:T(8,128)(2,1)S(1)} %get-tuple-element.38), channel_id=1, source_target_pairs={{0,8},{2,10},{4,12},{6,14},{8,1},{10,3},{12,5},{14,7},{1,0},{3,2},... | collective-permute-start | bytes 307208 | tf_op jit(solution)/shard_map/ppermute | solution.py:255
  13.4 1.8 %collective-permute-start.8 = (f32[4,40,128]{2,1,0:T(8,128)S(1)}, f32[4,40,128]{2,1,0:T(8,128)S(1)}, u32[]{:S(2)}, u32[]{:S(2)}) collective-permute-start(f32[4,40,128]{2,1,0:T(8,128)S(1)} %get-tuple-element.44), channel_id=1, source_target_pairs={{0,1},{1,0},{2,3},{3,2},{4,5},{5,4},{6,7},{7,6},{8,9},{9,8},{10,11... | collective-permute-start | bytes 245768 | tf_op jit(solution)/shard_map/ppermute | solution.py:256
  13.5 1.4 %collective-permute-start.6 = (f32[3,40,128]{2,1,0:T(8,128)S(1)}, f32[3,40,128]{2,1,0:T(8,128)S(1)}, u32[]{:S(2)}, u32[]{:S(2)}) collective-permute-start(f32[3,40,128]{2,1,0:T(8,128)S(1)} %get-tuple-element.42), channel_id=1, source_target_pairs={{0,1},{1,0},{2,3},{3,2},{4,5},{5,4},{6,7},{7,6},{8,9},{9,8},{10,11... | collective-permute-start | bytes 184328 | tf_op jit(solution)/shard_map/ppermute | solution.py:256
  14.0 1.2 %collective-permute-start.7 = (f32[3,40,128]{2,1,0:T(8,128)S(1)}, f32[3,40,128]{2,1,0:T(8,128)S(1)}, u32[]{:S(2)}, u32[]{:S(2)}) collective-permute-start(f32[3,40,128]{2,1,0:T(8,128)S(1)} %get-tuple-element.43), channel_id=1, source_target_pairs={{0,1},{1,0},{2,3},{3,2},{4,5},{5,4},{6,7},{7,6},{8,9},{9,8},{10,11... | collective-permute-start | bytes 184328 | tf_op jit(solution)/shard_map/ppermute | solution.py:256

commit v7 on v6

--- a/solution.py
+++ b/solution.py
@@ -112,11 +112,18 @@
     products(left_ref, 0, right_ref, early, range(0, tile_ref.shape[1], 8), tile_ref)
 
 
-def far_kernel(half, far_ref, w_ref, right_ref, _, left_ref, tile_ref):
+def put_far(far_ref, w_ref, left_ref):
     rows, hidden = left_ref.shape[0] // 2, left_ref.shape[-1]
     left_ref[pl.ds(rows, rows), :] = side(normalised(far_ref), w_ref[:, : 2 * hidden])
+
+
+def far_kernel(half, far_ref, w_ref, right_ref, _, left_ref, tile_ref):
     early, middle, _ = strips_of(half, tile_ref.shape[0])
-    products(left_ref, rows, right_ref, early + middle, early + middle, tile_ref)
+
+    @pl.when(lax.axis_index("col") == 1)
+    def _():
+        put_far(far_ref, w_ref, left_ref)
+        products(left_ref, left_ref.shape[0] // 2, right_ref, early + middle, early + middle, tile_ref)
 
 
 def give_kernel(half, step, x_ref, w_ref, left_ref, _r, _t, right_ref, tile_ref):
@@ -128,14 +135,33 @@
         products(left_ref, left_ref.shape[0] // 2, right_ref, late, late, tile_ref)
 
 
-def keep_kernel(half, step, x_ref, w_ref, left_ref, own_ref, _, right_ref, last_ref, part_ref, *piece_refs):
+def late_sender(half):
+    return (lax.axis_index("row") >= half) & (lax.axis_index("col") == 0)
+
+
+def keep_kernel(half, step, far_ref, x_ref, w_ref, own_ref, _l, _r, left_ref, right_ref, tile_ref, *part_refs):
+    early, middle, late = strips_of(half, tile_ref.shape[0])
+    strips = early + middle + late
+
+    @pl.when(lax.axis_index("col") == 0)
+    def _():
+        put_far(far_ref, w_ref, left_ref)
+        put_right(half, step, x_ref, w_ref, right_ref)
+        products(left_ref, left_ref.shape[0] // 2, right_ref, strips, strips, tile_ref)
+
+    @pl.when(jnp.logical_not(late_sender(half)))
+    def _():
+        own_sums(half, left_ref, right_ref, own_ref, *part_refs)
+
+
+def norm_kernel(tile_ref, got_ref, tri_ref):
+    @pl.when(lax.axis_index("col") == 0)
+    def _():
+        tri_ref[...] = layer_norm(tile_ref[...] + got_ref[...]).astype(BF16)
+
+
+def own_sums(half, left_ref, right_ref, own_ref, part_ref, *piece_refs):
     early, middle, late = strips_of(half, part_ref.shape[0])
-
-    @pl.when(lax.axis_index("col") == 0)
-    def _():
-        put_right(half, step, x_ref, w_ref, right_ref)
-        products(left_ref, left_ref.shape[0] // 2, right_ref, late, range(0, last_ref.shape[1], 8), last_ref)
-
     for n, s in enumerate(early):
         part_ref[:, pl.ds(s, 8), :] = own_ref[:, 8 * n : 8 * n + 8, :]
     products(left_ref, 0, right_ref, middle + late, middle + late, part_ref)
@@ -143,20 +169,15 @@
         ref[...] = part_ref[rows]
 
 
+def own_sums_kernel(half, left_ref, right_ref, own_ref, *refs):
+    @pl.when(late_sender(half))
+    def _():
+        own_sums(half, left_ref, right_ref, own_ref, *refs[-1 - PIECES :])
+
+
 def pieces_of(count):
     ends = [count * n // PIECES for n in range(PIECES + 1)]
     return [slice(a, b) for a, b in itertools.pairwise(ends)]
-
-
-def norm_kernel(half, tile_ref, last_ref, got_ref, *refs):
-    tri_ref, sum_ref = refs[PIECES], refs[-1]
-
-    @pl.when(lax.axis_index("col") == 0)
-    def _():
-        sum_ref[...] = tile_ref[...] + got_ref[...]
-        for n, s in enumerate(strips_of(half, tri_ref.shape[0])[2]):
-            sum_ref[:, pl.ds(s, 8), :] = last_ref[:, 8 * n : 8 * n + 8, :] + got_ref[:, pl.ds(s, 8), :]
-        tri_ref[...] = layer_norm(sum_ref[...]).astype(BF16)
 
 
 def write_update(tri, gate_ref, o_ref, out_ref, done_ref, sem):
@@ -211,8 +232,7 @@
 
     for step in range(half // 2 - 1, 1, -1):
         right = with_block(step, right)
-    early, _, late = strips_of(half, rows_here)
-    early_part, late_part = (pltpu.VMEM((rows_here, 8 * len(s), hidden), F32) for s in (early, late))
+    early_part = pltpu.VMEM((rows_here, 8 * len(strips_of(half, rows_here)[0]), hidden), F32)
     tile_part = pltpu.VMEM((rows_here, half * rows_here, hidden), F32)
     right, own_early = in_vmem(
         *call(functools.partial(near_kernel, half, 1), out_shape=(rights, early_part), input_output_aliases={3: 0})(
@@ -235,24 +255,24 @@
     )
     got_far = lax.ppermute(far_tile, "col", swap)
     own_pieces = [pltpu.VMEM((p.stop - p.start, *tile_part.shape[1:]), F32) for p in pieces_of(rows_here)]
-    _, far_last, own_tile, *pieces = in_vmem(
+    left, right, keep, *own_parts = in_vmem(
         *call(
             functools.partial(keep_kernel, half, last),
-            out_shape=(rights, late_part, tile_part, *own_pieces),
-            input_output_aliases={4: 0},
-        )(block, w_v, left, own_early, right)
-    )
-    tri, *pieces = in_vmem(
-        *call(
-            functools.partial(norm_kernel, half),
-            out_shape=(pltpu.VMEM(x.shape, BF16), *own_pieces),
-            input_output_aliases={3 + n: 1 + n for n in range(PIECES)},
-            scratch_shapes=[pltpu.VMEM(tile_part.shape, F32)],
-        )(far_tile, far_last, *in_vmem(got_far), *pieces)
-    )
+            out_shape=(lefts, rights, tile_part, tile_part, *own_pieces),
+            input_output_aliases={4: 0, 5: 1},
+        )(*in_vmem(far), block, w_v, own_early, left, right)
+    )
+    (tri,) = in_vmem(call(norm_kernel, out_shape=pltpu.VMEM(x.shape, BF16))(keep, *in_vmem(got_far)))
     pairs = [(2 * r, 2 * (r ^ half) + r // half) for r in range(rows)]
     pairs += [(2 * r + 1, 2 * r if r < half else 2 * (r ^ 1) + 1) for r in range(rows)]
     arrived = lax.ppermute(tri, ("row", "col"), pairs)
+    own_tile, *pieces = in_vmem(
+        *call(
+            functools.partial(own_sums_kernel, half),
+            out_shape=(tile_part, *own_pieces),
+            input_output_aliases={4 + n: n for n in range(1 + PIECES)},
+        )(left, right, own_early, tri, *own_parts)
+    )
     got_own = [lax.ppermute(piece, "col", swap) for piece in pieces]
     in_place = pl.BlockSpec(memory_space=pltpu.VMEM)
     in_hbm = pl.BlockSpec(memory_space=pltpu.HBM)

time: 19.9 us -> 19.7 us (0.990)
  Pallas kernels: 5.78 us -> 5.55 us
    pallas_call x1, Pallas kernels: 0.83 us -> 0.03 us  [fast_plan(): call(functools.partial(far_kernel, half), out_shape=(lefts, tile_part), i...]
    pallas_call x2 -> x3, Pallas kernels: 1.43 us -> 2.01 us  [the longest x1 1.29 us: fast_plan(): call(functools.partial(keep_kernel, half, last), out_shape=(lefts, rights...]
where the time goes in v7:
time: 19.7 us; the launch traced here: 19.5 us
  waiting for transfers between devices  9.19 us (47%)
  Pallas kernels  5.55 us (28%)
  starting transfers between devices  4.67 us (24%)
    ppermute x4, waiting for transfers between devices, from_step(): return lax.ppermute(x, 'row', [(i, i ^ step) for i in range(rows)])  4.18 us
    ppermute x4, starting transfers between devices, from_step(): return lax.ppermute(x, 'row', [(i, i ^ step) for i in range(rows)])  3.82 us
    ppermute x1, waiting for transfers between devices, fast_plan(): arrived = lax.ppermute(tri, ('row', 'col'), pairs)  3.76 us
    pallas_call x1, Pallas kernels, fast_plan(): call(functools.partial(own_kernel, half), in_specs=[pl.BlockSpec(memory_s...  1.61 us
    pallas_call x1, Pallas kernels, fast_plan(): call(functools.partial(keep_kernel, half, last), out_shape=(lefts, rights...  1.29 us
    ppermute x3, waiting for transfers between devices, fast_plan(): got_own = [lax.ppermute(piece, 'col', swap) for piece in pieces]  1.11 us
    pallas_call x1, Pallas kernels, fast_plan(): call(functools.partial(finish_far_kernel, half), in_specs=[in_place] * 3...  0.84 us
    ppermute x3, starting transfers between devices, fast_plan(): got_own = [lax.ppermute(piece, 'col', swap) for piece in pieces]  0.71 us
  transfers between devices with their start and end apart: 9, of which 5 were waited for; matrix products, arithmetic and copies ran while one was open for 0% of the time, Pallas kernels for 23%

profile of v7, /device:TPU:26, one launch (start us, length us, event | category | flops | bytes accessed | tf_op | source)
XLA Modules:
  0.0 19.5 jit_solution(15658147178816874491)
XLA Ops:
  0.0 1.5 %collective-permute-start.2 = (bf16[10,40,128]{2,1,0:T(8,128)(2,1)}, bf16[10,40,128]{2,1,0:T(8,128)(2,1)S(1)}, u32[]{:S(2)}, u32[]{:S(2)}) collective-permute-start(bf16[10,40,128]{2,1,0:T(8,128)(2,1)} %x_ref.1), channel_id=1, source_target_pairs={{0,2},{2,0},{4,6},{6,4},{8,10},{10,8},{12,14},{14,12},{1,3},{3,1},... | collective-permute-start | bytes 307208 | tf_op jit(solution)/shard_map/ppermute | solution.py:214
  1.5 0.4 %collective-permute-start.3 = (bf16[10,40,128]{2,1,0:T(8,128)(2,1)}, bf16[10,40,128]{2,1,0:T(8,128)(2,1)S(1)}, u32[]{:S(2)}, u32[]{:S(2)}) collective-permute-start(bf16[10,40,128]{2,1,0:T(8,128)(2,1)} %x_ref.1), channel_id=1, source_target_pairs={{0,6},{2,4},{4,2},{6,0},{8,14},{10,12},{12,10},{14,8},{1,7},{3,5},... | collective-permute-start | bytes 307208 | tf_op jit(solution)/shard_map/ppermute | solution.py:214
  1.9 0.3 %collective-permute-start = (bf16[10,40,128]{2,1,0:T(8,128)(2,1)}, bf16[10,40,128]{2,1,0:T(8,128)(2,1)S(1)}, u32[]{:S(2)}, u32[]{:S(2)}) collective-permute-start(bf16[10,40,128]{2,1,0:T(8,128)(2,1)} %x_ref.1), channel_id=1, source_target_pairs={{0,8},{2,10},{4,12},{6,14},{8,0},{10,2},{12,4},{14,6},{1,9},{3,11}... | collective-permute-start | bytes 307208 | tf_op jit(solution)/shard_map/ppermute | solution.py:214
  2.2 1.6 %collective-permute-start.1 = (bf16[10,40,128]{2,1,0:T(8,128)(2,1)}, bf16[10,40,128]{2,1,0:T(8,128)(2,1)S(1)}, u32[]{:S(2)}, u32[]{:S(2)}) collective-permute-start(bf16[10,40,128]{2,1,0:T(8,128)(2,1)} %x_ref.1), channel_id=1, source_target_pairs={{0,4},{2,6},{4,0},{6,2},{8,12},{10,14},{12,8},{14,10},{1,5},{3,7},... | collective-permute-start | bytes 307208 | tf_op jit(solution)/shard_map/ppermute | solution.py:214
  3.8 1.6 %shard_map.46 = (f32[800,128]{1,0:T(8,128)S(1)}, f32[1600,128]{1,0:T(8,128)S(1)}, f32[400,128]{1,0:T(8,128)S(1)}, bf16[128,512]{1,0:T(8,128)(2,1)S(1)}, bf16[128...) custom-call(bf16[10,40,128]{2,1,0:T(8,128)(2,1)} %x_ref.1, bf16[128,512]{1,0:T(8,128)(2,1)} %w_ref.1, ...), custom_call_target="tpu_custom_call" | custom-call | tf_op jit(solution)/shard_map/pallas_call | solution.py:221
  5.4 0.0 collective-permute-done.2.x_ref
  5.5 0.7 %shard_map.47 = (f32[1600,128]{1,0:T(8,128)S(1)}, f32[10,16,128]{2,1,0:T(8,128)S(1)}) custom-call(bf16[10,40,128]{2,1,0:T(8,128)(2,1)S(1)} %collective-permute-done.2.x_ref, bf16[128,512]{1,0:T(8,128)(2,1)S(1)} %get-tuple-element.27.w_ref, f32[800,128]{1,0:T(8,128)S(1)} %get-tuple-element.28.left_ref._, ...), custom_call_target="tpu_custom_call", output_to_operand_aliasing={{0}: (3, {})} | custom-call | tf_op jit(solution)/shard_map/pallas_call | solution.py:238
  6.1 4.2 %collective-permute-done.3.x_ref = bf16[10,40,128]{2,1,0:T(8,128)(2,1)S(1)} collective-permute-done((bf16[10,40,128]{2,1,0:T(8,128)(2,1)}, bf16[10,40,128]{2,1,0:T(8,128)(2,1)S(1)}, u32[]{:S(2)}, u32[]{:S(2)}) %collective-permute-start.3) | collective-permute-done | bytes 102432 | tf_op jit(solution)/shard_map/ppermute | solution.py:214
  10.3 0.4 %shard_map.48.right_ref._r = f32[1600,128]{1,0:T(8,128)S(1)} custom-call(bf16[10,40,128]{2,1,0:T(8,128)(2,1)S(1)} %collective-permute-done.3.x_ref, bf16[128,512]{1,0:T(8,128)(2,1)S(1)} %get-tuple-element.27.w_ref, f32[1600,128]{1,0:T(8,128)S(1)} %get-tuple-element.31._), custom_call_target="tpu_custom_call", output_to_operand_aliasing={{}: (2, {})} | custom-call | tf_op jit(solution)/shard_map/pallas_call | solution.py:231
  10.7 0.0 collective-permute-done.far_ref
  10.7 0.0 collective-permute-done.1.x_ref
  10.8 0.1 collective-permute-start.4
  10.8 1.3 %shard_map.51 = (f32[800,128]{1,0:T(8,128)S(1)}, f32[1600,128]{1,0:T(8,128)S(1)}, f32[10,40,128]{2,1,0:T(8,128)S(1)}, f32[10,40,128]{2,1,0:T(8,128)S(1)}, f32[3,...) custom-call(bf16[10,40,128]{2,1,0:T(8,128)(2,1)S(1)} %collective-per, ...), custom_call_target="tpu_custom_call", output_to_operand_aliasing={{0}: (4, {}), {1}: (5, {})} | custom-call | tf_op jit(solution)/shard_map/pallas_call | solution.py:259
  12.1 0.1 collective-permute-done.4.got_ref
  12.3 0.2 %shard_map.52.refs_0_ = bf16[10,40,128]{2,1,0:T(8,128)(2,1)S(1)} custom-call(f32[10,40,128]{2,1,0:T(8,128)S(1)} %get-tuple-element.35.tile_ref, f32[10,40,128]{2,1,0:T(8,128)S(1)} %collective-permute-done.4.got_ref), custom_call_target="tpu_custom_call" | custom-call | tf_op jit(solution)/shard_map/pallas_call | solution.py:265
  12.5 0.1 collective-permute-start.5
  12.6 0.5 %shard_map.53 = (f32[10,40,128]{2,1,0:T(8,128)S(1)}, f32[3,40,128]{2,1,0:T(8,128)S(1)}, f32[3,40,128]{2,1,0:T(8,128)S(1)}, f32[4,40,128]{2,1,0:T(8,128)S(1)}) custom-call(f32[800,128]{1,0:T(8,128)S(1)} %get-tuple-element.39.left_ref, ...), custom_call_target="tpu_custom_call", output_to_operand_aliasing={{0}: (4, {}), {1}: (5, {}), {2}: (6, {}), {3}: (7, {})} | custom-call | tf_op jit(solution)/shard_map/pallas_call | solution.py:270
  13.1 0.2 %collective-permute-start.8 = (f32[4,40,128]{2,1,0:T(8,128)S(1)}, f32[4,40,128]{2,1,0:T(8,128)S(1)}, u32[]{:S(2)}, u32[]{:S(2)}) collective-permute-start(f32[4,40,128]{2,1,0:T(8,128)S(1)} %get-tuple-element.48), channel_id=1, source_target_pairs={{0,1},{1,0},{2,3},{3,2},{4,5},{5,4},{6,7},{7,6},{8,9},{9,8},{10,11... | collective-permute-start | bytes 245768 | tf_op jit(solution)/shard_map/ppermute | solution.py:276
  13.3 0.4 %collective-permute-start.6 = (f32[3,40,128]{2,1,0:T(8,128)S(1)}, f32[3,40,128]{2,1,0:T(8,128)S(1)}, u32[]{:S(2)}, u32[]{:S(2)}) collective-permute-start(f32[3,40,128]{2,1,0:T(8,128)S(1)} %get-tuple-element.46), channel_id=1, source_target_pairs={{0,1},{1,0},{2,3},{3,2},{4,5},{5,4},{6,7},{7,6},{8,9},{9,8},{10,11... | collective-permute-start | bytes 184328 | tf_op jit(solution)/shard_map/ppermute | solution.py:276
  13.7 0.1 collective-permute-start.7
  13.8 0.8 %collective-permute-done.6.refs_0_ = f32[3,40,128]{2,1,0:T(8,128)S(1)} collective-permute-done((f32[3,40,128]{2,1,0:T(8,128)S(1)}, f32[3,40,128]{2,1,0:T(8,128)S(1)}, u32[]{:S(2)}, u32[]{:S(2)}) %collective-permute-start.6) | collective-permute-done | bytes 61472 | tf_op jit(solution)/shard_map/ppermute | solution.py:276
  14.5 0.4 %collective-permute-done.7.refs_1_ = f32[3,40,128]{2,1,0:T(8,128)S(1)} collective-permute-done((f32[3,40,128]{2,1,0:T(8,128)S(1)}, f32[3,40,128]{2,1,0:T(8,128)S(1)}, u32[]{:S(2)}, u32[]{:S(2)}) %collective-permute-start.7) | collective-permute-done | bytes 61472 | tf_op jit(solution)/shard_map/ppermute | solution.py:276
  14.9 0.0 collective-permute-done.8.refs_2_
  14.9 3.8 %collective-permute-done.5.tri_ref = bf16[10,40,128]{2,1,0:T(8,128)(2,1)S(1)} collective-permute-done((bf16[10,40,128]{2,1,0:T(8,128)(2,1)S(1)}, bf16[10,40,128]{2,1,0:T(8,128)(2,1)S(1)}, u32[]{:S(2)}, u32[]{:S(2)}) %collective-permute-start.5) | collective-permute-done | bytes 102432 | tf_op jit(solution)/shard_map/ppermute | solution.py:268
  18.7 0.8 %shard_map.55 = bf16[10,40,128]{2,1,0:T(8,128)(2,1)} custom-call(bf16[10,40,128]{2,1,0:T(8,128)(2,1)S(1)} %collective-permute-done.5.tri_ref, f32[400,128]{1,0:T(8,128)S(1)} %get-tuple-element.37.refs_3_.gate_ref, bf16[128,128]{1,0:T(8,128)(2,1)S(1)} %get-tuple-element.38.refs_4_.o_ref, bf16[10,40,128]{2,1,0:T(8,128)(2,1)} %shard_map.54._), custom_call_target="tpu_custom_call", output_to_operand_aliasing={{}: (3, {})} | custom-call | tf_op jit(solution)/shard_map/pallas_call | solution.py:287
  (3 shorter events, 0.1 us)
Async XLA Ops:
  0.0 5.4 %collective-permute-start.2 = (bf16[10,40,128]{2,1,0:T(8,128)(2,1)}, bf16[10,40,128]{2,1,0:T(8,128)(2,1)S(1)}, u32[]{:S(2)}, u32[]{:S(2)}) collective-permute-start(bf16[10,40,128]{2,1,0:T(8,128)(2,1)} %x_ref.1), channel_id=1, source_target_pairs={{0,2},{2,0},{4,6},{6,4},{8,10},{10,8},{12,14},{14,12},{1,3},{3,1},... | collective-permute-start | bytes 307208 | tf_op jit(solution)/shard_map/ppermute | solution.py:214
  1.5 8.8 %collective-permute-start.3 = (bf16[10,40,128]{2,1,0:T(8,128)(2,1)}, bf16[10,40,128]{2,1,0:T(8,128)(2,1)S(1)}, u32[]{:S(2)}, u32[]{:S(2)}) collective-permute-start(bf16[10,40,128]{2,1,0:T(8,128)(2,1)} %x_ref.1), channel_id=1, source_target_pairs={{0,6},{2,4},{4,2},{6,0},{8,14},{10,12},{12,10},{14,8},{1,7},{3,5},... | collective-permute-start | bytes 307208 | tf_op jit(solution)/shard_map/ppermute | solution.py:214
  1.9 8.8 %collective-permute-start = (bf16[10,40,128]{2,1,0:T(8,128)(2,1)}, bf16[10,40,128]{2,1,0:T(8,128)(2,1)S(1)}, u32[]{:S(2)}, u32[]{:S(2)}) collective-permute-start(bf16[10,40,128]{2,1,0:T(8,128)(2,1)} %x_ref.1), channel_id=1, source_target_pairs={{0,8},{2,10},{4,12},{6,14},{8,0},{10,2},{12,4},{14,6},{1,9},{3,11}... | collective-permute-start | bytes 307208 | tf_op jit(solution)/shard_map/ppermute | solution.py:214
  2.2 8.5 %collective-permute-start.1 = (bf16[10,40,128]{2,1,0:T(8,128)(2,1)}, bf16[10,40,128]{2,1,0:T(8,128)(2,1)S(1)}, u32[]{:S(2)}, u32[]{:S(2)}) collective-permute-start(bf16[10,40,128]{2,1,0:T(8,128)(2,1)} %x_ref.1), channel_id=1, source_target_pairs={{0,4},{2,6},{4,0},{6,2},{8,12},{10,14},{12,8},{14,10},{1,5},{3,7},... | collective-permute-start | bytes 307208 | tf_op jit(solution)/shard_map/ppermute | solution.py:214
  10.8 1.5 %collective-permute-start.4 = (f32[10,40,128]{2,1,0:T(8,128)S(1)}, f32[10,40,128]{2,1,0:T(8,128)S(1)}, u32[]{:S(2)}, u32[]{:S(2)}) collective-permute-start(f32[10,40,128]{2,1,0:T(8,128)S(1)} %get-tuple-element.36), channel_id=1, source_target_pairs={{0,1},{1,0},{2,3},{3,2},{4,5},{5,4},{6,7},{7,6},{8,9},{9,8},{10,11... | collective-permute-start | bytes 614408 | tf_op jit(solution)/shard_map/ppermute | solution.py:256
  12.5 6.2 %collective-permute-start.5 = (bf16[10,40,128]{2,1,0:T(8,128)(2,1)S(1)}, bf16[10,40,128]{2,1,0:T(8,128)(2,1)S(1)}, u32[]{:S(2)}, u32[]{:S(2)}) collective-permute-start(bf16[10,40,128]{2,1,0:T(8,128)(2,1)S(1)} %shard_map.52.refs_0_), channel_id=1, source_target_pairs={{0,8},{2,10},{4,12},{6,14},{8,1},{10,3},{12,5},{14,7},{1,0},{3,2},... | collective-permute-start | bytes 307208 | tf_op jit(solution)/shard_map/ppermute | solution.py:268
  13.1 1.8 %collective-permute-start.8 = (f32[4,40,128]{2,1,0:T(8,128)S(1)}, f32[4,40,128]{2,1,0:T(8,128)S(1)}, u32[]{:S(2)}, u32[]{:S(2)}) collective-permute-start(f32[4,40,128]{2,1,0:T(8,128)S(1)} %get-tuple-element.48), channel_id=1, source_target_pairs={{0,1},{1,0},{2,3},{3,2},{4,5},{5,4},{6,7},{7,6},{8,9},{9,8},{10,11... | collective-permute-start | bytes 245768 | tf_op jit(solution)/shard_map/ppermute | solution.py:276
  13.3 1.3 %collective-permute-start.6 = (f32[3,40,128]{2,1,0:T(8,128)S(1)}, f32[3,40,128]{2,1,0:T(8,128)S(1)}, u32[]{:S(2)}, u32[]{:S(2)}) collective-permute-start(f32[3,40,128]{2,1,0:T(8,128)S(1)} %get-tuple-element.46), channel_id=1, source_target_pairs={{0,1},{1,0},{2,3},{3,2},{4,5},{5,4},{6,7},{7,6},{8,9},{9,8},{10,11... | collective-permute-start | bytes 184328 | tf_op jit(solution)/shard_map/ppermute | solution.py:276
  13.7 1.2 %collective-permute-start.7 = (f32[3,40,128]{2,1,0:T(8,128)S(1)}, f32[3,40,128]{2,1,0:T(8,128)S(1)}, u32[]{:S(2)}, u32[]{:S(2)}) collective-permute-start(f32[3,40,128]{2,1,0:T(8,128)S(1)} %get-tuple-element.47), channel_id=1, source_target_pairs={{0,1},{1,0},{2,3},{3,2},{4,5},{5,4},{6,7},{7,6},{8,9},{9,8},{10,11... | collective-permute-start | bytes 184328 | tf_op jit(solution)/shard_map/ppermute | solution.py:276

commit v8 on v7

--- a/solution.py
+++ b/solution.py
@@ -215,7 +215,7 @@
 
     far = from_step(half)
     blocks = {step: from_step(step) for step in range(1, half)}
-    lefts, rights = pltpu.VMEM((2 * positions, hidden), F32), pltpu.VMEM((half * positions, hidden), F32)
+    lefts, rights = pltpu.VMEM((2 * positions, hidden), F32), pltpu.VMEM((half * positions + depth, hidden), F32)
     brought = (x, proj_weight, gate_weight, out_weight)
     left, right, gate, w_v, _, o_v = in_vmem(
         *call(

time: 19.7 us -> 19.7 us (level)
  no operation moved by 1% of the time
where the time goes in v8:
time: 19.7 us; the launch traced here: 19.5 us
  waiting for transfers between devices  9.19 us (47%)
  Pallas kernels  5.55 us (28%)
  starting transfers between devices  4.67 us (24%)
    ppermute x4, waiting for transfers between devices, from_step(): return lax.ppermute(x, 'row', [(i, i ^ step) for i in range(rows)])  4.18 us
    ppermute x4, starting transfers between devices, from_step(): return lax.ppermute(x, 'row', [(i, i ^ step) for i in range(rows)])  3.82 us
    ppermute x1, waiting for transfers between devices, fast_plan(): arrived = lax.ppermute(tri, ('row', 'col'), pairs)  3.76 us
    pallas_call x1, Pallas kernels, fast_plan(): call(functools.partial(own_kernel, half), in_specs=[pl.BlockSpec(memory_s...  1.61 us
    pallas_call x1, Pallas kernels, fast_plan(): call(functools.partial(keep_kernel, half, last), out_shape=(lefts, rights...  1.29 us
    ppermute x3, waiting for transfers between devices, fast_plan(): got_own = [lax.ppermute(piece, 'col', swap) for piece in pieces]  1.11 us
    pallas_call x1, Pallas kernels, fast_plan(): call(functools.partial(finish_far_kernel, half), in_specs=[in_place] * 3...  0.84 us
    ppermute x3, starting transfers between devices, fast_plan(): got_own = [lax.ppermute(piece, 'col', swap) for piece in pieces]  0.71 us
  transfers between devices with their start and end apart: 9, of which 5 were waited for; matrix products, arithmetic and copies ran while one was open for 0% of the time, Pallas kernels for 23%

profile of v8, /device:TPU:26, one launch (start us, length us, event | category | flops | bytes accessed | tf_op | source)
XLA Modules:
  0.0 19.5 jit_solution(5358498555885278044)
XLA Ops:
  0.0 1.5 %collective-permute-start.2 = (bf16[10,40,128]{2,1,0:T(8,128)(2,1)}, bf16[10,40,128]{2,1,0:T(8,128)(2,1)S(1)}, u32[]{:S(2)}, u32[]{:S(2)}) collective-permute-start(bf16[10,40,128]{2,1,0:T(8,128)(2,1)} %x_ref.1), channel_id=1, source_target_pairs={{0,2},{2,0},{4,6},{6,4},{8,10},{10,8},{12,14},{14,12},{1,3},{3,1},... | collective-permute-start | bytes 307208 | tf_op jit(solution)/shard_map/ppermute | solution.py:214
  1.5 0.4 %collective-permute-start.3 = (bf16[10,40,128]{2,1,0:T(8,128)(2,1)}, bf16[10,40,128]{2,1,0:T(8,128)(2,1)S(1)}, u32[]{:S(2)}, u32[]{:S(2)}) collective-permute-start(bf16[10,40,128]{2,1,0:T(8,128)(2,1)} %x_ref.1), channel_id=1, source_target_pairs={{0,6},{2,4},{4,2},{6,0},{8,14},{10,12},{12,10},{14,8},{1,7},{3,5},... | collective-permute-start | bytes 307208 | tf_op jit(solution)/shard_map/ppermute | solution.py:214
  1.9 0.3 %collective-permute-start = (bf16[10,40,128]{2,1,0:T(8,128)(2,1)}, bf16[10,40,128]{2,1,0:T(8,128)(2,1)S(1)}, u32[]{:S(2)}, u32[]{:S(2)}) collective-permute-start(bf16[10,40,128]{2,1,0:T(8,128)(2,1)} %x_ref.1), channel_id=1, source_target_pairs={{0,8},{2,10},{4,12},{6,14},{8,0},{10,2},{12,4},{14,6},{1,9},{3,11}... | collective-permute-start | bytes 307208 | tf_op jit(solution)/shard_map/ppermute | solution.py:214
  2.2 1.6 %collective-permute-start.1 = (bf16[10,40,128]{2,1,0:T(8,128)(2,1)}, bf16[10,40,128]{2,1,0:T(8,128)(2,1)S(1)}, u32[]{:S(2)}, u32[]{:S(2)}) collective-permute-start(bf16[10,40,128]{2,1,0:T(8,128)(2,1)} %x_ref.1), channel_id=1, source_target_pairs={{0,4},{2,6},{4,0},{6,2},{8,12},{10,14},{12,8},{14,10},{1,5},{3,7},... | collective-permute-start | bytes 307208 | tf_op jit(solution)/shard_map/ppermute | solution.py:214
  3.8 1.6 %shard_map.46 = (f32[800,128]{1,0:T(8,128)S(1)}, f32[1640,128]{1,0:T(8,128)S(1)}, f32[400,128]{1,0:T(8,128)S(1)}, bf16[128,512]{1,0:T(8,128)(2,1)S(1)}, bf16[128...) custom-call(bf16[10,40,128]{2,1,0:T(8,128)(2,1)} %x_ref.1, bf16[128,512]{1,0:T(8,128)(2,1)} %w_ref.1, ...), custom_call_target="tpu_custom_call" | custom-call | tf_op jit(solution)/shard_map/pallas_call | solution.py:221
  5.4 0.0 collective-permute-done.2.x_ref
  5.5 0.7 %shard_map.47 = (f32[1640,128]{1,0:T(8,128)S(1)}, f32[10,16,128]{2,1,0:T(8,128)S(1)}) custom-call(bf16[10,40,128]{2,1,0:T(8,128)(2,1)S(1)} %collective-permute-done.2.x_ref, bf16[128,512]{1,0:T(8,128)(2,1)S(1)} %get-tuple-element.27.w_ref, f32[800,128]{1,0:T(8,128)S(1)} %get-tuple-element.28.left_ref._, ...), custom_call_target="tpu_custom_call", output_to_operand_aliasing={{0}: (3, {})} | custom-call | tf_op jit(solution)/shard_map/pallas_call | solution.py:238
  6.1 4.2 %collective-permute-done.3.x_ref = bf16[10,40,128]{2,1,0:T(8,128)(2,1)S(1)} collective-permute-done((bf16[10,40,128]{2,1,0:T(8,128)(2,1)}, bf16[10,40,128]{2,1,0:T(8,128)(2,1)S(1)}, u32[]{:S(2)}, u32[]{:S(2)}) %collective-permute-start.3) | collective-permute-done | bytes 102432 | tf_op jit(solution)/shard_map/ppermute | solution.py:214
  10.3 0.4 %shard_map.48.right_ref._r = f32[1640,128]{1,0:T(8,128)S(1)} custom-call(bf16[10,40,128]{2,1,0:T(8,128)(2,1)S(1)} %collective-permute-done.3.x_ref, bf16[128,512]{1,0:T(8,128)(2,1)S(1)} %get-tuple-element.27.w_ref, f32[1640,128]{1,0:T(8,128)S(1)} %get-tuple-element.31._), custom_call_target="tpu_custom_call", output_to_operand_aliasing={{}: (2, {})} | custom-call | tf_op jit(solution)/shard_map/pallas_call | solution.py:231
  10.7 0.0 collective-permute-done.far_ref
  10.7 0.0 collective-permute-done.1.x_ref
  10.8 0.1 collective-permute-start.4
  10.8 1.3 %shard_map.51 = (f32[800,128]{1,0:T(8,128)S(1)}, f32[1640,128]{1,0:T(8,128)S(1)}, f32[10,40,128]{2,1,0:T(8,128)S(1)}, f32[10,40,128]{2,1,0:T(8,128)S(1)}, f32[3,...) custom-call(bf16[10,40,128]{2,1,0:T(8,128)(2,1)S(1)} %collective-per, ...), custom_call_target="tpu_custom_call", output_to_operand_aliasing={{0}: (4, {}), {1}: (5, {})} | custom-call | tf_op jit(solution)/shard_map/pallas_call | solution.py:259
  12.1 0.1 collective-permute-done.4.got_ref
  12.3 0.2 %shard_map.52.refs_0_ = bf16[10,40,128]{2,1,0:T(8,128)(2,1)S(1)} custom-call(f32[10,40,128]{2,1,0:T(8,128)S(1)} %get-tuple-element.35.tile_ref, f32[10,40,128]{2,1,0:T(8,128)S(1)} %collective-permute-done.4.got_ref), custom_call_target="tpu_custom_call" | custom-call | tf_op jit(solution)/shard_map/pallas_call | solution.py:265
  12.5 0.1 collective-permute-start.5
  12.6 0.5 %shard_map.53 = (f32[10,40,128]{2,1,0:T(8,128)S(1)}, f32[3,40,128]{2,1,0:T(8,128)S(1)}, f32[3,40,128]{2,1,0:T(8,128)S(1)}, f32[4,40,128]{2,1,0:T(8,128)S(1)}) custom-call(f32[800,128]{1,0:T(8,128)S(1)} %get-tuple-element.39.left_ref, ...), custom_call_target="tpu_custom_call", output_to_operand_aliasing={{0}: (4, {}), {1}: (5, {}), {2}: (6, {}), {3}: (7, {})} | custom-call | tf_op jit(solution)/shard_map/pallas_call | solution.py:270
  13.1 0.2 %collective-permute-start.8 = (f32[4,40,128]{2,1,0:T(8,128)S(1)}, f32[4,40,128]{2,1,0:T(8,128)S(1)}, u32[]{:S(2)}, u32[]{:S(2)}) collective-permute-start(f32[4,40,128]{2,1,0:T(8,128)S(1)} %get-tuple-element.48), channel_id=1, source_target_pairs={{0,1},{1,0},{2,3},{3,2},{4,5},{5,4},{6,7},{7,6},{8,9},{9,8},{10,11... | collective-permute-start | bytes 245768 | tf_op jit(solution)/shard_map/ppermute | solution.py:276
  13.3 0.4 %collective-permute-start.6 = (f32[3,40,128]{2,1,0:T(8,128)S(1)}, f32[3,40,128]{2,1,0:T(8,128)S(1)}, u32[]{:S(2)}, u32[]{:S(2)}) collective-permute-start(f32[3,40,128]{2,1,0:T(8,128)S(1)} %get-tuple-element.46), channel_id=1, source_target_pairs={{0,1},{1,0},{2,3},{3,2},{4,5},{5,4},{6,7},{7,6},{8,9},{9,8},{10,11... | collective-permute-start | bytes 184328 | tf_op jit(solution)/shard_map/ppermute | solution.py:276
  13.7 0.1 collective-permute-start.7
  13.8 0.8 %collective-permute-done.6.refs_0_ = f32[3,40,128]{2,1,0:T(8,128)S(1)} collective-permute-done((f32[3,40,128]{2,1,0:T(8,128)S(1)}, f32[3,40,128]{2,1,0:T(8,128)S(1)}, u32[]{:S(2)}, u32[]{:S(2)}) %collective-permute-start.6) | collective-permute-done | bytes 61472 | tf_op jit(solution)/shard_map/ppermute | solution.py:276
  14.5 0.4 %collective-permute-done.7.refs_1_ = f32[3,40,128]{2,1,0:T(8,128)S(1)} collective-permute-done((f32[3,40,128]{2,1,0:T(8,128)S(1)}, f32[3,40,128]{2,1,0:T(8,128)S(1)}, u32[]{:S(2)}, u32[]{:S(2)}) %collective-permute-start.7) | collective-permute-done | bytes 61472 | tf_op jit(solution)/shard_map/ppermute | solution.py:276
  14.9 0.0 collective-permute-done.8.refs_2_
  14.9 3.8 %collective-permute-done.5.tri_ref = bf16[10,40,128]{2,1,0:T(8,128)(2,1)S(1)} collective-permute-done((bf16[10,40,128]{2,1,0:T(8,128)(2,1)S(1)}, bf16[10,40,128]{2,1,0:T(8,128)(2,1)S(1)}, u32[]{:S(2)}, u32[]{:S(2)}) %collective-permute-start.5) | collective-permute-done | bytes 102432 | tf_op jit(solution)/shard_map/ppermute | solution.py:268
  18.7 0.8 %shard_map.55 = bf16[10,40,128]{2,1,0:T(8,128)(2,1)} custom-call(bf16[10,40,128]{2,1,0:T(8,128)(2,1)S(1)} %collective-permute-done.5.tri_ref, f32[400,128]{1,0:T(8,128)S(1)} %get-tuple-element.37.refs_3_.gate_ref, bf16[128,128]{1,0:T(8,128)(2,1)S(1)} %get-tuple-element.38.refs_4_.o_ref, bf16[10,40,128]{2,1,0:T(8,128)(2,1)} %shard_map.54._), custom_call_target="tpu_custom_call", output_to_operand_aliasing={{}: (3, {})} | custom-call | tf_op jit(solution)/shard_map/pallas_call | solution.py:287
  (3 shorter events, 0.1 us)
Async XLA Ops:
  0.0 5.4 %collective-permute-start.2 = (bf16[10,40,128]{2,1,0:T(8,128)(2,1)}, bf16[10,40,128]{2,1,0:T(8,128)(2,1)S(1)}, u32[]{:S(2)}, u32[]{:S(2)}) collective-permute-start(bf16[10,40,128]{2,1,0:T(8,128)(2,1)} %x_ref.1), channel_id=1, source_target_pairs={{0,2},{2,0},{4,6},{6,4},{8,10},{10,8},{12,14},{14,12},{1,3},{3,1},... | collective-permute-start | bytes 307208 | tf_op jit(solution)/shard_map/ppermute | solution.py:214
  1.5 8.8 %collective-permute-start.3 = (bf16[10,40,128]{2,1,0:T(8,128)(2,1)}, bf16[10,40,128]{2,1,0:T(8,128)(2,1)S(1)}, u32[]{:S(2)}, u32[]{:S(2)}) collective-permute-start(bf16[10,40,128]{2,1,0:T(8,128)(2,1)} %x_ref.1), channel_id=1, source_target_pairs={{0,6},{2,4},{4,2},{6,0},{8,14},{10,12},{12,10},{14,8},{1,7},{3,5},... | collective-permute-start | bytes 307208 | tf_op jit(solution)/shard_map/ppermute | solution.py:214
  1.9 8.8 %collective-permute-start = (bf16[10,40,128]{2,1,0:T(8,128)(2,1)}, bf16[10,40,128]{2,1,0:T(8,128)(2,1)S(1)}, u32[]{:S(2)}, u32[]{:S(2)}) collective-permute-start(bf16[10,40,128]{2,1,0:T(8,128)(2,1)} %x_ref.1), channel_id=1, source_target_pairs={{0,8},{2,10},{4,12},{6,14},{8,0},{10,2},{12,4},{14,6},{1,9},{3,11}... | collective-permute-start | bytes 307208 | tf_op jit(solution)/shard_map/ppermute | solution.py:214
  2.2 8.5 %collective-permute-start.1 = (bf16[10,40,128]{2,1,0:T(8,128)(2,1)}, bf16[10,40,128]{2,1,0:T(8,128)(2,1)S(1)}, u32[]{:S(2)}, u32[]{:S(2)}) collective-permute-start(bf16[10,40,128]{2,1,0:T(8,128)(2,1)} %x_ref.1), channel_id=1, source_target_pairs={{0,4},{2,6},{4,0},{6,2},{8,12},{10,14},{12,8},{14,10},{1,5},{3,7},... | collective-permute-start | bytes 307208 | tf_op jit(solution)/shard_map/ppermute | solution.py:214
  10.8 1.5 %collective-permute-start.4 = (f32[10,40,128]{2,1,0:T(8,128)S(1)}, f32[10,40,128]{2,1,0:T(8,128)S(1)}, u32[]{:S(2)}, u32[]{:S(2)}) collective-permute-start(f32[10,40,128]{2,1,0:T(8,128)S(1)} %get-tuple-element.36), channel_id=1, source_target_pairs={{0,1},{1,0},{2,3},{3,2},{4,5},{5,4},{6,7},{7,6},{8,9},{9,8},{10,11... | collective-permute-start | bytes 614408 | tf_op jit(solution)/shard_map/ppermute | solution.py:256
  12.5 6.2 %collective-permute-start.5 = (bf16[10,40,128]{2,1,0:T(8,128)(2,1)S(1)}, bf16[10,40,128]{2,1,0:T(8,128)(2,1)S(1)}, u32[]{:S(2)}, u32[]{:S(2)}) collective-permute-start(bf16[10,40,128]{2,1,0:T(8,128)(2,1)S(1)} %shard_map.52.refs_0_), channel_id=1, source_target_pairs={{0,8},{2,10},{4,12},{6,14},{8,1},{10,3},{12,5},{14,7},{1,0},{3,2},... | collective-permute-start | bytes 307208 | tf_op jit(solution)/shard_map/ppermute | solution.py:268
  13.1 1.8 %collective-permute-start.8 = (f32[4,40,128]{2,1,0:T(8,128)S(1)}, f32[4,40,128]{2,1,0:T(8,128)S(1)}, u32[]{:S(2)}, u32[]{:S(2)}) collective-permute-start(f32[4,40,128]{2,1,0:T(8,128)S(1)} %get-tuple-element.48), channel_id=1, source_target_pairs={{0,1},{1,0},{2,3},{3,2},{4,5},{5,4},{6,7},{7,6},{8,9},{9,8},{10,11... | collective-permute-start | bytes 245768 | tf_op jit(solution)/shard_map/ppermute | solution.py:276
  13.3 1.3 %collective-permute-start.6 = (f32[3,40,128]{2,1,0:T(8,128)S(1)}, f32[3,40,128]{2,1,0:T(8,128)S(1)}, u32[]{:S(2)}, u32[]{:S(2)}) collective-permute-start(f32[3,40,128]{2,1,0:T(8,128)S(1)} %get-tuple-element.46), channel_id=1, source_target_pairs={{0,1},{1,0},{2,3},{3,2},{4,5},{5,4},{6,7},{7,6},{8,9},{9,8},{10,11... | collective-permute-start | bytes 184328 | tf_op jit(solution)/shard_map/ppermute | solution.py:276
  13.7 1.2 %collective-permute-start.7 = (f32[3,40,128]{2,1,0:T(8,128)S(1)}, f32[3,40,128]{2,1,0:T(8,128)S(1)}, u32[]{:S(2)}, u32[]{:S(2)}) collective-permute-start(f32[3,40,128]{2,1,0:T(8,128)S(1)} %get-tuple-element.47), channel_id=1, source_target_pairs={{0,1},{1,0},{2,3},{3,2},{4,5},{5,4},{6,7},{7,6},{8,9},{9,8},{10,11... | collective-permute-start | bytes 184328 | tf_op jit(solution)/shard_map/ppermute | solution.py:276

commit v9 on v8

--- a/solution.py
+++ b/solution.py
@@ -81,7 +81,7 @@
             return tuple(added)
 
         zero = jnp.zeros((8, left_ref.shape[-1]), F32)
-        sums = lax.fori_loop(0, depth, body, tuple(tuple(zero for _ in some) for _ in rows), unroll=4)
+        sums = lax.fori_loop(0, depth, body, tuple(tuple(zero for _ in some) for _ in rows), unroll=20)
         for n, i in enumerate(rows):
             for place, total in zip(places[at : at + 3], sums[n], strict=True):
                 out_ref[i, pl.ds(place, 8), :] = total

time: 19.7 us -> 19.7 us (level)
  Pallas kernels: 5.55 us -> 5.21 us
  waiting for transfers between devices: 9.19 us -> 9.43 us
  transfers between devices with their start and end apart: 9 -> 9, of which waited for: 5 -> 5; matrix products, arithmetic and copies ran while one was open for 0% -> 0% of each run, Pallas kernels for 23% -> 21%
where the time goes in v9:
time: 19.7 us; the launch traced here: 19.5 us
  waiting for transfers between devices  9.43 us (48%)
  Pallas kernels  5.21 us (26%)
  starting transfers between devices  4.76 us (24%)
    ppermute x4, waiting for transfers between devices, from_step(): return lax.ppermute(x, 'row', [(i, i ^ step) for i in range(rows)])  4.25 us
    ppermute x1, waiting for transfers between devices, fast_plan(): arrived = lax.ppermute(tri, ('row', 'col'), pairs)  3.85 us
    ppermute x4, starting transfers between devices, from_step(): return lax.ppermute(x, 'row', [(i, i ^ step) for i in range(rows)])  3.82 us
    pallas_call x1, Pallas kernels, fast_plan(): call(functools.partial(own_kernel, half), in_specs=[pl.BlockSpec(memory_s...  1.61 us
    pallas_call x1, Pallas kernels, fast_plan(): call(functools.partial(keep_kernel, half, last), out_shape=(lefts, rights...  1.12 us
    ppermute x3, waiting for transfers between devices, fast_plan(): got_own = [lax.ppermute(piece, 'col', swap) for piece in pieces]  1.01 us
    pallas_call x1, Pallas kernels, fast_plan(): call(functools.partial(finish_far_kernel, half), in_specs=[in_place] * 3...  0.84 us
    ppermute x3, starting transfers between devices, fast_plan(): got_own = [lax.ppermute(piece, 'col', swap) for piece in pieces]  0.81 us
  transfers between devices with their start and end apart: 9, of which 5 were waited for; matrix products, arithmetic and copies ran while one was open for 0% of the time, Pallas kernels for 21%

profile of v9, /device:TPU:26, one launch (start us, length us, event | category | flops | bytes accessed | tf_op | source)
XLA Modules:
  0.0 19.5 jit_solution(976336158560121489)
XLA Ops:
  0.0 1.5 %collective-permute-start.2 = (bf16[10,40,128]{2,1,0:T(8,128)(2,1)}, bf16[10,40,128]{2,1,0:T(8,128)(2,1)S(1)}, u32[]{:S(2)}, u32[]{:S(2)}) collective-permute-start(bf16[10,40,128]{2,1,0:T(8,128)(2,1)} %x_ref.1), channel_id=1, source_target_pairs={{0,2},{2,0},{4,6},{6,4},{8,10},{10,8},{12,14},{14,12},{1,3},{3,1},... | collective-permute-start | bytes 307208 | tf_op jit(solution)/shard_map/ppermute | solution.py:214
  1.5 0.4 %collective-permute-start.3 = (bf16[10,40,128]{2,1,0:T(8,128)(2,1)}, bf16[10,40,128]{2,1,0:T(8,128)(2,1)S(1)}, u32[]{:S(2)}, u32[]{:S(2)}) collective-permute-start(bf16[10,40,128]{2,1,0:T(8,128)(2,1)} %x_ref.1), channel_id=1, source_target_pairs={{0,6},{2,4},{4,2},{6,0},{8,14},{10,12},{12,10},{14,8},{1,7},{3,5},... | collective-permute-start | bytes 307208 | tf_op jit(solution)/shard_map/ppermute | solution.py:214
  1.9 0.3 %collective-permute-start = (bf16[10,40,128]{2,1,0:T(8,128)(2,1)}, bf16[10,40,128]{2,1,0:T(8,128)(2,1)S(1)}, u32[]{:S(2)}, u32[]{:S(2)}) collective-permute-start(bf16[10,40,128]{2,1,0:T(8,128)(2,1)} %x_ref.1), channel_id=1, source_target_pairs={{0,8},{2,10},{4,12},{6,14},{8,0},{10,2},{12,4},{14,6},{1,9},{3,11}... | collective-permute-start | bytes 307208 | tf_op jit(solution)/shard_map/ppermute | solution.py:214
  2.2 1.6 %collective-permute-start.1 = (bf16[10,40,128]{2,1,0:T(8,128)(2,1)}, bf16[10,40,128]{2,1,0:T(8,128)(2,1)S(1)}, u32[]{:S(2)}, u32[]{:S(2)}) collective-permute-start(bf16[10,40,128]{2,1,0:T(8,128)(2,1)} %x_ref.1), channel_id=1, source_target_pairs={{0,4},{2,6},{4,0},{6,2},{8,12},{10,14},{12,8},{14,10},{1,5},{3,7},... | collective-permute-start | bytes 307208 | tf_op jit(solution)/shard_map/ppermute | solution.py:214
  3.8 1.6 %shard_map.46 = (f32[800,128]{1,0:T(8,128)S(1)}, f32[1640,128]{1,0:T(8,128)S(1)}, f32[400,128]{1,0:T(8,128)S(1)}, bf16[128,512]{1,0:T(8,128)(2,1)S(1)}, bf16[128...) custom-call(bf16[10,40,128]{2,1,0:T(8,128)(2,1)} %x_ref.1, bf16[128,512]{1,0:T(8,128)(2,1)} %w_ref.1, ...), custom_call_target="tpu_custom_call" | custom-call | tf_op jit(solution)/shard_map/pallas_call | solution.py:221
  5.4 0.0 collective-permute-done.2.x_ref
  5.5 0.6 %shard_map.47 = (f32[1640,128]{1,0:T(8,128)S(1)}, f32[10,16,128]{2,1,0:T(8,128)S(1)}) custom-call(bf16[10,40,128]{2,1,0:T(8,128)(2,1)S(1)} %collective-permute-done.2.x_ref, bf16[128,512]{1,0:T(8,128)(2,1)S(1)} %get-tuple-element.27.w_ref, f32[800,128]{1,0:T(8,128)S(1)} %get-tuple-element.28.left_ref._, ...), custom_call_target="tpu_custom_call", output_to_operand_aliasing={{0}: (3, {})} | custom-call | tf_op jit(solution)/shard_map/pallas_call | solution.py:238
  6.1 4.2 %collective-permute-done.3.x_ref = bf16[10,40,128]{2,1,0:T(8,128)(2,1)S(1)} collective-permute-done((bf16[10,40,128]{2,1,0:T(8,128)(2,1)}, bf16[10,40,128]{2,1,0:T(8,128)(2,1)S(1)}, u32[]{:S(2)}, u32[]{:S(2)}) %collective-permute-start.3) | collective-permute-done | bytes 102432 | tf_op jit(solution)/shard_map/ppermute | solution.py:214
  10.3 0.4 %shard_map.48.right_ref._r = f32[1640,128]{1,0:T(8,128)S(1)} custom-call(bf16[10,40,128]{2,1,0:T(8,128)(2,1)S(1)} %collective-permute-done.3.x_ref, bf16[128,512]{1,0:T(8,128)(2,1)S(1)} %get-tuple-element.27.w_ref, f32[1640,128]{1,0:T(8,128)S(1)} %get-tuple-element.31._), custom_call_target="tpu_custom_call", output_to_operand_aliasing={{}: (2, {})} | custom-call | tf_op jit(solution)/shard_map/pallas_call | solution.py:231
  10.7 0.0 collective-permute-done.far_ref
  10.7 0.0 collective-permute-done.1.x_ref
  10.8 0.1 collective-permute-start.4
  10.8 1.1 %shard_map.51 = (f32[800,128]{1,0:T(8,128)S(1)}, f32[1640,128]{1,0:T(8,128)S(1)}, f32[10,40,128]{2,1,0:T(8,128)S(1)}, f32[10,40,128]{2,1,0:T(8,128)S(1)}, f32[3,...) custom-call(bf16[10,40,128]{2,1,0:T(8,128)(2,1)S(1)} %collective-per, ...), custom_call_target="tpu_custom_call", output_to_operand_aliasing={{0}: (4, {}), {1}: (5, {})} | custom-call | tf_op jit(solution)/shard_map/pallas_call | solution.py:259
  12.0 0.3 %collective-permute-done.4.got_ref = f32[10,40,128]{2,1,0:T(8,128)S(1)} collective-permute-done((f32[10,40,128]{2,1,0:T(8,128)S(1)}, f32[10,40,128]{2,1,0:T(8,128)S(1)}, u32[]{:S(2)}, u32[]{:S(2)}) %collective-permute-start.4) | collective-permute-done | bytes 204832 | tf_op jit(solution)/shard_map/ppermute | solution.py:256
  12.3 0.2 %shard_map.52.refs_0_ = bf16[10,40,128]{2,1,0:T(8,128)(2,1)S(1)} custom-call(f32[10,40,128]{2,1,0:T(8,128)S(1)} %get-tuple-element.35.tile_ref, f32[10,40,128]{2,1,0:T(8,128)S(1)} %collective-permute-done.4.got_ref), custom_call_target="tpu_custom_call" | custom-call | tf_op jit(solution)/shard_map/pallas_call | solution.py:265
  12.5 0.1 collective-permute-start.5
  12.6 0.4 %shard_map.53 = (f32[10,40,128]{2,1,0:T(8,128)S(1)}, f32[3,40,128]{2,1,0:T(8,128)S(1)}, f32[3,40,128]{2,1,0:T(8,128)S(1)}, f32[4,40,128]{2,1,0:T(8,128)S(1)}) custom-call(f32[800,128]{1,0:T(8,128)S(1)} %get-tuple-element.39.left_ref, ...), custom_call_target="tpu_custom_call", output_to_operand_aliasing={{0}: (4, {}), {1}: (5, {}), {2}: (6, {}), {3}: (7, {})} | custom-call | tf_op jit(solution)/shard_map/pallas_call | solution.py:270
  13.0 0.3 %collective-permute-start.8 = (f32[4,40,128]{2,1,0:T(8,128)S(1)}, f32[4,40,128]{2,1,0:T(8,128)S(1)}, u32[]{:S(2)}, u32[]{:S(2)}) collective-permute-start(f32[4,40,128]{2,1,0:T(8,128)S(1)} %get-tuple-element.48), channel_id=1, source_target_pairs={{0,1},{1,0},{2,3},{3,2},{4,5},{5,4},{6,7},{7,6},{8,9},{9,8},{10,11... | collective-permute-start | bytes 245768 | tf_op jit(solution)/shard_map/ppermute | solution.py:276
  13.3 0.3 %collective-permute-start.6 = (f32[3,40,128]{2,1,0:T(8,128)S(1)}, f32[3,40,128]{2,1,0:T(8,128)S(1)}, u32[]{:S(2)}, u32[]{:S(2)}) collective-permute-start(f32[3,40,128]{2,1,0:T(8,128)S(1)} %get-tuple-element.46), channel_id=1, source_target_pairs={{0,1},{1,0},{2,3},{3,2},{4,5},{5,4},{6,7},{7,6},{8,9},{9,8},{10,11... | collective-permute-start | bytes 184328 | tf_op jit(solution)/shard_map/ppermute | solution.py:276
  13.6 0.2 %collective-permute-start.7 = (f32[3,40,128]{2,1,0:T(8,128)S(1)}, f32[3,40,128]{2,1,0:T(8,128)S(1)}, u32[]{:S(2)}, u32[]{:S(2)}) collective-permute-start(f32[3,40,128]{2,1,0:T(8,128)S(1)} %get-tuple-element.47), channel_id=1, source_target_pairs={{0,1},{1,0},{2,3},{3,2},{4,5},{5,4},{6,7},{7,6},{8,9},{9,8},{10,11... | collective-permute-start | bytes 184328 | tf_op jit(solution)/shard_map/ppermute | solution.py:276
  13.8 0.7 %collective-permute-done.6.refs_0_ = f32[3,40,128]{2,1,0:T(8,128)S(1)} collective-permute-done((f32[3,40,128]{2,1,0:T(8,128)S(1)}, f32[3,40,128]{2,1,0:T(8,128)S(1)}, u32[]{:S(2)}, u32[]{:S(2)}) %collective-permute-start.6) | collective-permute-done | bytes 61472 | tf_op jit(solution)/shard_map/ppermute | solution.py:276
  14.5 0.3 %collective-permute-done.7.refs_1_ = f32[3,40,128]{2,1,0:T(8,128)S(1)} collective-permute-done((f32[3,40,128]{2,1,0:T(8,128)S(1)}, f32[3,40,128]{2,1,0:T(8,128)S(1)}, u32[]{:S(2)}, u32[]{:S(2)}) %collective-permute-start.7) | collective-permute-done | bytes 61472 | tf_op jit(solution)/shard_map/ppermute | solution.py:276
  14.8 0.0 collective-permute-done.8.refs_2_
  14.8 3.9 %collective-permute-done.5.tri_ref = bf16[10,40,128]{2,1,0:T(8,128)(2,1)S(1)} collective-permute-done((bf16[10,40,128]{2,1,0:T(8,128)(2,1)S(1)}, bf16[10,40,128]{2,1,0:T(8,128)(2,1)S(1)}, u32[]{:S(2)}, u32[]{:S(2)}) %collective-permute-start.5) | collective-permute-done | bytes 102432 | tf_op jit(solution)/shard_map/ppermute | solution.py:268
  18.7 0.8 %shard_map.55 = bf16[10,40,128]{2,1,0:T(8,128)(2,1)} custom-call(bf16[10,40,128]{2,1,0:T(8,128)(2,1)S(1)} %collective-permute-done.5.tri_ref, f32[400,128]{1,0:T(8,128)S(1)} %get-tuple-element.37.refs_3_.gate_ref, bf16[128,128]{1,0:T(8,128)(2,1)S(1)} %get-tuple-element.38.refs_4_.o_ref, bf16[10,40,128]{2,1,0:T(8,128)(2,1)} %shard_map.54._), custom_call_target="tpu_custom_call", output_to_operand_aliasing={{}: (3, {})} | custom-call | tf_op jit(solution)/shard_map/pallas_call | solution.py:287
  (3 shorter events, 0.1 us)
Async XLA Ops:
  0.0 5.4 %collective-permute-start.2 = (bf16[10,40,128]{2,1,0:T(8,128)(2,1)}, bf16[10,40,128]{2,1,0:T(8,128)(2,1)S(1)}, u32[]{:S(2)}, u32[]{:S(2)}) collective-permute-start(bf16[10,40,128]{2,1,0:T(8,128)(2,1)} %x_ref.1), channel_id=1, source_target_pairs={{0,2},{2,0},{4,6},{6,4},{8,10},{10,8},{12,14},{14,12},{1,3},{3,1},... | collective-permute-start | bytes 307208 | tf_op jit(solution)/shard_map/ppermute | solution.py:214
  1.5 8.8 %collective-permute-start.3 = (bf16[10,40,128]{2,1,0:T(8,128)(2,1)}, bf16[10,40,128]{2,1,0:T(8,128)(2,1)S(1)}, u32[]{:S(2)}, u32[]{:S(2)}) collective-permute-start(bf16[10,40,128]{2,1,0:T(8,128)(2,1)} %x_ref.1), channel_id=1, source_target_pairs={{0,6},{2,4},{4,2},{6,0},{8,14},{10,12},{12,10},{14,8},{1,7},{3,5},... | collective-permute-start | bytes 307208 | tf_op jit(solution)/shard_map/ppermute | solution.py:214
  1.9 8.8 %collective-permute-start = (bf16[10,40,128]{2,1,0:T(8,128)(2,1)}, bf16[10,40,128]{2,1,0:T(8,128)(2,1)S(1)}, u32[]{:S(2)}, u32[]{:S(2)}) collective-permute-start(bf16[10,40,128]{2,1,0:T(8,128)(2,1)} %x_ref.1), channel_id=1, source_target_pairs={{0,8},{2,10},{4,12},{6,14},{8,0},{10,2},{12,4},{14,6},{1,9},{3,11}... | collective-permute-start | bytes 307208 | tf_op jit(solution)/shard_map/ppermute | solution.py:214
  2.2 8.5 %collective-permute-start.1 = (bf16[10,40,128]{2,1,0:T(8,128)(2,1)}, bf16[10,40,128]{2,1,0:T(8,128)(2,1)S(1)}, u32[]{:S(2)}, u32[]{:S(2)}) collective-permute-start(bf16[10,40,128]{2,1,0:T(8,128)(2,1)} %x_ref.1), channel_id=1, source_target_pairs={{0,4},{2,6},{4,0},{6,2},{8,12},{10,14},{12,8},{14,10},{1,5},{3,7},... | collective-permute-start | bytes 307208 | tf_op jit(solution)/shard_map/ppermute | solution.py:214
  10.8 1.5 %collective-permute-start.4 = (f32[10,40,128]{2,1,0:T(8,128)S(1)}, f32[10,40,128]{2,1,0:T(8,128)S(1)}, u32[]{:S(2)}, u32[]{:S(2)}) collective-permute-start(f32[10,40,128]{2,1,0:T(8,128)S(1)} %get-tuple-element.36), channel_id=1, source_target_pairs={{0,1},{1,0},{2,3},{3,2},{4,5},{5,4},{6,7},{7,6},{8,9},{9,8},{10,11... | collective-permute-start | bytes 614408 | tf_op jit(solution)/shard_map/ppermute | solution.py:256
  12.5 6.2 %collective-permute-start.5 = (bf16[10,40,128]{2,1,0:T(8,128)(2,1)S(1)}, bf16[10,40,128]{2,1,0:T(8,128)(2,1)S(1)}, u32[]{:S(2)}, u32[]{:S(2)}) collective-permute-start(bf16[10,40,128]{2,1,0:T(8,128)(2,1)S(1)} %shard_map.52.refs_0_), channel_id=1, source_target_pairs={{0,8},{2,10},{4,12},{6,14},{8,1},{10,3},{12,5},{14,7},{1,0},{3,2},... | collective-permute-start | bytes 307208 | tf_op jit(solution)/shard_map/ppermute | solution.py:268
  13.0 1.8 %collective-permute-start.8 = (f32[4,40,128]{2,1,0:T(8,128)S(1)}, f32[4,40,128]{2,1,0:T(8,128)S(1)}, u32[]{:S(2)}, u32[]{:S(2)}) collective-permute-start(f32[4,40,128]{2,1,0:T(8,128)S(1)} %get-tuple-element.48), channel_id=1, source_target_pairs={{0,1},{1,0},{2,3},{3,2},{4,5},{5,4},{6,7},{7,6},{8,9},{9,8},{10,11... | collective-permute-start | bytes 245768 | tf_op jit(solution)/shard_map/ppermute | solution.py:276
  13.3 1.2 %collective-permute-start.6 = (f32[3,40,128]{2,1,0:T(8,128)S(1)}, f32[3,40,128]{2,1,0:T(8,128)S(1)}, u32[]{:S(2)}, u32[]{:S(2)}) collective-permute-start(f32[3,40,128]{2,1,0:T(8,128)S(1)} %get-tuple-element.46), channel_id=1, source_target_pairs={{0,1},{1,0},{2,3},{3,2},{4,5},{5,4},{6,7},{7,6},{8,9},{9,8},{10,11... | collective-permute-start | bytes 184328 | tf_op jit(solution)/shard_map/ppermute | solution.py:276
  13.6 1.2 %collective-permute-start.7 = (f32[3,40,128]{2,1,0:T(8,128)S(1)}, f32[3,40,128]{2,1,0:T(8,128)S(1)}, u32[]{:S(2)}, u32[]{:S(2)}) collective-permute-start(f32[3,40,128]{2,1,0:T(8,128)S(1)} %get-tuple-element.47), channel_id=1, source_target_pairs={{0,1},{1,0},{2,3},{3,2},{4,5},{5,4},{6,7},{7,6},{8,9},{9,8},{10,11... | collective-permute-start | bytes 184328 | tf_op jit(solution)/shard_map/ppermute | solution.py:276

commit v10 on v9

--- a/solution.py
+++ b/solution.py
@@ -120,9 +120,12 @@
 def far_kernel(half, far_ref, w_ref, right_ref, _, left_ref, tile_ref):
     early, middle, _ = strips_of(half, tile_ref.shape[0])
 
+    @pl.when(jnp.logical_not(late_sender(half)))
+    def _():
+        put_far(far_ref, w_ref, left_ref)
+
     @pl.when(lax.axis_index("col") == 1)
     def _():
-        put_far(far_ref, w_ref, left_ref)
         products(left_ref, left_ref.shape[0] // 2, right_ref, early + middle, early + middle, tile_ref)
 
 
@@ -143,9 +146,12 @@
     early, middle, late = strips_of(half, tile_ref.shape[0])
     strips = early + middle + late
 
+    @pl.when(late_sender(half))
+    def _():
+        put_far(far_ref, w_ref, left_ref)
+
     @pl.when(lax.axis_index("col") == 0)
     def _():
-        put_far(far_ref, w_ref, left_ref)
         put_right(half, step, x_ref, w_ref, right_ref)
         products(left_ref, left_ref.shape[0] // 2, right_ref, strips, strips, tile_ref)
 

time: 19.7 us -> 19.7 us (level)
  Pallas kernels: 5.21 us -> 5.45 us
  waiting for transfers between devices: 9.43 us -> 9.2 us
    pallas_call x1, Pallas kernels: 1.12 us -> 1.36 us  [fast_plan(): call(functools.partial(keep_kernel, half, last), out_shape=(lefts, rights...]
    ppermute x1, waiting for transfers between devices: 0.31 us -> 0.08 us  [fast_plan(): got_far = lax.ppermute(far_tile, 'col', swap)]
  transfers between devices with their start and end apart: 9 -> 9, of which waited for: 5 -> 5; matrix products, arithmetic and copies ran while one was open for 0% -> 0% of each run, Pallas kernels for 21% -> 22%
where the time goes in v10:
time: 19.7 us; the launch traced here: 19.5 us
  waiting for transfers between devices  9.2 us (47%)
  Pallas kernels  5.45 us (28%)
  starting transfers between devices  4.76 us (24%)
    ppermute x4, waiting for transfers between devices, from_step(): return lax.ppermute(x, 'row', [(i, i ^ step) for i in range(rows)])  4.25 us
    ppermute x1, waiting for transfers between devices, fast_plan(): arrived = lax.ppermute(tri, ('row', 'col'), pairs)  3.85 us
    ppermute x4, starting transfers between devices, from_step(): return lax.ppermute(x, 'row', [(i, i ^ step) for i in range(rows)])  3.82 us
    pallas_call x1, Pallas kernels, fast_plan(): call(functools.partial(own_kernel, half), in_specs=[pl.BlockSpec(memory_s...  1.61 us
    pallas_call x1, Pallas kernels, fast_plan(): call(functools.partial(keep_kernel, half, last), out_shape=(lefts, rights...  1.36 us
    ppermute x3, waiting for transfers between devices, fast_plan(): got_own = [lax.ppermute(piece, 'col', swap) for piece in pieces]  1.02 us
    pallas_call x1, Pallas kernels, fast_plan(): call(functools.partial(finish_far_kernel, half), in_specs=[in_place] * 3...  0.84 us
    ppermute x3, starting transfers between devices, fast_plan(): got_own = [lax.ppermute(piece, 'col', swap) for piece in pieces]  0.81 us
  transfers between devices with their start and end apart: 9, of which 5 were waited for; matrix products, arithmetic and copies ran while one was open for 0% of the time, Pallas kernels for 22%

profile of v10, /device:TPU:26, one launch (start us, length us, event | category | flops | bytes accessed | tf_op | source)
XLA Modules:
  0.0 19.5 jit_solution(11374979059738739545)
XLA Ops:
  0.0 1.5 %collective-permute-start.2 = (bf16[10,40,128]{2,1,0:T(8,128)(2,1)}, bf16[10,40,128]{2,1,0:T(8,128)(2,1)S(1)}, u32[]{:S(2)}, u32[]{:S(2)}) collective-permute-start(bf16[10,40,128]{2,1,0:T(8,128)(2,1)} %x_ref.1), channel_id=1, source_target_pairs={{0,2},{2,0},{4,6},{6,4},{8,10},{10,8},{12,14},{14,12},{1,3},{3,1},... | collective-permute-start | bytes 307208 | tf_op jit(solution)/shard_map/ppermute | solution.py:220
  1.5 0.4 %collective-permute-start.3 = (bf16[10,40,128]{2,1,0:T(8,128)(2,1)}, bf16[10,40,128]{2,1,0:T(8,128)(2,1)S(1)}, u32[]{:S(2)}, u32[]{:S(2)}) collective-permute-start(bf16[10,40,128]{2,1,0:T(8,128)(2,1)} %x_ref.1), channel_id=1, source_target_pairs={{0,6},{2,4},{4,2},{6,0},{8,14},{10,12},{12,10},{14,8},{1,7},{3,5},... | collective-permute-start | bytes 307208 | tf_op jit(solution)/shard_map/ppermute | solution.py:220
  1.9 0.3 %collective-permute-start = (bf16[10,40,128]{2,1,0:T(8,128)(2,1)}, bf16[10,40,128]{2,1,0:T(8,128)(2,1)S(1)}, u32[]{:S(2)}, u32[]{:S(2)}) collective-permute-start(bf16[10,40,128]{2,1,0:T(8,128)(2,1)} %x_ref.1), channel_id=1, source_target_pairs={{0,8},{2,10},{4,12},{6,14},{8,0},{10,2},{12,4},{14,6},{1,9},{3,11}... | collective-permute-start | bytes 307208 | tf_op jit(solution)/shard_map/ppermute | solution.py:220
  2.2 1.6 %collective-permute-start.1 = (bf16[10,40,128]{2,1,0:T(8,128)(2,1)}, bf16[10,40,128]{2,1,0:T(8,128)(2,1)S(1)}, u32[]{:S(2)}, u32[]{:S(2)}) collective-permute-start(bf16[10,40,128]{2,1,0:T(8,128)(2,1)} %x_ref.1), channel_id=1, source_target_pairs={{0,4},{2,6},{4,0},{6,2},{8,12},{10,14},{12,8},{14,10},{1,5},{3,7},... | collective-permute-start | bytes 307208 | tf_op jit(solution)/shard_map/ppermute | solution.py:220
  3.8 1.6 %shard_map.46 = (f32[800,128]{1,0:T(8,128)S(1)}, f32[1640,128]{1,0:T(8,128)S(1)}, f32[400,128]{1,0:T(8,128)S(1)}, bf16[128,512]{1,0:T(8,128)(2,1)S(1)}, bf16[128...) custom-call(bf16[10,40,128]{2,1,0:T(8,128)(2,1)} %x_ref.1, bf16[128,512]{1,0:T(8,128)(2,1)} %w_ref.1, ...), custom_call_target="tpu_custom_call" | custom-call | tf_op jit(solution)/shard_map/pallas_call | solution.py:227
  5.4 0.0 collective-permute-done.2.x_ref
  5.5 0.6 %shard_map.47 = (f32[1640,128]{1,0:T(8,128)S(1)}, f32[10,16,128]{2,1,0:T(8,128)S(1)}) custom-call(bf16[10,40,128]{2,1,0:T(8,128)(2,1)S(1)} %collective-permute-done.2.x_ref, bf16[128,512]{1,0:T(8,128)(2,1)S(1)} %get-tuple-element.27.w_ref, f32[800,128]{1,0:T(8,128)S(1)} %get-tuple-element.28.left_ref._, ...), custom_call_target="tpu_custom_call", output_to_operand_aliasing={{0}: (3, {})} | custom-call | tf_op jit(solution)/shard_map/pallas_call | solution.py:244
  6.1 4.2 %collective-permute-done.3.x_ref = bf16[10,40,128]{2,1,0:T(8,128)(2,1)S(1)} collective-permute-done((bf16[10,40,128]{2,1,0:T(8,128)(2,1)}, bf16[10,40,128]{2,1,0:T(8,128)(2,1)S(1)}, u32[]{:S(2)}, u32[]{:S(2)}) %collective-permute-start.3) | collective-permute-done | bytes 102432 | tf_op jit(solution)/shard_map/ppermute | solution.py:220
  10.3 0.4 %shard_map.48.right_ref._r = f32[1640,128]{1,0:T(8,128)S(1)} custom-call(bf16[10,40,128]{2,1,0:T(8,128)(2,1)S(1)} %collective-permute-done.3.x_ref, bf16[128,512]{1,0:T(8,128)(2,1)S(1)} %get-tuple-element.27.w_ref, f32[1640,128]{1,0:T(8,128)S(1)} %get-tuple-element.31._), custom_call_target="tpu_custom_call", output_to_operand_aliasing={{}: (2, {})} | custom-call | tf_op jit(solution)/shard_map/pallas_call | solution.py:237
  10.7 0.0 collective-permute-done.far_ref
  10.7 0.0 collective-permute-done.1.x_ref
  10.8 0.1 collective-permute-start.4
  10.8 1.4 %shard_map.51 = (f32[800,128]{1,0:T(8,128)S(1)}, f32[1640,128]{1,0:T(8,128)S(1)}, f32[10,40,128]{2,1,0:T(8,128)S(1)}, f32[10,40,128]{2,1,0:T(8,128)S(1)}, f32[3,...) custom-call(bf16[10,40,128]{2,1,0:T(8,128)(2,1)S(1)} %collective-per, ...), custom_call_target="tpu_custom_call", output_to_operand_aliasing={{0}: (4, {}), {1}: (5, {})} | custom-call | tf_op jit(solution)/shard_map/pallas_call | solution.py:265
  12.2 0.1 collective-permute-done.4.got_ref
  12.3 0.2 %shard_map.52.refs_0_ = bf16[10,40,128]{2,1,0:T(8,128)(2,1)S(1)} custom-call(f32[10,40,128]{2,1,0:T(8,128)S(1)} %get-tuple-element.35.tile_ref, f32[10,40,128]{2,1,0:T(8,128)S(1)} %collective-permute-done.4.got_ref), custom_call_target="tpu_custom_call" | custom-call | tf_op jit(solution)/shard_map/pallas_call | solution.py:271
  12.5 0.1 collective-permute-start.5
  12.6 0.4 %shard_map.53 = (f32[10,40,128]{2,1,0:T(8,128)S(1)}, f32[3,40,128]{2,1,0:T(8,128)S(1)}, f32[3,40,128]{2,1,0:T(8,128)S(1)}, f32[4,40,128]{2,1,0:T(8,128)S(1)}) custom-call(f32[800,128]{1,0:T(8,128)S(1)} %get-tuple-element.39.left_ref, ...), custom_call_target="tpu_custom_call", output_to_operand_aliasing={{0}: (4, {}), {1}: (5, {}), {2}: (6, {}), {3}: (7, {})} | custom-call | tf_op jit(solution)/shard_map/pallas_call | solution.py:276
  13.0 0.3 %collective-permute-start.8 = (f32[4,40,128]{2,1,0:T(8,128)S(1)}, f32[4,40,128]{2,1,0:T(8,128)S(1)}, u32[]{:S(2)}, u32[]{:S(2)}) collective-permute-start(f32[4,40,128]{2,1,0:T(8,128)S(1)} %get-tuple-element.48), channel_id=1, source_target_pairs={{0,1},{1,0},{2,3},{3,2},{4,5},{5,4},{6,7},{7,6},{8,9},{9,8},{10,11... | collective-permute-start | bytes 245768 | tf_op jit(solution)/shard_map/ppermute | solution.py:282
  13.3 0.3 %collective-permute-start.6 = (f32[3,40,128]{2,1,0:T(8,128)S(1)}, f32[3,40,128]{2,1,0:T(8,128)S(1)}, u32[]{:S(2)}, u32[]{:S(2)}) collective-permute-start(f32[3,40,128]{2,1,0:T(8,128)S(1)} %get-tuple-element.46), channel_id=1, source_target_pairs={{0,1},{1,0},{2,3},{3,2},{4,5},{5,4},{6,7},{7,6},{8,9},{9,8},{10,11... | collective-permute-start | bytes 184328 | tf_op jit(solution)/shard_map/ppermute | solution.py:282
  13.6 0.2 %collective-permute-start.7 = (f32[3,40,128]{2,1,0:T(8,128)S(1)}, f32[3,40,128]{2,1,0:T(8,128)S(1)}, u32[]{:S(2)}, u32[]{:S(2)}) collective-permute-start(f32[3,40,128]{2,1,0:T(8,128)S(1)} %get-tuple-element.47), channel_id=1, source_target_pairs={{0,1},{1,0},{2,3},{3,2},{4,5},{5,4},{6,7},{7,6},{8,9},{9,8},{10,11... | collective-permute-start | bytes 184328 | tf_op jit(solution)/shard_map/ppermute | solution.py:282
  13.8 0.7 %collective-permute-done.6.refs_0_ = f32[3,40,128]{2,1,0:T(8,128)S(1)} collective-permute-done((f32[3,40,128]{2,1,0:T(8,128)S(1)}, f32[3,40,128]{2,1,0:T(8,128)S(1)}, u32[]{:S(2)}, u32[]{:S(2)}) %collective-permute-start.6) | collective-permute-done | bytes 61472 | tf_op jit(solution)/shard_map/ppermute | solution.py:282
  14.5 0.3 %collective-permute-done.7.refs_1_ = f32[3,40,128]{2,1,0:T(8,128)S(1)} collective-permute-done((f32[3,40,128]{2,1,0:T(8,128)S(1)}, f32[3,40,128]{2,1,0:T(8,128)S(1)}, u32[]{:S(2)}, u32[]{:S(2)}) %collective-permute-start.7) | collective-permute-done | bytes 61472 | tf_op jit(solution)/shard_map/ppermute | solution.py:282
  14.8 0.0 collective-permute-done.8.refs_2_
  14.8 3.8 %collective-permute-done.5.tri_ref = bf16[10,40,128]{2,1,0:T(8,128)(2,1)S(1)} collective-permute-done((bf16[10,40,128]{2,1,0:T(8,128)(2,1)S(1)}, bf16[10,40,128]{2,1,0:T(8,128)(2,1)S(1)}, u32[]{:S(2)}, u32[]{:S(2)}) %collective-permute-start.5) | collective-permute-done | bytes 102432 | tf_op jit(solution)/shard_map/ppermute | solution.py:274
  18.7 0.8 %shard_map.55 = bf16[10,40,128]{2,1,0:T(8,128)(2,1)} custom-call(bf16[10,40,128]{2,1,0:T(8,128)(2,1)S(1)} %collective-permute-done.5.tri_ref, f32[400,128]{1,0:T(8,128)S(1)} %get-tuple-element.37.refs_3_.gate_ref, bf16[128,128]{1,0:T(8,128)(2,1)S(1)} %get-tuple-element.38.refs_4_.o_ref, bf16[10,40,128]{2,1,0:T(8,128)(2,1)} %shard_map.54._), custom_call_target="tpu_custom_call", output_to_operand_aliasing={{}: (3, {})} | custom-call | tf_op jit(solution)/shard_map/pallas_call | solution.py:293
  (3 shorter events, 0.1 us)
Async XLA Ops:
  0.0 5.4 %collective-permute-start.2 = (bf16[10,40,128]{2,1,0:T(8,128)(2,1)}, bf16[10,40,128]{2,1,0:T(8,128)(2,1)S(1)}, u32[]{:S(2)}, u32[]{:S(2)}) collective-permute-start(bf16[10,40,128]{2,1,0:T(8,128)(2,1)} %x_ref.1), channel_id=1, source_target_pairs={{0,2},{2,0},{4,6},{6,4},{8,10},{10,8},{12,14},{14,12},{1,3},{3,1},... | collective-permute-start | bytes 307208 | tf_op jit(solution)/shard_map/ppermute | solution.py:220
  1.5 8.8 %collective-permute-start.3 = (bf16[10,40,128]{2,1,0:T(8,128)(2,1)}, bf16[10,40,128]{2,1,0:T(8,128)(2,1)S(1)}, u32[]{:S(2)}, u32[]{:S(2)}) collective-permute-start(bf16[10,40,128]{2,1,0:T(8,128)(2,1)} %x_ref.1), channel_id=1, source_target_pairs={{0,6},{2,4},{4,2},{6,0},{8,14},{10,12},{12,10},{14,8},{1,7},{3,5},... | collective-permute-start | bytes 307208 | tf_op jit(solution)/shard_map/ppermute | solution.py:220
  1.9 8.8 %collective-permute-start = (bf16[10,40,128]{2,1,0:T(8,128)(2,1)}, bf16[10,40,128]{2,1,0:T(8,128)(2,1)S(1)}, u32[]{:S(2)}, u32[]{:S(2)}) collective-permute-start(bf16[10,40,128]{2,1,0:T(8,128)(2,1)} %x_ref.1), channel_id=1, source_target_pairs={{0,8},{2,10},{4,12},{6,14},{8,0},{10,2},{12,4},{14,6},{1,9},{3,11}... | collective-permute-start | bytes 307208 | tf_op jit(solution)/shard_map/ppermute | solution.py:220
  2.2 8.5 %collective-permute-start.1 = (bf16[10,40,128]{2,1,0:T(8,128)(2,1)}, bf16[10,40,128]{2,1,0:T(8,128)(2,1)S(1)}, u32[]{:S(2)}, u32[]{:S(2)}) collective-permute-start(bf16[10,40,128]{2,1,0:T(8,128)(2,1)} %x_ref.1), channel_id=1, source_target_pairs={{0,4},{2,6},{4,0},{6,2},{8,12},{10,14},{12,8},{14,10},{1,5},{3,7},... | collective-permute-start | bytes 307208 | tf_op jit(solution)/shard_map/ppermute | solution.py:220
  10.8 1.5 %collective-permute-start.4 = (f32[10,40,128]{2,1,0:T(8,128)S(1)}, f32[10,40,128]{2,1,0:T(8,128)S(1)}, u32[]{:S(2)}, u32[]{:S(2)}) collective-permute-start(f32[10,40,128]{2,1,0:T(8,128)S(1)} %get-tuple-element.36), channel_id=1, source_target_pairs={{0,1},{1,0},{2,3},{3,2},{4,5},{5,4},{6,7},{7,6},{8,9},{9,8},{10,11... | collective-permute-start | bytes 614408 | tf_op jit(solution)/shard_map/ppermute | solution.py:262
  12.5 6.2 %collective-permute-start.5 = (bf16[10,40,128]{2,1,0:T(8,128)(2,1)S(1)}, bf16[10,40,128]{2,1,0:T(8,128)(2,1)S(1)}, u32[]{:S(2)}, u32[]{:S(2)}) collective-permute-start(bf16[10,40,128]{2,1,0:T(8,128)(2,1)S(1)} %shard_map.52.refs_0_), channel_id=1, source_target_pairs={{0,8},{2,10},{4,12},{6,14},{8,1},{10,3},{12,5},{14,7},{1,0},{3,2},... | collective-permute-start | bytes 307208 | tf_op jit(solution)/shard_map/ppermute | solution.py:274
  13.0 1.8 %collective-permute-start.8 = (f32[4,40,128]{2,1,0:T(8,128)S(1)}, f32[4,40,128]{2,1,0:T(8,128)S(1)}, u32[]{:S(2)}, u32[]{:S(2)}) collective-permute-start(f32[4,40,128]{2,1,0:T(8,128)S(1)} %get-tuple-element.48), channel_id=1, source_target_pairs={{0,1},{1,0},{2,3},{3,2},{4,5},{5,4},{6,7},{7,6},{8,9},{9,8},{10,11... | collective-permute-start | bytes 245768 | tf_op jit(solution)/shard_map/ppermute | solution.py:282
  13.3 1.2 %collective-permute-start.6 = (f32[3,40,128]{2,1,0:T(8,128)S(1)}, f32[3,40,128]{2,1,0:T(8,128)S(1)}, u32[]{:S(2)}, u32[]{:S(2)}) collective-permute-start(f32[3,40,128]{2,1,0:T(8,128)S(1)} %get-tuple-element.46), channel_id=1, source_target_pairs={{0,1},{1,0},{2,3},{3,2},{4,5},{5,4},{6,7},{7,6},{8,9},{9,8},{10,11... | collective-permute-start | bytes 184328 | tf_op jit(solution)/shard_map/ppermute | solution.py:282
  13.6 1.2 %collective-permute-start.7 = (f32[3,40,128]{2,1,0:T(8,128)S(1)}, f32[3,40,128]{2,1,0:T(8,128)S(1)}, u32[]{:S(2)}, u32[]{:S(2)}) collective-permute-start(f32[3,40,128]{2,1,0:T(8,128)S(1)} %get-tuple-element.47), channel_id=1, source_target_pairs={{0,1},{1,0},{2,3},{3,2},{4,5},{5,4},{6,7},{7,6},{8,9},{9,8},{10,11... | collective-permute-start | bytes 184328 | tf_op jit(solution)/shard_map/ppermute | solution.py:282
